TPU v7x, 32 devices: a whole 2x2x4 slice. The times are simulated.
32 devices in a mesh: seq: 8 (over z, core), dp: 4 (over y, x).
Axes of the slice: x: 2, y: 2, z: 4, core: 2. Of those that a mesh axis runs over, the one named last changes fastest.
Arguments:
- tokens: bfloat16 [4, 1024, 1024], P('dp', 'seq'), may hold values from -6 to 6
- cotangent: bfloat16 [4, 1024, 1024], P('dp', 'seq'), may hold values from -6 to 6
- doc_lengths: int32 [4, 4], P('dp'), may hold values from 1 to 960, 1024 in all within a row
- decay_exponent: int32 [1536], replicated, may hold values from 4 to 19
- branch_weight: bfloat16 [1024, 1536], P(('seq', 'dp')), may hold values from -0.1875 to 0.1875
- input_weight: bfloat16 [1024, 1536], P(('seq', 'dp')), may hold values from -0.1875 to 0.1875
- decay_weight: bfloat16 [1536, 1536], P(('seq', 'dp')), may hold values from -0.15625 to 0.15625
- inject_weight: bfloat16 [1536, 1536], P(('seq', 'dp')), may hold values from -0.15625 to 0.15625
- output_weight: bfloat16 [1536, 1024], P(('seq', 'dp')), may hold values from -0.15625 to 0.15625
- mlp_gate: bfloat16 [1024, 3072], P(('seq', 'dp')), may hold values from -0.1875 to 0.1875
- mlp_up: bfloat16 [1024, 3072], P(('seq', 'dp')), may hold values from -0.1875 to 0.1875
- mlp_down: bfloat16 [3072, 1024], P(('seq', 'dp')), may hold values from -0.109375 to 0.109375
- first_gain: bfloat16 [1024], P(('seq', 'dp')), may hold values from 0.5 to 1.5
- second_gain: bfloat16 [1024], P(('seq', 'dp')), may hold values from 0.5 to 1.5
- conv_taps: bfloat16 [1536, 4], P(('seq', 'dp')), may hold values from -3 to 3
- conv_bias: bfloat16 [1536], P(('seq', 'dp')), may hold values from -3 to 3
- decay_bias: bfloat16 [1536], P(('seq', 'dp')), may hold values from -4 to 4
- inject_bias: bfloat16 [1536], P(('seq', 'dp')), may hold values from -4 to 4
Outputs:
- activations: bfloat16 [4, 1024, 1024], P('dp', 'seq')
- d_tokens: float32 [4, 1024, 1024], P('dp', 'seq')
- grad_branch_weight: float32 [1024, 1536], P(('seq', 'dp'))
- grad_input_weight: float32 [1024, 1536], P(('seq', 'dp'))
- grad_decay_weight: float32 [1536, 1536], P(('seq', 'dp'))
- grad_inject_weight: float32 [1536, 1536], P(('seq', 'dp'))
- grad_output_weight: float32 [1536, 1024], P(('seq', 'dp'))
- grad_mlp_gate: float32 [1024, 3072], P(('seq', 'dp'))
- grad_mlp_up: float32 [1024, 3072], P(('seq', 'dp'))
- grad_mlp_down: float32 [3072, 1024], P(('seq', 'dp'))
- grad_first_gain: float32 [1024], P(('seq', 'dp'))
- grad_second_gain: float32 [1024], P(('seq', 'dp'))
- grad_conv_taps: float32 [1536, 4], P(('seq', 'dp'))
- grad_conv_bias: float32 [1536], P(('seq', 'dp'))
- grad_decay_bias: float32 [1536], P(('seq', 'dp'))
- grad_inject_bias: float32 [1536], P(('seq', 'dp'))
Inputs may be any that keep to these rules, and one draw needn't show every extreme that they name: `doc_lengths`: each row sums to 1024; in each row the longest document has exactly 960 tokens.
All inputs are finite; a program needn't handle non-finite values.
Results may differ from a plain program's by a relative error of at most 0.018.
Values may be sent and summed in bfloat16 or wider, within the bound.
A program may use at most 256 MiB of HBM per device.

v0:
```python
from functools import partial

import jax
import jax.numpy as jnp
from jax import lax
from jax.sharding import PartitionSpec as P

eps_norm = 1e-06
floor_gap = 1e-05
rate_scale = 8.0


def prefix(value, axis, combine, identity, reverse):
    peers, here = (lax.axis_size(axis), lax.axis_index(axis))
    everything = jax.tree.map(lambda part: lax.all_gather(part, axis), value)
    start = jax.tree.map(
        lambda part, zero: jnp.broadcast_to(jnp.asarray(zero, part.dtype), part.shape),
        value,
        identity,
    )

    def hop(k, before):
        at = peers - 1 - k if reverse else k
        reached = at > here if reverse else at < here
        new = combine(before, jax.tree.map(lambda part: part[at], everything))
        return jax.tree.map(lambda a, b: jnp.where(reached, a, b), new, before)

    return lax.fori_loop(0, peers, hop, start)


def from_behind(value, axis, steps):
    count = lax.axis_size(axis)
    first, last = (max(0, -steps), min(count, count - steps))
    return lax.ppermute(value, axis, [(source, source + steps) for source in range(first, last)])


def matmul(left, right):
    return jnp.dot(left, right, preferred_element_type=jnp.float32)


def left_product(left, right):
    return lax.dot_general(
        left, right, (((0,), (0,)), ((), ())), preferred_element_type=jnp.float32
    )


def right_product(left, right):
    return lax.dot_general(
        left, right, (((1,), (1,)), ((), ())), preferred_element_type=jnp.float32
    )


def normed(values, gain):
    return values * lax.rsqrt(jnp.mean(values * values, axis=-1, keepdims=True) + eps_norm) * gain


def combine(early, late):
    return (early[0] * late[0], late[0] * early[1] + late[1])


def convolve(extended, taps, bias, masks):
    rows = extended.shape[0] - 3
    total = bias + taps[:, 0] * extended[3:]
    for k in range(1, 4):
        total = total + jnp.where(masks[k - 1], taps[:, k] * extended[3 - k : 3 - k + rows], 0.0)
    return total


def recur_inputs(pre_decay, pre_inject, conv_val, scale, first):
    rgate = jax.nn.sigmoid(pre_decay)
    igate = jax.nn.sigmoid(pre_inject)
    log_a = -rate_scale * rgate * scale
    gap = -jnp.expm1(2.0 * log_a)
    mult = jnp.where(first, 1.0, jnp.sqrt(jnp.maximum(gap, floor_gap)))
    decay = jnp.where(first, 0.0, jnp.exp(log_a))
    return (decay, mult * igate * conv_val)


def gelu_product(left, right):
    return jax.nn.gelu(left) * right


def carry_forward(summary, width):
    identity = (jnp.ones((width,), jnp.float32), jnp.zeros((width,), jnp.float32))
    return prefix(summary, "seq", combine, identity, False)[1]


def carry_backward(summary, width):
    identity = (jnp.ones((width,), jnp.float32), jnp.zeros((width,), jnp.float32))
    return prefix(summary, "seq", combine, identity, True)[1]


def local(
    tokens,
    cotangent,
    doc_lengths,
    decay_exponent,
    branch_weight,
    input_weight,
    decay_weight,
    inject_weight,
    output_weight,
    mlp_gate,
    mlp_up,
    mlp_down,
    first_gain,
    second_gain,
    conv_taps,
    conv_bias,
    decay_bias,
    inject_bias,
):
    gathered = (
        lax.all_gather(branch_weight, ("seq", "dp"), axis=0, tiled=True),
        lax.all_gather(input_weight, ("seq", "dp"), axis=0, tiled=True),
        lax.all_gather(decay_weight, ("seq", "dp"), axis=0, tiled=True),
        lax.all_gather(inject_weight, ("seq", "dp"), axis=0, tiled=True),
        lax.all_gather(output_weight, ("seq", "dp"), axis=0, tiled=True),
        lax.all_gather(mlp_gate, ("seq", "dp"), axis=0, tiled=True),
        lax.all_gather(mlp_up, ("seq", "dp"), axis=0, tiled=True),
        lax.all_gather(mlp_down, ("seq", "dp"), axis=0, tiled=True),
        lax.all_gather(first_gain, ("seq", "dp"), axis=0, tiled=True),
        lax.all_gather(second_gain, ("seq", "dp"), axis=0, tiled=True),
        lax.all_gather(conv_taps, ("seq", "dp"), axis=0, tiled=True),
        lax.all_gather(conv_bias, ("seq", "dp"), axis=0, tiled=True),
        lax.all_gather(decay_bias, ("seq", "dp"), axis=0, tiled=True),
        lax.all_gather(inject_bias, ("seq", "dp"), axis=0, tiled=True),
    )
    (
        w_branch,
        w_input,
        w_decay,
        w_inject,
        w_output,
        w_gate,
        w_up,
        w_down,
        gain_low_one,
        gain_low_two,
        taps_low,
        cbias_low,
        dbias_low,
        ibias_low,
    ) = gathered
    gain_one = gain_low_one.astype(jnp.float32)
    gain_two = gain_low_two.astype(jnp.float32)
    taps = taps_low.astype(jnp.float32)
    cbias = cbias_low.astype(jnp.float32)
    dbias = dbias_low.astype(jnp.float32)
    ibias = ibias_low.astype(jnp.float32)
    rows = tokens.shape[1]
    width = w_input.shape[1]
    scale = jnp.exp2(-decay_exponent.astype(jnp.float32))
    index = lax.axis_index("seq")
    positions = index * rows - 3 + jnp.arange(rows + 3, dtype=jnp.int32)
    lengths = doc_lengths[0]
    ends = jnp.cumsum(lengths)
    starts = ends - lengths
    seg = jnp.sum((ends[None, :] <= positions[:, None]).astype(jnp.int32), axis=1)
    first = jnp.any(starts[None, :] == positions[3:, None], axis=1)[:, None]
    seg_here = seg[3:]
    masks = [
        ((seg[3 - k : 3 - k + rows] == seg_here) & (positions[3 - k : 3 - k + rows] >= 0))[:, None]
        for k in range(1, 4)
    ]
    x_val = tokens[0].astype(jnp.float32)
    n_one_f, pull_one = jax.vjp(normed, x_val, gain_one)
    n_one = n_one_f.astype(jnp.bfloat16)
    gate_pre = matmul(n_one, w_branch)
    gated, gelu_pull = jax.vjp(jax.nn.gelu, gate_pre)
    u_low = matmul(n_one, w_input).astype(jnp.bfloat16)
    behind = from_behind(u_low[rows - 3 :], "seq", 1)
    extended = jnp.concatenate([behind, u_low], 0).astype(jnp.float32)
    conv_pre, conv_pull = jax.vjp(partial(convolve, masks=masks), extended, taps, cbias)
    conv_low = conv_pre.astype(jnp.bfloat16)
    conv_val = conv_low.astype(jnp.float32)
    pre_decay = matmul(conv_low, w_decay) + dbias
    pre_inject = matmul(conv_low, w_inject) + ibias
    (decay, drive), recur_pull = jax.vjp(
        partial(recur_inputs, scale=scale, first=first), pre_decay, pre_inject, conv_val
    )
    cum_decay, local_state = lax.associative_scan(combine, (decay, drive), axis=0)
    incoming = carry_forward((cum_decay[-1], local_state[-1]), width)
    state = local_state + cum_decay * incoming
    mixed = (state * gated).astype(jnp.bfloat16)
    x_one = x_val + matmul(mixed, w_output)
    n_two_f, pull_two = jax.vjp(normed, x_one, gain_two)
    n_two = n_two_f.astype(jnp.bfloat16)
    p_one = matmul(n_two, w_gate)
    p_two = matmul(n_two, w_up)
    hidden_f, mix_pull = jax.vjp(gelu_product, p_one, p_two)
    hidden = hidden_f.astype(jnp.bfloat16)
    x_two = x_one + matmul(hidden, w_down)
    activations = x_two.astype(jnp.bfloat16)[None]
    cot_low = cotangent[0]
    cot_val = cot_low.astype(jnp.float32)
    grad_down = left_product(hidden, cot_low)
    d_hidden = right_product(cot_low, w_down)
    d_pone_f, d_ptwo_f = mix_pull(d_hidden)
    d_pone = d_pone_f.astype(jnp.bfloat16)
    d_ptwo = d_ptwo_f.astype(jnp.bfloat16)
    grad_gate = left_product(n_two, d_pone)
    grad_up = left_product(n_two, d_ptwo)
    d_ntwo = right_product(d_pone, w_gate) + right_product(d_ptwo, w_up)
    d_xone_norm, grad_gain_two = pull_two(d_ntwo)
    d_xone = cot_val + d_xone_norm
    d_out = d_xone.astype(jnp.bfloat16)
    grad_output = left_product(mixed, d_out)
    d_mixed = right_product(d_out, w_output)
    d_state = d_mixed * gated
    d_gpre = gelu_pull(d_mixed * state)[0].astype(jnp.bfloat16)
    grad_branch = left_product(n_one, d_gpre)
    d_none = right_product(d_gpre, w_branch)
    next_decay = jnp.concatenate([decay[1:], jnp.ones((1, width), jnp.float32)], 0)
    tail_prod, local_adjoint = lax.associative_scan(
        combine, (next_decay, d_state), reverse=True, axis=0
    )
    from_right = carry_backward((cum_decay[-1], decay[0] * local_adjoint[0]), width)
    adjoint = local_adjoint + tail_prod * from_right
    previous = jnp.concatenate([incoming[None], state[:-1]], 0)
    d_rdecay_f, d_rinject_f, d_conv_val = recur_pull((adjoint * previous, adjoint))
    d_rdecay = d_rdecay_f.astype(jnp.bfloat16)
    d_rinject = d_rinject_f.astype(jnp.bfloat16)
    grad_decay = left_product(conv_low, d_rdecay)
    grad_inject = left_product(conv_low, d_rinject)
    grad_dbias = jnp.sum(d_rdecay.astype(jnp.float32), axis=0)
    grad_ibias = jnp.sum(d_rinject.astype(jnp.float32), axis=0)
    d_conv = d_conv_val + right_product(d_rdecay, w_decay) + right_product(d_rinject, w_inject)
    d_extended, grad_taps, grad_cbias = conv_pull(d_conv)
    returned = from_behind(d_extended[:3], "seq", -1)
    d_u = d_extended[3:] + jnp.concatenate([jnp.zeros((rows - 3, width), jnp.float32), returned], 0)
    d_u_low = d_u.astype(jnp.bfloat16)
    grad_input = left_product(n_one, d_u_low)
    d_none = d_none + right_product(d_u_low, w_input)
    d_x_norm, grad_gain_one = pull_one(d_none)
    d_tokens = (d_xone + d_x_norm)[None]
    all_part = (
        lax.psum_scatter(
            grad_branch.astype(jnp.bfloat16), "seq", scatter_dimension=0, tiled=True
        ).astype(jnp.float32),
        lax.psum_scatter(
            grad_input.astype(jnp.bfloat16), "seq", scatter_dimension=0, tiled=True
        ).astype(jnp.float32),
        lax.psum_scatter(
            grad_decay.astype(jnp.bfloat16), "seq", scatter_dimension=0, tiled=True
        ).astype(jnp.float32),
        lax.psum_scatter(
            grad_inject.astype(jnp.bfloat16), "seq", scatter_dimension=0, tiled=True
        ).astype(jnp.float32),
        lax.psum_scatter(
            grad_output.astype(jnp.bfloat16), "seq", scatter_dimension=0, tiled=True
        ).astype(jnp.float32),
        lax.psum_scatter(
            grad_gate.astype(jnp.bfloat16), "seq", scatter_dimension=0, tiled=True
        ).astype(jnp.float32),
        lax.psum_scatter(
            grad_up.astype(jnp.bfloat16), "seq", scatter_dimension=0, tiled=True
        ).astype(jnp.float32),
        lax.psum_scatter(
            grad_down.astype(jnp.bfloat16), "seq", scatter_dimension=0, tiled=True
        ).astype(jnp.float32),
        lax.psum_scatter(
            grad_gain_one.astype(jnp.bfloat16), "seq", scatter_dimension=0, tiled=True
        ).astype(jnp.float32),
        lax.psum_scatter(
            grad_gain_two.astype(jnp.bfloat16), "seq", scatter_dimension=0, tiled=True
        ).astype(jnp.float32),
        lax.psum_scatter(
            grad_taps.astype(jnp.bfloat16), "seq", scatter_dimension=0, tiled=True
        ).astype(jnp.float32),
        lax.psum_scatter(
            grad_cbias.astype(jnp.bfloat16), "seq", scatter_dimension=0, tiled=True
        ).astype(jnp.float32),
        lax.psum_scatter(
            grad_dbias.astype(jnp.bfloat16), "seq", scatter_dimension=0, tiled=True
        ).astype(jnp.float32),
        lax.psum_scatter(
            grad_ibias.astype(jnp.bfloat16), "seq", scatter_dimension=0, tiled=True
        ).astype(jnp.float32),
    )
    (
        grad_branch,
        grad_input,
        grad_decay,
        grad_inject,
        grad_output,
        grad_gate,
        grad_up,
        grad_down,
        grad_gain_one,
        grad_gain_two,
        grad_taps,
        grad_cbias,
        grad_dbias,
        grad_ibias,
    ) = (
        lax.psum_scatter(
            all_part[0].astype(jnp.bfloat16), "dp", scatter_dimension=0, tiled=True
        ).astype(jnp.float32),
        lax.psum_scatter(
            all_part[1].astype(jnp.bfloat16), "dp", scatter_dimension=0, tiled=True
        ).astype(jnp.float32),
        lax.psum_scatter(
            all_part[2].astype(jnp.bfloat16), "dp", scatter_dimension=0, tiled=True
        ).astype(jnp.float32),
        lax.psum_scatter(
            all_part[3].astype(jnp.bfloat16), "dp", scatter_dimension=0, tiled=True
        ).astype(jnp.float32),
        lax.psum_scatter(
            all_part[4].astype(jnp.bfloat16), "dp", scatter_dimension=0, tiled=True
        ).astype(jnp.float32),
        lax.psum_scatter(
            all_part[5].astype(jnp.bfloat16), "dp", scatter_dimension=0, tiled=True
        ).astype(jnp.float32),
        lax.psum_scatter(
            all_part[6].astype(jnp.bfloat16), "dp", scatter_dimension=0, tiled=True
        ).astype(jnp.float32),
        lax.psum_scatter(
            all_part[7].astype(jnp.bfloat16), "dp", scatter_dimension=0, tiled=True
        ).astype(jnp.float32),
        lax.psum_scatter(
            all_part[8].astype(jnp.bfloat16), "dp", scatter_dimension=0, tiled=True
        ).astype(jnp.float32),
        lax.psum_scatter(
            all_part[9].astype(jnp.bfloat16), "dp", scatter_dimension=0, tiled=True
        ).astype(jnp.float32),
        lax.psum_scatter(
            all_part[10].astype(jnp.bfloat16), "dp", scatter_dimension=0, tiled=True
        ).astype(jnp.float32),
        lax.psum_scatter(
            all_part[11].astype(jnp.bfloat16), "dp", scatter_dimension=0, tiled=True
        ).astype(jnp.float32),
        lax.psum_scatter(
            all_part[12].astype(jnp.bfloat16), "dp", scatter_dimension=0, tiled=True
        ).astype(jnp.float32),
        lax.psum_scatter(
            all_part[13].astype(jnp.bfloat16), "dp", scatter_dimension=0, tiled=True
        ).astype(jnp.float32),
    )
    return (
        activations,
        d_tokens,
        grad_branch,
        grad_input,
        grad_decay,
        grad_inject,
        grad_output,
        grad_gate,
        grad_up,
        grad_down,
        grad_gain_one,
        grad_gain_two,
        grad_taps,
        grad_cbias,
        grad_dbias,
        grad_ibias,
    )


def solution(mesh):
    in_specs = (
        P("dp", "seq", None),
        P("dp", "seq", None),
        P("dp", None),
        P(),
        P(("seq", "dp"), None),
        P(("seq", "dp"), None),
        P(("seq", "dp"), None),
        P(("seq", "dp"), None),
        P(("seq", "dp"), None),
        P(("seq", "dp"), None),
        P(("seq", "dp"), None),
        P(("seq", "dp"), None),
        P(("seq", "dp")),
        P(("seq", "dp")),
        P(("seq", "dp"), None),
        P(("seq", "dp")),
        P(("seq", "dp")),
        P(("seq", "dp")),
    )
    out_specs = (
        P("dp", "seq", None),
        P("dp", "seq", None),
        P(("seq", "dp"), None),
        P(("seq", "dp"), None),
        P(("seq", "dp"), None),
        P(("seq", "dp"), None),
        P(("seq", "dp"), None),
        P(("seq", "dp"), None),
        P(("seq", "dp"), None),
        P(("seq", "dp"), None),
        P(("seq", "dp")),
        P(("seq", "dp")),
        P(("seq", "dp"), None),
        P(("seq", "dp")),
        P(("seq", "dp")),
        P(("seq", "dp")),
    )
    return jax.shard_map(local, mesh=mesh, in_specs=in_specs, out_specs=out_specs, check_vma=False)
```

profile of v0, /device:TPU:0, one launch (start us, length us, event | category | flops | bytes accessed | tf_op | source)
XLA Modules:
  0.0 1399.6 jit_solution(18086398510768843468)
XLA Ops:
  16.9 42.4 %all-reduce.83 = (bf16[1024]{0:T(1024)(128)(2,1)S(1)}, bf16[1536]{0:T(1024)(128)(2,1)S(1)}, bf16[1536]{0:T(1024)(128)(2,1)S(1)}, bf16[1536]{0:T(1024)(128)(2,1)S(1)}, bf16[1024]{0:T(1024)(128)(2,1)S(1)}) all-reduce(bf16[1024]{0:T(1024)(128)(2,1)S(1)} %dynamic-update-slice.1, ...), channel_id=1, replica_groups=mesh['seq'=8,'dp'=4] {'seq','dp'}, use_global_device_ids=true, to_apply=%add.68 | all-reduce | flops 6656 | bytes 26624
  62.2 66.2 %all-gather = bf16[32,48,4]{1,2,0:T(4,128)(2,1)S(1)} all-gather(bf16[1,48,4]{1,2,0:T(4,128)(2,1)} %bitcast.100), channel_id=1, replica_groups=mesh['seq'=8,'dp'=4] {'seq','dp'}, dimensions={0}, use_global_device_ids=true | all-gather | bytes 12672 | tf_op jit(solution)/shard_map/all_gather | solution.py:124
  141.6 62.0 %all-gather.17.cloned.1.call-done = bf16[1536,1536]{1,0:T(8,128)(2,1)} async-done(((bf16[48,1536]{1,0:T(8,128)(2,1)}), bf16[1536,1536]{1,0:T(8,128)(2,1)}) %all-gather.17.cloned.1.call-update) | async-done | bytes 4718608 | tf_op jit(solution)/shard_map/all_gather | solution.py:117
  203.6 4.9 convert_multiply_fusion.5
  295.3 14.0 %all-gather.2 = f32[8,1,1536]{2,1,0:T(1,128)S(1)} all-gather(f32[1,1,1536]{2,1,0:T(1,128)S(1)} %add_bitcast_fusion), channel_id=1, replica_groups=mesh['seq'=8,'dp'=4] {'seq'}, dimensions={0}, use_global_device_ids=true | all-gather | bytes 55296 | tf_op jit(solution)/shard_map/all_gather | solution.py:15
  318.4 14.2 %all-gather.1 = f32[8,1,1536]{2,1,0:T(1,128)S(1)} all-gather(f32[1,1,1536]{2,1,0:T(1,128)S(1)} %add_bitcast_fusion.1), channel_id=1, replica_groups=mesh['seq'=8,'dp'=4] {'seq'}, dimensions={0}, use_global_device_ids=true | all-gather | bytes 55296 | tf_op jit(solution)/shard_map/all_gather | solution.py:15
  332.6 6.3 slice.581
  338.9 6.3 slice.588
  345.2 3.8 slice.579
  349.0 7.0 while.30
  356.7 4.5 multiply_convert_fusion.2
  363.9 32.3 %all-gather.23.cloned.1.call-done = bf16[1024,3072]{1,0:T(8,128)(2,1)} async-done(((bf16[32,3072]{1,0:T(8,128)(2,1)}), bf16[1024,3072]{1,0:T(8,128)(2,1)}) %all-gather.23.cloned.1.call-update) | async-done | bytes 6291472 | tf_op jit(solution)/shard_map/all_gather | solution.py:119
  396.2 5.0 fusion.96
  401.2 66.1 %all-gather.25.cloned.1.call-done = bf16[1024,3072]{1,0:T(8,128)(2,1)} async-done(((bf16[32,3072]{1,0:T(8,128)(2,1)}), bf16[1024,3072]{1,0:T(8,128)(2,1)}) %all-gather.25.cloned.1.call-update) | async-done | bytes 6291472 | tf_op jit(solution)/shard_map/all_gather | solution.py:120
  467.2 4.9 fusion.97
  472.1 66.1 %all-gather.27.cloned.1.call-done = bf16[3072,1024]{1,0:T(8,128)(2,1)} async-done(((bf16[96,1024]{1,0:T(8,128)(2,1)}), bf16[3072,1024]{1,0:T(8,128)(2,1)}) %all-gather.27.cloned.1.call-update) | async-done | bytes 6291472 | tf_op jit(solution)/shard_map/all_gather | solution.py:121
  538.2 7.6 multiply_convert_fusion
  545.8 5.6 fusion.98
  562.6 6.3 slice.583
  568.9 6.3 slice.585
  582.6 13.0 slice.594
  671.0 3.8 convolution_convert_fusion.7
  693.2 6.4 slice.633
  710.9 14.0 all-gather.3
  734.1 6.8 rev.9
  740.9 6.9 rev.8
  747.8 7.1 while.31
  760.0 4.2 convolution_add_fusion.1
  781.7 4.5 convolution_convert_fusion.4
  787.4 4.4 convolution_convert_fusion.3
  793.0 4.5 convolution_convert_fusion.2
  800.0 12.2 reduce-scatter.25.cloned.1.call-done
  812.3 56.1 %reduce-scatter.29.cloned.1.call-done = bf16[192,1536]{1,0:T(8,128)(2,1)} async-done(((bf16[1536,1536]{1,0:T(8,128)(2,1)}), bf16[192,1536]{1,0:T(8,128)(2,1)}) %reduce-scatter.29.cloned.1.call-update) | async-done | bytes 589840 | tf_op jit(solution)/shard_map/reduce_scatter | solution.py:244
  868.5 55.6 %reduce-scatter.33.cloned.1.call-done = bf16[192,1536]{1,0:T(8,128)(2,1)} async-done(((bf16[1536,1536]{1,0:T(8,128)(2,1)}), bf16[192,1536]{1,0:T(8,128)(2,1)}) %reduce-scatter.33.cloned.1.call-update) | async-done | bytes 589840 | tf_op jit(solution)/shard_map/reduce_scatter | solution.py:247
  924.1 70.3 %reduce-scatter.41.cloned.1.call-done = bf16[128,3072]{1,0:T(8,128)(2,1)} async-done(((bf16[1024,3072]{1,0:T(8,128)(2,1)}), bf16[128,3072]{1,0:T(8,128)(2,1)}) %reduce-scatter.41.cloned.1.call-update) | async-done | bytes 786448 | tf_op jit(solution)/shard_map/reduce_scatter | solution.py:253
  994.5 70.3 %reduce-scatter.45.cloned.1.call-done = bf16[128,3072]{1,0:T(8,128)(2,1)} async-done(((bf16[1024,3072]{1,0:T(8,128)(2,1)}), bf16[128,3072]{1,0:T(8,128)(2,1)}) %reduce-scatter.45.cloned.1.call-update) | async-done | bytes 786448 | tf_op jit(solution)/shard_map/reduce_scatter | solution.py:256
  1068.6 4.7 fusion.16
  1073.4 61.7 %reduce-scatter.49.cloned.1.call-done = bf16[384,1024]{1,0:T(8,128)(2,1)} async-done(((bf16[3072,1024]{1,0:T(8,128)(2,1)}), bf16[384,1024]{1,0:T(8,128)(2,1)}) %reduce-scatter.49.cloned.1.call-update) | async-done | bytes 786448 | tf_op jit(solution)/shard_map/reduce_scatter | solution.py:259
  1141.4 26.0 %all-reduce.84 = (bf16[1024]{0:T(1024)(128)(2,1)S(1)}, bf16[1024]{0:T(1024)(128)(2,1)S(1)}, bf16[1536]{0:T(1024)(128)(2,1)S(1)}, bf16[1536]{0:T(1024)(128)(2,1)S(1)}, bf16[1536]{0:T(1024)(128)(2,1)S(1)}) all-reduce(bf16[1024]{0:T(1024)(128)(2,1)S(1)} %get-tuple-element.287, ...), channel_id=18, replica_groups=mesh['seq'=8,'dp'=4] {'seq'}, use_global_device_ids=true, to_apply=%region_28.29.clone | all-reduce | flops 6656 | bytes 26624
  1169.7 10.3 all-reduce.85
  1183.5 8.8 reduce-scatter.39.cloned.1.call-done
  1193.9 25.9 %reduce-scatter.23.cloned.1.call-done = bf16[32,1536]{1,0:T(8,128)(2,1)} async-done(((bf16[128,1536]{1,0:T(8,128)(2,1)}), bf16[32,1536]{1,0:T(8,128)(2,1)}) %reduce-scatter.23.cloned.1.call-update) | async-done | bytes 98320 | tf_op jit(solution)/shard_map/reduce_scatter | solution.py:297
  1221.4 25.7 %reduce-scatter.27.cloned.1.call-done = bf16[32,1536]{1,0:T(8,128)(2,1)} async-done(((bf16[128,1536]{1,0:T(8,128)(2,1)}), bf16[32,1536]{1,0:T(8,128)(2,1)}) %reduce-scatter.27.cloned.1.call-update) | async-done | bytes 98320 | tf_op jit(solution)/shard_map/reduce_scatter | solution.py:300
  1248.7 26.6 %reduce-scatter.31.cloned.1.call-done = bf16[48,1536]{1,0:T(8,128)(2,1)} async-done(((bf16[192,1536]{1,0:T(8,128)(2,1)}), bf16[48,1536]{1,0:T(8,128)(2,1)}) %reduce-scatter.31.cloned.1.call-update) | async-done | bytes 147472 | tf_op jit(solution)/shard_map/reduce_scatter | solution.py:303
  1276.9 26.3 %reduce-scatter.35.cloned.1.call-done = bf16[48,1536]{1,0:T(8,128)(2,1)} async-done(((bf16[192,1536]{1,0:T(8,128)(2,1)}), bf16[48,1536]{1,0:T(8,128)(2,1)}) %reduce-scatter.35.cloned.1.call-update) | async-done | bytes 147472 | tf_op jit(solution)/shard_map/reduce_scatter | solution.py:306
  1304.9 27.7 %reduce-scatter.43.cloned.1.call-done = bf16[32,3072]{1,0:T(8,128)(2,1)} async-done(((bf16[128,3072]{1,0:T(8,128)(2,1)}), bf16[32,3072]{1,0:T(8,128)(2,1)}) %reduce-scatter.43.cloned.1.call-update) | async-done | bytes 196624 | tf_op jit(solution)/shard_map/reduce_scatter | solution.py:312
  1334.3 27.4 %reduce-scatter.47.cloned.1.call-done = bf16[32,3072]{1,0:T(8,128)(2,1)} async-done(((bf16[128,3072]{1,0:T(8,128)(2,1)}), bf16[32,3072]{1,0:T(8,128)(2,1)}) %reduce-scatter.47.cloned.1.call-update) | async-done | bytes 196624 | tf_op jit(solution)/shard_map/reduce_scatter | solution.py:315
  1363.4 27.6 %reduce-scatter.51.cloned.1.call-done = bf16[96,1024]{1,0:T(8,128)(2,1)} async-done(((bf16[384,1024]{1,0:T(8,128)(2,1)}), bf16[96,1024]{1,0:T(8,128)(2,1)}) %reduce-scatter.51.cloned.1.call-update) | async-done | bytes 196624 | tf_op jit(solution)/shard_map/reduce_scatter | solution.py:318
  (564 shorter events, 323.9 us)
Async XLA Ops:
  7.2 122.7 %all-gather.13.cloned.1.call-start = ((), (), s32[]{:S(2)}) async-start(), calls=%async_computation.17 | async-start | bytes 3244032 | tf_op jit(solution)/shard_map/all_gather | solution.py:115
  7.9 130.4 %all-gather.15.cloned.1.call-start = ((), (), s32[]{:S(2)}) async-start(), calls=%async_computation.18 | async-start | bytes 4866048 | tf_op jit(solution)/shard_map/all_gather | solution.py:116
  8.7 194.9 %all-gather.17.cloned.1.call-start = ((), (), s32[]{:S(2)}) async-start(), calls=%async_computation.19 | async-start | bytes 4866048 | tf_op jit(solution)/shard_map/all_gather | solution.py:117
  9.4 347.3 %all-gather.19.cloned.1.call-start = ((), (), s32[]{:S(2)}) async-start(), calls=%async_computation.20 | async-start | bytes 3244032 | tf_op jit(solution)/shard_map/all_gather | solution.py:114
  10.0 351.2 %all-gather.21.cloned.1.call-start = ((), (), s32[]{:S(2)}) async-start(), calls=%async_computation.21 | async-start | bytes 3244032 | tf_op jit(solution)/shard_map/all_gather | solution.py:118
  10.6 385.6 %all-gather.23.cloned.1.call-start = ((), (), s32[]{:S(2)}) async-start(), calls=%async_computation.22 | async-start | bytes 6488064 | tf_op jit(solution)/shard_map/all_gather | solution.py:119
  11.1 456.1 %all-gather.25.cloned.1.call-start = ((), (), s32[]{:S(2)}) async-start(), calls=%async_computation.23 | async-start | bytes 6488064 | tf_op jit(solution)/shard_map/all_gather | solution.py:120
  11.9 526.3 %all-gather.27.cloned.1.call-start = ((), (), s32[]{:S(2)}) async-start(), calls=%async_computation.24 | async-start | bytes 6488064 | tf_op jit(solution)/shard_map/all_gather | solution.py:121
  12.6 786.1 %reduce-scatter.37.cloned.1.call-start = ((), (), s32[]{:S(2)}) async-start(), calls=%async_computation.33 | async-start | bytes 3538944 | tf_op jit(solution)/shard_map/reduce_scatter | solution.py:250
  59.3 76.1 %copy-start.30 = (f32[1024]{0:T(1024)}, f32[1024]{0:T(1024)S(1)}, u32[]{:S(2)}) copy-start(f32[1024]{0:T(1024)S(1)} %convert_element_type.195) | copy-start | bytes 12292
  60.4 75.0 %copy-start.63 = (f32[128]{0:T(128)}, f32[128]{0:T(128)S(1)}, u32[]{:S(2)}) copy-start(f32[128]{0:T(128)S(1)} %fusion.74) | copy-start | bytes 1540
  62.2 73.2 %copy-start.66 = (pred[128]{0:T(512)(128)(4,1)}, pred[128]{0:T(512)(128)(4,1)S(1)}, u32[]{:S(2)}) copy-start(pred[128]{0:T(512)(128)(4,1)S(1)} %get-tuple-element.413) | copy-start | bytes 388
  62.2 73.2 %copy-start.69 = (pred[128]{0:T(512)(128)(4,1)}, pred[128]{0:T(512)(128)(4,1)S(1)}, u32[]{:S(2)}) copy-start(pred[128]{0:T(512)(128)(4,1)S(1)} %get-tuple-element.414) | copy-start | bytes 388
  62.2 73.2 %copy-start.72 = (pred[128]{0:T(512)(128)(4,1)}, pred[128]{0:T(512)(128)(4,1)S(1)}, u32[]{:S(2)}) copy-start(pred[128]{0:T(512)(128)(4,1)S(1)} %get-tuple-element.415) | copy-start | bytes 388
  129.9 73.7 %copy-start.43 = (f32[1536]{0:T(1024)}, f32[1536]{0:T(1024)S(1)}, u32[]{:S(2)}) copy-start(f32[1536]{0:T(1024)S(1)} %get-tuple-element.412) | copy-start | bytes 18436
  132.6 2.1 collective-permute-start
  134.0 69.6 %copy-start.76 = (pred[128]{0:T(512)(128)(4,1)}, pred[128]{0:T(512)(128)(4,1)S(1)}, u32[]{:S(2)}) copy-start(pred[128]{0:T(512)(128)(4,1)S(1)} %compare_reduce_fusion) | copy-start | bytes 388
  208.5 61.7 %copy-start.4 = (f32[128,1536]{1,0:T(8,128)}, f32[128,1536]{1,0:T(8,128)S(1)}, u32[]{:S(2)}) copy-start(f32[128,1536]{1,0:T(8,128)S(1)} %get-tuple-element.346) | copy-start | bytes 2359300
  291.5 53.7 %copy-start.17 = (f32[63,1536]{1,0:T(8,128)S(1)}, f32[63,1536]{1,0:T(8,128)}, u32[]{:S(2)}) copy-start(f32[63,1536]{1,0:T(8,128)} %slice.578) | copy-start | bytes 1161220
  294.5 54.5 %copy-start.26 = (f32[1536]{0:T(1024)S(1)}, f32[1536]{0:T(1024)}, u32[]{:S(2)}) copy-start(f32[1536]{0:T(1024)} %custom-call) | copy-start | bytes 18436
  309.3 47.4 %copy-start.1 = (bf16[1,128,1024]{2,1,0:T(8,128)(2,1)S(1)}, bf16[1,128,1024]{2,1,0:T(8,128)(2,1)}, u32[]{:S(2)}) copy-start(bf16[1,128,1024]{2,1,0:T(8,128)(2,1)} %param.22) | copy-start | bytes 786436
  309.3 47.4 %copy-start.31 = (f32[1024]{0:T(1024)S(1)}, f32[1024]{0:T(1024)}, u32[]{:S(2)}) copy-start(f32[1024]{0:T(1024)} %copy-done.30) | copy-start | bytes 12292
  309.3 47.4 %copy-start.64 = (f32[128]{0:T(128)S(1)}, f32[128]{0:T(128)}, u32[]{:S(2)}) copy-start(f32[128]{0:T(128)} %copy-done.63) | copy-start | bytes 1540
  613.6 29.2 %copy-start.14 = (f32[64,1536]{1,0:T(8,128)S(1)}, f32[64,1536]{1,0:T(8,128)}, u32[]{:S(2)}) copy-start(f32[64,1536]{1,0:T(8,128)} %get-tuple-element.353) | copy-start | bytes 1179652
  613.6 185.7 %reduce-scatter.21.cloned.1.call-start = ((), (), s32[]{:S(2)}) async-start(), calls=%async_computation.25 | async-start | bytes 3538944 | tf_op jit(solution)/shard_map/reduce_scatter | solution.py:238
  676.9 135.3 %reduce-scatter.25.cloned.1.call-start = ((), (), s32[]{:S(2)}) async-start(), calls=%async_computation.27 | async-start | bytes 3538944 | tf_op jit(solution)/shard_map/reduce_scatter | solution.py:241
  703.9 24.0 %copy-start.18 = (f32[63,1536]{1,0:T(8,128)S(1)}, f32[63,1536]{1,0:T(8,128)}, u32[]{:S(2)}) copy-start(f32[63,1536]{1,0:T(8,128)} %get-tuple-element.351) | copy-start | bytes 1161220
  731.6 23.3 %copy-start.44 = (f32[1536]{0:T(1024)S(1)}, f32[1536]{0:T(1024)}, u32[]{:S(2)}) copy-start(f32[1536]{0:T(1024)} %copy-done.43) | copy-start | bytes 18436
  766.5 3.1 collective-permute-start.1
  772.3 96.1 %reduce-scatter.29.cloned.1.call-start = ((), (), s32[]{:S(2)}) async-start(), calls=%async_computation.29 | async-start | bytes 5308416 | tf_op jit(solution)/shard_map/reduce_scatter | solution.py:244
  776.0 148.0 %reduce-scatter.33.cloned.1.call-start = ((), (), s32[]{:S(2)}) async-start(), calls=%async_computation.31 | async-start | bytes 5308416 | tf_op jit(solution)/shard_map/reduce_scatter | solution.py:247
  780.5 213.8 %reduce-scatter.41.cloned.1.call-start = ((), (), s32[]{:S(2)}) async-start(), calls=%async_computation.35 | async-start | bytes 7077888 | tf_op jit(solution)/shard_map/reduce_scatter | solution.py:253
  786.2 278.5 %reduce-scatter.45.cloned.1.call-start = ((), (), s32[]{:S(2)}) async-start(), calls=%async_computation.37 | async-start | bytes 7077888 | tf_op jit(solution)/shard_map/reduce_scatter | solution.py:256
  791.8 343.3 %reduce-scatter.49.cloned.1.call-start = ((), (), s32[]{:S(2)}) async-start(), calls=%async_computation.39 | async-start | bytes 7077888 | tf_op jit(solution)/shard_map/reduce_scatter | solution.py:259
  797.5 267.3 %copy-start.82 = (u32[32]{0:T(128)S(1)}, u32[32]{0:T(128)}, u32[]{:S(2)}) copy-start(u32[32]{0:T(128)} %constant.302) | copy-start | bytes 388
  797.5 269.2 %copy-start.81 = (u32[32]{0:T(128)S(1)}, u32[32]{0:T(128)}, u32[]{:S(2)}) copy-start(u32[32]{0:T(128)} %constant.306) | copy-start | bytes 388
  797.5 371.3 %reduce-scatter.53.cloned.1.call-start = ((), (), s32[]{:S(2)}) async-start(), calls=%async_computation.41 | async-start | bytes 442368
  798.7 393.7 %reduce-scatter.39.cloned.1.call-start = ((), (), s32[]{:S(2)}) async-start(), calls=%async_computation.34 | async-start | bytes 491520 | tf_op jit(solution)/shard_map/reduce_scatter | solution.py:309
  799.3 420.5 %reduce-scatter.23.cloned.1.call-start = ((), (), s32[]{:S(2)}) async-start(), calls=%async_computation.26 | async-start | bytes 491520 | tf_op jit(solution)/shard_map/reduce_scatter | solution.py:297
  800.0 447.1 %reduce-scatter.27.cloned.1.call-start = ((), (), s32[]{:S(2)}) async-start(), calls=%async_computation.28 | async-start | bytes 491520 | tf_op jit(solution)/shard_map/reduce_scatter | solution.py:300
  812.2 463.1 %reduce-scatter.31.cloned.1.call-start = ((), (), s32[]{:S(2)}) async-start(), calls=%async_computation.30 | async-start | bytes 737280 | tf_op jit(solution)/shard_map/reduce_scatter | solution.py:303
  868.4 434.8 %reduce-scatter.35.cloned.1.call-start = ((), (), s32[]{:S(2)}) async-start(), calls=%async_computation.32 | async-start | bytes 737280 | tf_op jit(solution)/shard_map/reduce_scatter | solution.py:306
  924.0 408.5 %reduce-scatter.43.cloned.1.call-start = ((), (), s32[]{:S(2)}) async-start(), calls=%async_computation.36 | async-start | bytes 983040 | tf_op jit(solution)/shard_map/reduce_scatter | solution.py:312
  994.4 367.3 %reduce-scatter.47.cloned.1.call-start = ((), (), s32[]{:S(2)}) async-start(), calls=%async_computation.38 | async-start | bytes 983040 | tf_op jit(solution)/shard_map/reduce_scatter | solution.py:315
  1064.8 326.2 %reduce-scatter.51.cloned.1.call-start = ((), (), s32[]{:S(2)}) async-start(), calls=%async_computation.40 | async-start | bytes 983040 | tf_op jit(solution)/shard_map/reduce_scatter | solution.py:318
  1068.6 66.5 %copy-start.19 = (bf16[128,1536]{1,0:T(8,128)(2,1)S(1)}, bf16[128,1536]{1,0:T(8,128)(2,1)}, u32[]{:S(2)}) copy-start(bf16[128,1536]{1,0:T(8,128)(2,1)} %get-tuple-element.344) | copy-start | bytes 1179652
  1138.2 29.6 %copy-start.80 = (f32[128]{0:T(128)S(1)}, f32[128]{0:T(128)}, u32[]{:S(2)}) copy-start(f32[128]{0:T(128)} %copy-done.79) | copy-start | bytes 1540
  1138.2 29.6 %copy-start.6 = (f32[128,1024]{1,0:T(8,128)S(1)}, f32[128,1024]{1,0:T(8,128)}, u32[]{:S(2)}) copy-start(f32[128,1024]{1,0:T(8,128)} %copy-done.5) | copy-start | bytes 1572868
  (64 other events, 515.2 us)
Sparse Core Ops, SparseCore 0:
  10.9 61.7 all-gather.12
  75.6 62.6 all-gather.14
  141.2 62.3 all-gather.16
  206.3 57.8 all-gather.18
  267.0 57.9 all-gather.20
  327.7 68.4 all-gather.22
  399.1 68.0 all-gather.24
  470.1 68.0 all-gather.26
  613.7 38.8 reduce-scatter.36
  677.0 38.8 reduce-scatter.20
  772.4 39.7 reduce-scatter.24
  814.4 53.9 reduce-scatter.28
  870.7 53.2 reduce-scatter.32
  926.2 68.1 reduce-scatter.40
  996.5 68.1 reduce-scatter.44
  1066.9 68.1 reduce-scatter.48
  1137.8 28.9 reduce-scatter.52
  1169.7 22.5 reduce-scatter.38
  1195.4 24.4 reduce-scatter.22
  1222.7 24.3 reduce-scatter.26
  1250.2 25.0 reduce-scatter.30
  1278.2 25.0 reduce-scatter.34
  1306.4 26.1 reduce-scatter.42
  1335.6 26.0 reduce-scatter.46
  1364.9 26.0 reduce-scatter.50
where the time goes:
time: 1420 us; the launch traced here: 1400 us
  waiting for transfers between devices  759 us (53%)
  local copies, waits for them, and re-layouts  242 us (17%)
  blocking collectives  187 us (13%)
  matrix products  94.7 us (7%)
  other arithmetic  93 us (7%)
  between operations  18.8 us (1%)
    slice x49, local copies, waits for them, and re-layouts, local(): lax.associative_scan(combine, (next_decay, d_state), reverse=True, axis=0)  108 us
    unnamed x3, blocking collectives  78.7 us
    reduce_scatter x1, waiting for transfers between devices, local(): lax.psum_scatter(grad_gate.astype(jnp.bfloat16), 'seq', scatter_dimension...  70.3 us
    reduce_scatter x1, waiting for transfers between devices, local(): lax.psum_scatter(grad_up.astype(jnp.bfloat16), 'seq', scatter_dimension=0...  70.3 us
    all_gather x1, blocking collectives, local(): lax.all_gather(conv_taps, ('seq', 'dp'), axis=0, tiled=True)  66.2 us
    all_gather x1, waiting for transfers between devices, local(): lax.all_gather(mlp_down, ('seq', 'dp'), axis=0, tiled=True)  66.1 us
    all_gather x1, waiting for transfers between devices, local(): lax.all_gather(mlp_up, ('seq', 'dp'), axis=0, tiled=True)  66.1 us
    all_gather x1, waiting for transfers between devices, local(): lax.all_gather(inject_weight, ('seq', 'dp'), axis=0, tiled=True)  62 us
  transfers between devices with their start and end apart: 27, of which 21 were waited for; matrix products, arithmetic and copies ran while one was open for 25% of the time, Pallas kernels for 0%

commit v1 on v0

v1 whole, which is shorter than its diff:
```python
import itertools
import math
from functools import partial
from types import SimpleNamespace

import jax
import jax.numpy as jnp
from jax import lax
from jax.experimental import pallas as pl
from jax.experimental.pallas import tpu as pltpu
from jax.sharding import Mesh, PartitionSpec as P

f32, bf16 = jnp.float32, jnp.bfloat16
MESH = pl.DeviceIdType.MESH
AXES = ("zh", "zl", "c", "yh", "yl", "xh", "xl")
RING = 4
PLANE = 4
SHARES = RING * 2 * PLANE
SEMS = 512

eps_norm = 1e-06
floor_gap = 1e-05
rate_scale = 8.0
gelu_root = math.sqrt(2.0 / math.pi)
gelu_cube = 0.044715


def dot(left, right):
    return jnp.dot(left, right, preferred_element_type=f32)


def dot_nt(left, right):
    return lax.dot_general(left, right, (((1,), (1,)), ((), ())), preferred_element_type=f32)


def dot_tn(left, right):
    return lax.dot_general(left, right, (((0,), (0,)), ((), ())), preferred_element_type=f32)


def gelu_parts(v):
    t = jnp.tanh(gelu_root * (v + gelu_cube * v * v * v))
    half = 0.5 * (1.0 + t)
    slope = half + 0.5 * v * (1.0 - t * t) * gelu_root * (1.0 + 3.0 * gelu_cube * v * v)
    return v * half, slope


def minus_expm1(y):
    poly = jnp.full_like(y, 1.0 / 8.0)
    poly = 1.0 + y * poly
    for k in (7, 6, 5, 4, 3, 2):
        poly = 1.0 + y * poly * (1.0 / k)
    return jnp.where(y > -0.35, -y * poly, 1.0 - jnp.exp(y))


def inverse_rms(v):
    return lax.rsqrt(jnp.mean(v * v, axis=-1, keepdims=True) + eps_norm)


def loop(total, step, body):
    def run(j, _):
        body(pl.multiple_of(j * step, step))
        return 0

    lax.fori_loop(0, total // step, run, 0)


def layer(dims, *refs):
    T, D, W, F, CW, CF = dims.T, dims.D, dims.W, dims.F, dims.CW, dims.CF
    RD, RW, RF, NL = dims.RD, dims.RW, dims.RF, dims.NL
    M = PLANE * T
    r = SimpleNamespace(**dict(zip(dims.names, refs, strict=True)))

    zh, zl, c = lax.axis_index("zh"), lax.axis_index("zl"), lax.axis_index("c")
    yl, xl = lax.axis_index("yl"), lax.axis_index("xl")
    p = yl * 2 + xl
    px, py, pd = yl * 2 + (1 - xl), (1 - yl) * 2 + xl, (1 - yl) * 2 + (1 - xl)
    to_x, to_y, to_d = {"xl": 1 - xl}, {"yl": 1 - yl}, {"yl": 1 - yl, "xl": 1 - xl}
    plane_peers = ((px, to_x), (py, to_y), (pd, to_d))
    to_core = {"c": 1 - c}
    flat_z = zh * NL + zl
    places = RING * NL * 2
    pos = flat_z * 2 + c

    def place(at):
        return {"zh": at // (2 * NL), "zl": (at // 2) % NL, "c": at % 2}

    count = itertools.count()

    def new(n=1):
        first = next(count)
        for _ in range(n - 1):
            next(count)
        assert first + n <= SEMS
        return first

    sent = []

    def push(src, dst, dev, rsem, pred=None):
        i = new()

        def make():
            return pltpu.make_async_remote_copy(
                src, dst, r.ss.at[i], r.rs.at[rsem], device_id=dev, device_id_type=MESH
            )

        if pred is None:
            make().start()
        else:
            pl.when(pred)(lambda: make().start())
        entry = (make, pred)
        sent.append(entry)
        return entry

    def settle(*entries):
        for entry in entries:
            make, pred = entry
            if pred is None:
                make().wait_send()
            else:
                pl.when(pred)(lambda make=make: make().wait_send())
            sent.remove(entry)

    def arrived(dst, rsem, pred=None):
        def wait():
            pltpu.make_async_remote_copy(
                dst, dst, r.ss.at[0], r.rs.at[rsem], device_id=to_core, device_id_type=MESH
            ).wait_recv()

        if pred is None:
            wait()
        else:
            pl.when(pred)(wait)

    def keep_local(src, dst, rsem):
        pltpu.make_async_copy(src, dst, r.rs.at[rsem]).start()

    new()

    def ds(start, size, unit):
        return pl.ds(pl.multiple_of(start, unit), size)

    class Gather:
        def __init__(self, buf):
            self.buf, half = buf, buf.shape[1] // 2
            self.h0, self.h1 = pl.ds(0, half), pl.ds(half, half)
            self.rx0, self.rx1, self.ry0, self.ry1, self.rd0, self.rd1 = (new() for _ in range(6))
            self.out = []

        def start(self):
            b = self.buf
            own0, own1 = b.at[p, self.h0], b.at[p, self.h1]
            self.out.append(push(own0, own0, to_x, self.rx0))
            self.out.append(push(own1, own1, to_y, self.ry1))
            self.out.append(push(own1, own1, to_x, self.rx1))
            self.out.append(push(own0, own0, to_y, self.ry0))

        def mid(self):
            b = self.buf
            got0, got1 = b.at[px, self.h0], b.at[py, self.h1]
            arrived(got0, self.rx0)
            self.out.append(push(got0, got0, to_y, self.rd0))
            arrived(got1, self.ry1)
            self.out.append(push(got1, got1, to_x, self.rd1))

        def wait_x(self):
            arrived(self.buf.at[px, self.h1], self.rx1)

        def wait_y(self):
            arrived(self.buf.at[py, self.h0], self.ry0)

        def wait_d(self):
            arrived(self.buf.at[pd, self.h0], self.rd0)
            arrived(self.buf.at[pd, self.h1], self.rd1)

        def end(self):
            self.wait_x()
            self.wait_y()
            self.wait_d()
            settle(*self.out)

    class Scatter:
        def __init__(self, buf, recv):
            self.buf, self.recv = buf, recv
            self.half = buf.shape[1] // 2
            self.h0, self.h1 = pl.ds(0, self.half), pl.ds(self.half, self.half)
            self.sems = [new() for _ in range(6)]
            self.out = []

        def start(self):
            b, v, s = self.buf, self.recv, self.sems
            self.out.append(push(b.at[pd, self.h0], v.at[0], to_x, s[0]))
            self.out.append(push(b.at[pd, self.h1], v.at[1], to_y, s[1]))
            self.out.append(push(b.at[px, self.h0], v.at[2], to_x, s[2]))
            self.out.append(push(b.at[py, self.h1], v.at[3], to_y, s[3]))

        def mid(self):
            b, v, s = self.buf, self.recv, self.sems
            arrived(v.at[0], s[0])
            step = 16

            def add0(o):
                b[py, pl.ds(o, step)] = (b[py, pl.ds(o, step)].astype(f32) + v[0, pl.ds(o, step)].astype(f32)).astype(bf16)

            loop(self.half, step, add0)
            self.out.append(push(b.at[py, self.h0], v.at[4], to_y, s[4]))
            arrived(v.at[1], s[1])

            def add1(o):
                q = pl.ds(pl.multiple_of(self.half + o, step), step)
                b[px, q] = (b[px, q].astype(f32) + v[1, pl.ds(o, step)].astype(f32)).astype(bf16)

            loop(self.half, step, add1)
            self.out.append(push(b.at[px, self.h1], v.at[5], to_x, s[5]))

        def end(self):
            for k in (2, 3, 4, 5):
                arrived(self.recv.at[k], self.sems[k])
            settle(*self.out)

        def total(self, half, o, step):
            b, v = self.buf, self.recv
            own = b[p, pl.ds(pl.multiple_of(half * self.half + o, step), step)].astype(f32)
            q = pl.ds(o, step)
            return own + v[2 + half, q].astype(f32) + v[4 + half, q].astype(f32)

        def each(self, step, body):
            for half in (0, 1):
                loop(self.half, step, lambda o: body(pl.multiple_of(half * self.half + o, step), self.total(half, o, step)))

    def z_send(src, block, rz):
        out = []
        for s in (1, 2):
            out.append(push(src, block(zh), {"zh": zh + s}, rz + zh, zh + s < RING))
            out.append(push(src, block(zh), {"zh": zh - s}, rz + zh, zh - s >= 0))
        return out

    def z_forward(block, rz):
        last = RING - 1
        arrived(block(0), rz, zh == last - 1)
        one = push(block(0), block(0), {"zh": zh + 1}, rz, zh == last - 1)
        arrived(block(last), rz + last, zh == 1)
        two = push(block(last), block(last), {"zh": zh - 1}, rz + last, zh == 1)
        return [one, two]

    def z_wait(block, rz):
        last = RING - 1
        arrived(block(0), rz, (zh == 1) | (zh == last))
        arrived(block(1), rz + 1, zh != 1)
        arrived(block(2), rz + 2, zh != 2)
        arrived(block(last), rz + last, (zh == 0) | (zh == last - 1))

    class ZSum:
        def __init__(self, block, slot, add):
            self.block, self.slot, self.add = block, slot, add
            self.sems = new(4)
            self.out = []

        def send(self):
            b, v, s = self.block, self.slot, self.sems
            last = RING - 1
            o = self.out
            o.append(push(b(last), v(1), {"zh": zh + 1}, s + 1, zh == 0))
            o.append(push(b(0), v(3), {"zh": zh - 1}, s + 3, zh == last))
            o.append(push(b(zh + 2), v(1), {"zh": zh + 2}, s + 1, zh == 0))
            o.append(push(b(zh - 2), v(3), {"zh": zh - 2}, s + 3, zh == last))
            o.append(push(b(zh + 1), v(0), {"zh": zh + 1}, s + 0, zh < last))
            o.append(push(b(zh - 1), v(2), {"zh": zh - 1}, s + 2, zh > 0))

        def forward(self):
            b, v, s = self.block, self.slot, self.sems
            last = RING - 1

            def up():
                arrived(v(1), s + 1)
                self.add(last, 1)

            def down():
                arrived(v(3), s + 3)
                self.add(0, 3)

            pl.when(zh == 1)(up)
            self.out.append(push(b(last), v(1), {"zh": zh + 2}, s + 1, zh == 1))
            pl.when(zh == last - 1)(down)
            self.out.append(push(b(0), v(3), {"zh": zh - 2}, s + 3, zh == last - 1))

        def end(self):
            v, s = self.slot, self.sems
            arrived(v(0), s, zh >= 1)
            arrived(v(1), s + 1, zh >= 2)
            arrived(v(2), s + 2, zh <= 2)
            arrived(v(3), s + 3, zh <= 1)
            settle(*self.out)

        def total(self, own, parts):
            for part, pred in zip(parts, (zh >= 1, zh >= 2, zh <= 2, zh <= 1), strict=True):
                own = own + jnp.where(pred, part.astype(f32), 0.0)
            return own

    class Columns:
        def __init__(self, sources, w, R, C):
            self.sources, self.w, self.R, self.C = sources, w, R, C
            self.ra, self.rz, self.rc = new(), new(4), new()
            self.out = []

        def spread(self):
            R, C = self.R, self.C
            for i, src in enumerate(self.sources):
                dst = self.w.at[zh, c, ds(p * R, R, 16), pl.ds(i * C, C)]
                for k, dev in plane_peers:
                    self.out.append(push(src.at[:, ds(k * C, C, 128)], dst, dev, self.ra))
                keep_local(src.at[:, ds(p * C, C, 128)], dst, self.ra)

        def block(self, z):
            return self.w.at[z, c]

        def z_send(self):
            arrived(self.w.at[zh, c], self.ra)
            self.out += z_send(self.block(zh), self.block, self.rz)

        def z_forward(self):
            self.out += z_forward(self.block, self.rz)

        def z_wait(self):
            z_wait(self.block, self.rz)
            half = self.w.at[:, c]
            self.out.append(push(half, half, to_core, self.rc))

        def end(self):
            arrived(self.w.at[:, 1 - c], self.rc)
            settle(*self.out)

    class Rows:
        def __init__(self, src, w, stage, R):
            self.src, self.w, self.stage, self.R = src, w, stage, R
            self.rl, self.rz, self.rp, self.rc = new(), new(4), new(), new()
            self.out = []

        def block(self, z):
            return self.stage.at[z]

        def z_send(self):
            keep_local(self.src, self.block(zh), self.rl)
            self.out += z_send(self.src, self.block, self.rz)

        def z_forward(self):
            self.out += z_forward(self.block, self.rz)

        def z_wait(self):
            R = self.R
            pltpu.make_async_copy(self.src, self.block(zh), r.rs.at[self.rl]).wait()
            z_wait(self.block, self.rz)
            dst = self.w.at[ds((c * PLANE + p) * R, R, 16)]
            for k, dev in plane_peers:
                self.out.append(push(self.stage.at[k], dst, dev, self.rp))
            keep_local(self.stage.at[p], dst, self.rp)

        def plane_wait(self):
            H = PLANE * self.R
            half = self.w.at[ds(c * H, H, 16)]
            arrived(half, self.rp)
            self.out.append(push(half, half, to_core, self.rc))

        def end(self):
            H = PLANE * self.R
            arrived(self.w.at[ds((1 - c) * H, H, 16)], self.rc)
            settle(*self.out)

    class ColumnsGrad:
        def __init__(self, g, other, slots, land, R, lane0, lanes, outs):
            self.g, self.other, self.slots, self.land = g, other, slots, land
            self.R, self.lanes, self.outs = R, pl.ds(lane0, lanes), outs
            self.rc, self.rl = new(), new()
            self.zsum = ZSum(
                lambda z: g.at[z, c, :, self.lanes], lambda k: slots.at[k, :, self.lanes], self.add_slot
            )

        def add_slot(self, z, k):
            g, q = self.g, self.lanes

            def add(o):
                s = pl.ds(o, 16)
                g[z, c, s, q] = (g[z, c, s, q].astype(f32) + self.slots[k, s, q].astype(f32)).astype(bf16)

            loop(PLANE * self.R, 16, add)

        def core_send(self):
            self.pushed = push(
                self.g.at[:, 1 - c, :, self.lanes], self.other.at[:, :, self.lanes], to_core, self.rc
            )

        def z_send(self):
            g, q = self.g, self.lanes
            arrived(self.other.at[:, :, q], self.rc)
            for z in range(RING):

                def add(o):
                    s = pl.ds(o, 16)
                    g[z, c, s, q] = (g[z, c, s, q].astype(f32) + self.other[z, s, q].astype(f32)).astype(bf16)

                loop(PLANE * self.R, 16, add)
            self.zsum.send()

        def z_forward(self):
            self.zsum.forward()

        def plane_send(self):
            g, q, R = self.g, self.lanes, self.R
            self.zsum.end()

            def add(o):
                s = pl.ds(o, 16)
                parts = [self.slots[k, s, q] for k in range(4)]
                g[zh, c, s, q] = self.zsum.total(g[zh, c, s, q].astype(f32), parts).astype(bf16)

            loop(PLANE * R, 16, add)
            dst = self.land.at[p, :, q]
            self.out = [self.pushed]
            for k, dev in plane_peers:
                self.out.append(push(g.at[zh, c, ds(k * R, R, 16), q], dst, dev, self.rl))
            keep_local(g.at[zh, c, ds(p * R, R, 16), q], dst, self.rl)

        def end(self):
            arrived(self.land.at[:, :, self.lanes], self.rl)
            settle(*self.out)
            for lane0, C, out in self.outs:
                for k in range(PLANE):
                    out[:, k * C : (k + 1) * C] = self.land[k, :, lane0 : lane0 + C].astype(f32)

    class RowsGrad:
        def __init__(self, g, other, stage, slots, R, out):
            self.g, self.other, self.stage, self.slots, self.R, self.result = g, other, stage, slots, R, out
            self.rc, self.rl = new(), new()
            self.zsum = ZSum(lambda z: stage.at[z], lambda k: slots.at[k], self.add_slot)

        def add_slot(self, z, k):
            g = self.stage

            def add(o):
                s = pl.ds(o, 16)
                g[z, s] = (g[z, s].astype(f32) + self.slots[k, s].astype(f32)).astype(bf16)

            loop(self.R, 16, add)

        def core_send(self):
            H = PLANE * self.R
            self.out = [push(self.g.at[ds((1 - c) * H, H, 16)], self.other, to_core, self.rc)]

        def plane_send(self):
            R, H, g = self.R, PLANE * self.R, self.g
            arrived(self.other, self.rc)

            def add(o):
                s = ds(c * H + o, 16, 16)
                g[s] = (g[s].astype(f32) + self.other[pl.ds(o, 16)].astype(f32)).astype(bf16)

            loop(H, 16, add)
            dst = self.stage.at[p]
            for k, dev in plane_peers:
                self.out.append(push(g.at[ds(c * H + k * R, R, 16)], dst, dev, self.rl))
            keep_local(g.at[ds(c * H + p * R, R, 16)], dst, self.rl)

        def z_send(self):
            arrived(self.stage, self.rl)
            self.zsum.send()

        def z_forward(self):
            self.zsum.forward()

        def end(self):
            self.zsum.end()
            settle(*self.out)

            def add(o):
                s = pl.ds(o, 16)
                self.result[s] = self.zsum.total(self.stage[zh, s].astype(f32), [self.slots[k, s] for k in range(4)])

            loop(self.R, 16, add)

    class Carry:
        def __init__(self, buf, later):
            self.buf, self.later = buf, later
            self.sems = new(places)
            self.out = []

        def send(self):
            own = self.buf.at[pos]
            order = range(places) if self.later else reversed(range(places))
            for at in order:
                pred = (pos < at) if self.later else (pos > at)
                self.out.append(push(own, own, place(at), self.sems + pos, pred))

        def fold(self, into):
            into[...] = jnp.zeros_like(into)
            order = range(places) if self.later else reversed(range(places))
            for at in order:
                pred = (pos > at) if self.later else (pos < at)

                def take(at=at):
                    arrived(self.buf.at[at], self.sems + at)
                    part = self.buf[at]
                    into[0:PLANE] = part[0:PLANE] * into[0:PLANE] + part[PLANE : 2 * PLANE]

                pl.when(pred)(take)
            settle(*self.out)

    barrier = pltpu.get_barrier_semaphore()
    for _, dev in plane_peers:
        pl.semaphore_signal(barrier, 1, device_id=dev, device_id_type=MESH)
    for at in range(places):

        @pl.when(pos != at)
        def _(at=at):
            pl.semaphore_signal(barrier, 1, device_id=place(at), device_id_type=MESH)

    pl.semaphore_wait(barrier, len(plane_peers) + places - 1)

    in_branch = Columns((r.input_weight, r.branch_weight), r.w_ib, RD, CW)
    dec_inj = Columns((r.decay_weight, r.inject_weight), r.w_di, RW, CW)
    gate_up = Columns((r.mlp_gate, r.mlp_up), r.w_gu, RD, CF)
    output = Rows(r.output_weight, r.w_o, r.st_o, RW)
    down = Rows(r.mlp_down, r.w_dn, r.st_dn, RF)
    ag_one, ag_conv, ag_two = Gather(r.n_one), Gather(r.conv), Gather(r.n_two)
    ag_cot, ag_out = Gather(r.cot_all), Gather(r.d_out)

    in_branch.spread()
    output.z_send()

    def norm_one(o):
        s = pl.ds(o, 16)
        v = r.tokens[s].astype(f32)
        r.n_one[p, s] = (v * inverse_rms(v) * r.gains[0:1]).astype(bf16)

    loop(T, 16, norm_one)
    ag_one.start()
    dec_inj.spread()
    gate_up.spread()
    r.cot_all[p] = r.cotangent[...]
    in_branch.z_send()
    ag_one.mid()
    ag_cot.start()
    dec_inj.z_send()
    gate_up.z_send()
    down.z_send()
    output.z_forward()
    in_branch.z_forward()
    in_branch.z_wait()
    ag_one.end()
    in_branch.end()

    n_one = r.n_one[...].reshape(M, D)
    r.pair[:, 0 : 2 * CW] = dot(n_one, r.w_ib[...].reshape(D, 2 * CW))
    for k in range(PLANE):
        r.u[k, 8 : 8 + T] = r.pair[k * T : (k + 1) * T, 0:CW].astype(bf16).astype(f32)
    halo_f = new()
    after, before = flat_z + c, flat_z - (1 - c)
    to_next = {"zh": after // NL, "zl": after % NL, "c": 1 - c}
    to_prev = {"zh": before // NL, "zl": before % NL, "c": 1 - c}
    sent_f = push(r.u.at[:, pl.ds(T, 8)], r.u.at[:, pl.ds(0, 8)], to_next, halo_f, pos < places - 1)

    def gates_one(o):
        s = pl.ds(o, 16)
        r.gated[s], r.slope[s] = gelu_parts(r.pair[s, CW : 2 * CW])

    loop(M, 16, gates_one)

    @pl.when(pos == 0)
    def _():
        r.u[:, 0:8] = jnp.zeros((PLANE, 8, CW), f32)

    arrived(r.u.at[:, pl.ds(0, 8)], halo_f, pos > 0)
    settle(sent_f)

    for k in range(PLANE):

        def convolve(o, k=k):
            ext = r.u[k, pl.ds(o, 24)]
            rows = ds(k * T + o, 16, 16)
            keep = r.masks[rows]
            total = r.chan[4:5] + r.chan[0:1] * ext[8:24]
            for j in range(1, 4):
                total = total + jnp.where(keep[:, j : j + 1] > 0.5, r.chan[j : j + 1] * ext[8 - j : 24 - j], 0.0)
            r.conv[p, rows] = total.astype(bf16)

        loop(T, 16, convolve)
    ag_conv.start()
    ag_cot.mid()
    dec_inj.z_forward()
    ag_conv.mid()
    output.z_wait()
    dec_inj.z_wait()
    output.plane_wait()
    dec_inj.end()

    def pre(q):
        return dot(r.conv[q], r.w_di[q].reshape(W // RING, 2 * CW))

    r.pair[:, 0 : 2 * CW] = pre(p)
    for q, wait in ((px, ag_conv.wait_x), (py, ag_conv.wait_y), (pd, ag_conv.wait_d)):
        wait()
        r.pair[:, 0 : 2 * CW] += pre(q)
    settle(*ag_conv.out)

    def decay_terms(s, rg):
        log_a = -rate_scale * rg * r.chan[7:8]
        gap = minus_expm1(2.0 * log_a)
        first = r.masks[s][:, 0:1] > 0.5
        return log_a, gap, jnp.where(first, 1.0, jnp.sqrt(jnp.maximum(gap, floor_gap))), first

    def gates_two(o):
        s = pl.ds(o, 16)
        rg = jax.nn.sigmoid(r.pair[s, 0:CW] + r.chan[5:6])
        ig = jax.nn.sigmoid(r.pair[s, CW : 2 * CW] + r.chan[6:7])
        log_a, _, mult, first = decay_terms(s, rg)
        r.rgate[s], r.igate[s] = rg, ig
        r.decay[s] = jnp.where(first, 0.0, jnp.exp(log_a))
        r.work[s] = mult * ig * r.conv[p, s].astype(f32)

    loop(M, 16, gates_two)
    row = lax.broadcasted_iota(jnp.int32, (8, CW), 0)

    def scan_forward(j, carry):
        out = []
        for k in range(PLANE):
            s = ds(k * T + j * 8, 8, 8)
            a, b = r.decay[s], r.work[s]
            for n in (1, 2, 4):
                a_b = jnp.where(row >= n, pltpu.roll(a, n, 0), 1.0)
                b_b = jnp.where(row >= n, pltpu.roll(b, n, 0), 0.0)
                a, b = a * a_b, a * b_b + b
            total, prod = b + a * carry[2 * k], a * carry[2 * k + 1]
            r.state[k, ds(8 + j * 8, 8, 8)] = total
            r.cum[s] = prod
            out += [total[7:8], prod[7:8]]
        return tuple(out)

    zero, one = jnp.zeros((1, CW), f32), jnp.ones((1, CW), f32)
    ends = lax.fori_loop(0, T // 8, scan_forward, (zero, one) * PLANE)
    carry_f = Carry(r.carry_f, True)
    for k in range(PLANE):
        r.carry_f[pos, k : k + 1] = ends[2 * k + 1]
        r.carry_f[pos, PLANE + k : PLANE + k + 1] = ends[2 * k]
        r.ends[k : k + 1] = ends[2 * k + 1]
    carry_f.send()
    output.end()
    carry_f.fold(r.into)

    for k in range(PLANE):
        into = r.into[k : k + 1]
        r.state[k, 0:8] = jnp.broadcast_to(into, (8, CW))

        def mix(o, k=k, into=into):
            s, t = ds(k * T + o, 16, 16), ds(8 + o, 16, 8)
            state = r.state[k, t] + r.cum[s] * into
            r.state[k, t] = state
            r.mixed[s] = (state * r.gated[s]).astype(bf16)

        loop(T, 16, mix)

    step = 256

    def out_part(o):
        q = pl.ds(o, step)
        r.part[:, :, q] = dot(r.mixed[...], r.w_o[:, q]).astype(bf16).reshape(PLANE, T, step)

    loop(D, step, out_part)
    rs_one = Scatter(r.part, r.got_one)
    rs_one.start()
    ag_cot.end()
    gate_up.z_forward()
    rs_one.mid()
    rs_one.end()

    def norm_two(o, summed):
        s = pl.ds(o, 16)
        v = r.tokens[s].astype(f32) + summed
        r.x_one[s] = v
        r.n_two[p, s] = (v * inverse_rms(v) * r.gains[1:2]).astype(bf16)

    rs_one.each(16, norm_two)
    ag_two.start()
    gate_up.z_wait()
    down.z_forward()
    ag_two.mid()
    gate_up.end()
    ag_two.end()

    def mlp_in(o):
        q = pl.ds(o, step)
        r.pair[:, q] = dot(r.n_two[...].reshape(M, D), r.w_gu[:, :, :, q].reshape(D, step))

    loop(2 * CF, step, mlp_in)
    down.z_wait()

    def gates_mlp(o):
        s = pl.ds(o, 16)
        value, slope = gelu_parts(r.pair[s, 0:CF])
        up = r.pair[s, CF : 2 * CF]
        r.hidden[s] = (value * up).astype(bf16)
        r.pair[s, 0:CF] = slope * up
        r.pair[s, CF : 2 * CF] = value

    loop(M, 16, gates_mlp)
    down.plane_wait()
    down.end()

    for k in range(CF // step):
        q = pl.ds(k * step, step)
        back = dot_nt(r.cot_all[...].reshape(M, D), r.w_dn[q])
        r.d_pair[:, k * step : (k + 1) * step] = (back * r.pair[:, k * step : (k + 1) * step]).astype(bf16)
        r.d_pair[:, CF + k * step : CF + (k + 1) * step] = (
            back * r.pair[:, CF + k * step : CF + (k + 1) * step]
        ).astype(bf16)
    chunk = PLANE * RD * 2

    def d_two_part(z, _):
        q = ds(z * chunk, chunk, chunk)
        r.part[:, :, q] = (
            dot_nt(r.d_pair[...], r.w_gu[z].reshape(chunk, 2 * CF)).astype(bf16).reshape(PLANE, T, chunk)
        )
        return 0

    lax.fori_loop(0, RING, d_two_part, 0)
    rs_two = Scatter(r.part, r.got_two)
    rs_two.start()

    def act_part(o):
        q = pl.ds(o, step)
        r.part_act[:, :, q] = dot(r.hidden[...], r.w_dn[:, q]).astype(bf16).reshape(PLANE, T, step)

    loop(D, step, act_part)
    rs_act = Scatter(r.part_act, r.got_act)
    rs_act.start()

    def grad_down(o):
        q = pl.ds(o, step)
        r.w_dn[q] = dot_tn(r.hidden[:, q], r.cot_all[...].reshape(M, D)).astype(bf16)

    loop(CF, step, grad_down)
    g_down = RowsGrad(r.w_dn, r.h_dn, r.sg_dn, r.z_dn, RF, r.grad_mlp_down)
    g_down.core_send()
    rs_two.mid()
    g_down.plane_send()

    def grad_gate_up(z, _):
        q = ds(z * chunk, chunk, chunk)
        value = dot_tn(r.n_two[:, :, q].reshape(M, chunk), r.d_pair[...])
        r.w_gu[z] = value.astype(bf16).reshape(2, chunk // 2, 2 * CF)
        return 0

    lax.fori_loop(0, RING, grad_gate_up, 0)
    g_gu = ColumnsGrad(
        r.w_gu, r.h_gu, r.z_gu, r.l_gu, RD, 0, 2 * CF, ((0, CF, r.grad_mlp_gate), (CF, CF, r.grad_mlp_up))
    )
    g_gu.core_send()
    rs_two.end()
    r.ggain[...] = jnp.zeros_like(r.ggain)
    r.gchan[...] = jnp.zeros_like(r.gchan)

    def norm_two_back(o, d_two):
        s = pl.ds(o, 16)
        v = r.x_one[s]
        rs = inverse_rms(v)
        z = v * rs
        dz = d_two * r.gains[1:2]
        r.ggain[1:2] += jnp.sum(d_two * z, axis=0, keepdims=True)
        d_one = r.cotangent[s].astype(f32) + rs * (dz - z * jnp.mean(dz * z, axis=-1, keepdims=True))
        r.d_one[s] = d_one
        r.d_out[p, s] = d_one.astype(bf16)

    rs_two.each(16, norm_two_back)
    ag_out.start()
    g_down.z_send()
    rs_act.mid()
    g_gu.z_send()
    ag_out.mid()
    g_down.z_forward()
    rs_act.end()

    def finish_act(o, summed):
        s = pl.ds(o, 16)
        r.activations[s] = (r.x_one[s] + summed).astype(bf16)

    rs_act.each(16, finish_act)
    ag_out.end()

    r.work[...] = dot_nt(r.d_out[...].reshape(M, D), r.w_o[...])
    for k in range(PLANE):

        def split(o, k=k):
            s = ds(k * T + o, 16, 16)
            d_mixed = r.work[s]
            r.d_gu[s, CW : 2 * CW] = (d_mixed * r.state[k, ds(8 + o, 16, 8)] * r.slope[s]).astype(bf16)
            r.work[s] = d_mixed * r.gated[s]

        loop(T, 16, split)

    def scan_backward(i, carry):
        j = T // 8 - 1 - i
        out = []
        for k in range(PLANE):
            s = ds(k * T + j * 8, 8, 8)
            decay, b = r.decay[s], r.work[s]
            a = jnp.where(row < 7, pltpu.roll(decay, 7, 0), carry[3 * k + 2])
            for n in (1, 2, 4):
                a_b = jnp.where(row < 8 - n, pltpu.roll(a, 8 - n, 0), 1.0)
                b_b = jnp.where(row < 8 - n, pltpu.roll(b, 8 - n, 0), 0.0)
                a, b = a * a_b, a * b_b + b
            total, prod = b + a * carry[3 * k], a * carry[3 * k + 1]
            r.work[s], r.cum[s] = total, prod
            out += [total[0:1], prod[0:1], decay[0:1]]
        return tuple(out)

    heads = lax.fori_loop(0, T // 8, scan_backward, (zero, one, one) * PLANE)
    carry_b = Carry(r.carry_b, False)
    for k in range(PLANE):
        r.carry_b[pos, k : k + 1] = r.ends[k : k + 1]
        r.carry_b[pos, PLANE + k : PLANE + k + 1] = heads[3 * k] * heads[3 * k + 2]
    carry_b.send()

    def grad_out(o):
        q = pl.ds(o, 128)
        r.w_o[q] = dot_tn(r.mixed[:, q], r.d_out[...].reshape(M, D)).astype(bf16)

    loop(CW, 128, grad_out)
    g_out = RowsGrad(r.w_o, r.h_o, r.sg_o, r.z_o, RW, r.grad_output_weight)
    g_out.core_send()
    carry_b.fold(r.into)

    for k in range(PLANE):
        into = r.into[k : k + 1]

        def back(o, k=k, into=into):
            s = ds(k * T + o, 16, 16)
            adjoint = r.work[s] + r.cum[s] * into
            previous = r.state[k, pl.ds(o, 24)][7:23]
            rg, ig, decay, conv = r.rgate[s], r.igate[s], r.decay[s], r.conv[p, s].astype(f32)
            _, gap, mult, first = decay_terms(s, rg)
            d_mult = jnp.where(first, 0.0, adjoint * ig * conv)
            d_log = adjoint * previous * decay - jnp.where(
                gap > floor_gap, (1.0 - gap) * d_mult / mult, 0.0
            )
            d_decay = (-rate_scale * r.chan[7:8] * d_log * rg * (1.0 - rg)).astype(bf16)
            d_inject = (adjoint * mult * conv * ig * (1.0 - ig)).astype(bf16)
            r.d_pre[s, 0:CW] = d_decay
            r.d_pre[s, CW : 2 * CW] = d_inject
            r.gchan[5:6] += jnp.sum(d_decay.astype(f32), axis=0, keepdims=True)
            r.gchan[6:7] += jnp.sum(d_inject.astype(f32), axis=0, keepdims=True)
            r.d_conv[k, pl.ds(o, 16)] = adjoint * mult * ig

        loop(T, 16, back)

    def conv_part(q, _):
        r.part_conv[q] = dot_nt(r.d_pre[...], r.w_di[q].reshape(W // RING, 2 * CW)).astype(bf16)
        return 0

    lax.fori_loop(0, RING, conv_part, 0)
    rs_conv = Scatter(r.part_conv, r.got_conv)
    rs_conv.start()
    g_gu.z_forward()
    g_out.plane_send()

    def grad_dec_inj(q, _):
        value = dot_tn(r.conv[q], r.d_pre[...])
        r.w_di[q] = value.astype(bf16).reshape(2, W // SHARES * PLANE, 2 * CW)
        return 0

    lax.fori_loop(0, RING, grad_dec_inj, 0)
    g_di = ColumnsGrad(
        r.w_di, r.h_di, r.z_di, r.l_di, RW, 0, 2 * CW, ((0, CW, r.grad_decay_weight), (CW, CW, r.grad_inject_weight))
    )
    g_di.core_send()
    rs_conv.mid()

    def d_branch_part(z, _):
        q = ds(z * chunk, chunk, chunk)
        r.part[:, :, q] = (
            dot_nt(r.d_gu[:, CW : 2 * CW], r.w_ib[z, :, :, CW : 2 * CW].reshape(chunk, CW))
            .astype(bf16)
            .reshape(PLANE, T, chunk)
        )
        value = dot_tn(r.n_one[:, :, q].reshape(M, chunk), r.d_gu[:, CW : 2 * CW])
        r.w_ib[z, :, :, CW : 2 * CW] = value.astype(bf16).reshape(2, chunk // 2, CW)
        return 0

    lax.fori_loop(0, RING, d_branch_part, 0)
    g_branch = ColumnsGrad(r.w_ib, r.h_ib, r.z_ib, r.l_ib, RD, CW, CW, ((CW, CW, r.grad_branch_weight),))
    g_branch.core_send()
    g_out.z_send()
    g_di.z_send()
    g_branch.z_send()
    rs_conv.end()

    for half in (0, 1):
        rows = M // 2

        def add_conv(o, half=half):
            for k in (2 * half, 2 * half + 1):
                at = (k - 2 * half) * T + o
                r.d_conv[k, pl.ds(o, 16)] += rs_conv.total(half, pl.multiple_of(at, 16), 16)

        loop(T, 16, add_conv)
    halo_b = new()
    sent_b = push(r.d_conv.at[:, pl.ds(0, 8)], r.d_conv.at[:, pl.ds(T, 8)], to_prev, halo_b, pos > 0)
    for k in range(PLANE):

        def taps_back(o, k=k):
            ext = r.u[k, pl.ds(o, 24)]
            keep = r.masks[ds(k * T + o, 16, 16)]
            dc = r.d_conv[k, pl.ds(o, 16)]
            r.gchan[4:5] += jnp.sum(dc, axis=0, keepdims=True)
            r.gchan[0:1] += jnp.sum(dc * ext[8:24], axis=0, keepdims=True)
            for j in range(1, 4):
                term = jnp.where(keep[:, j : j + 1] > 0.5, dc * ext[8 - j : 24 - j], 0.0)
                r.gchan[j : j + 1] += jnp.sum(term, axis=0, keepdims=True)

        loop(T, 16, taps_back)

    @pl.when(pos == places - 1)
    def _():
        r.d_conv[:, T : T + 8] = jnp.zeros((PLANE, 8, CW), f32)

    arrived(r.d_conv.at[:, pl.ds(T, 8)], halo_b, pos < places - 1)
    settle(sent_b)
    for k in range(PLANE):

        def conv_back(o, k=k):
            ext = r.d_conv[k, pl.ds(o, 24)]
            rows = ds(k * T + o, 16, 16)
            keep = r.masks[rows]
            total = r.chan[0:1] * ext[0:16]
            for j in range(1, 4):
                total = total + jnp.where(keep[:, 3 + j : 4 + j] > 0.5, r.chan[j : j + 1] * ext[j : 16 + j], 0.0)
            r.d_gu[rows, 0:CW] = total.astype(bf16)

        loop(T, 16, conv_back)

    def d_input_part(z, _):
        q = ds(z * chunk, chunk, chunk)
        value = dot_nt(r.d_gu[:, 0:CW], r.w_ib[z, :, :, 0:CW].reshape(chunk, CW)).reshape(PLANE, T, chunk)
        r.part[:, :, q] = (r.part[:, :, q].astype(f32) + value).astype(bf16)
        return 0

    lax.fori_loop(0, RING, d_input_part, 0)
    rs_three = Scatter(r.part, r.got_three)
    rs_three.start()

    def grad_input(z, _):
        q = ds(z * chunk, chunk, chunk)
        value = dot_tn(r.n_one[:, :, q].reshape(M, chunk), r.d_gu[:, 0:CW])
        r.w_ib[z, :, :, 0:CW] = value.astype(bf16).reshape(2, chunk // 2, CW)
        return 0

    lax.fori_loop(0, RING, grad_input, 0)
    g_input = ColumnsGrad(r.w_ib, r.h_ib, r.z_ib, r.l_ib, RD, 0, CW, ((0, CW, r.grad_input_weight),))
    g_input.core_send()
    rs_three.mid()
    g_input.z_send()
    g_down.end()
    g_out.z_forward()
    g_di.z_forward()
    g_branch.z_forward()
    g_gu.plane_send()
    g_input.z_forward()
    rs_three.end()

    def norm_one_back(o, d_n):
        s = pl.ds(o, 16)
        v = r.tokens[s].astype(f32)
        rs = inverse_rms(v)
        z = v * rs
        dz = d_n * r.gains[0:1]
        r.ggain[0:1] += jnp.sum(d_n * z, axis=0, keepdims=True)
        r.d_tokens[s] = r.d_one[s] + rs * (dz - z * jnp.mean(dz * z, axis=-1, keepdims=True))

    rs_three.each(16, norm_one_back)
    g_out.end()
    g_di.plane_send()
    g_branch.plane_send()
    g_gu.end()
    g_input.plane_send()
    g_di.end()
    g_branch.end()
    g_input.end()
    assert not sent


WEIGHTS = (
    "branch_weight",
    "input_weight",
    "decay_weight",
    "inject_weight",
    "output_weight",
    "mlp_gate",
    "mlp_up",
    "mlp_down",
)


def run_layer(NL, tokens, cotangent, gains, chan, masks, weights):
    T, D = tokens.shape
    W, F = weights["branch_weight"].shape[1], weights["mlp_gate"].shape[1]
    CW, CF = W // PLANE, F // PLANE
    RD, RW, RF = D // SHARES, W // SHARES, F // SHARES
    M, places = PLANE * T, RING * NL * 2
    vmem, hbm = pl.BlockSpec(memory_space=pltpu.VMEM), pl.BlockSpec(memory_space=pl.ANY)
    ins = ["tokens", "cotangent", "gains", "chan", "masks", *WEIGHTS]
    outs = {
        "activations": ((T, D), bf16),
        "d_tokens": ((T, D), f32),
        **{"grad_" + name: (weights[name].shape, f32) for name in WEIGHTS},
        "ggain": ((8, D), f32),
        "gchan": ((8, CW), f32),
    }
    outs = {name if name[:5] != "grad_" else name: spec for name, spec in outs.items()}
    scratch = {
        "w_ib": ((RING, 2, PLANE * RD, 2 * CW), bf16),
        "w_di": ((RING, 2, PLANE * RW, 2 * CW), bf16),
        "w_gu": ((RING, 2, PLANE * RD, 2 * CF), bf16),
        "w_o": ((CW, D), bf16),
        "w_dn": ((CF, D), bf16),
        "st_o": ((RING, RW, D), bf16),
        "st_dn": ((RING, RF, D), bf16),
        "h_ib": ((RING, PLANE * RD, 2 * CW), bf16),
        "h_di": ((RING, PLANE * RW, 2 * CW), bf16),
        "h_gu": ((RING, PLANE * RD, 2 * CF), bf16),
        "h_o": ((CW // 2, D), bf16),
        "h_dn": ((CF // 2, D), bf16),
        "z_ib": ((4, PLANE * RD, 2 * CW), bf16),
        "z_di": ((4, PLANE * RW, 2 * CW), bf16),
        "z_gu": ((4, PLANE * RD, 2 * CF), bf16),
        "z_o": ((4, RW, D), bf16),
        "z_dn": ((4, RF, D), bf16),
        "l_ib": ((PLANE, RD, 2 * CW), bf16),
        "l_di": ((PLANE, RW, 2 * CW), bf16),
        "l_gu": ((PLANE, RD, 2 * CF), bf16),
        "sg_o": ((RING, RW, D), bf16),
        "sg_dn": ((RING, RF, D), bf16),
        "n_one": ((PLANE, T, D), bf16),
        "n_two": ((PLANE, T, D), bf16),
        "cot_all": ((PLANE, T, D), bf16),
        "d_out": ((PLANE, T, D), bf16),
        "conv": ((PLANE, M, CW), bf16),
        "part": ((PLANE, T, D), bf16),
        "part_act": ((PLANE, T, D), bf16),
        "part_conv": ((PLANE, M, CW), bf16),
        "got_one": ((6, T // 2, D), bf16),
        "got_two": ((6, T // 2, D), bf16),
        "got_three": ((6, T // 2, D), bf16),
        "got_act": ((6, T // 2, D), bf16),
        "got_conv": ((6, M // 2, CW), bf16),
        "mixed": ((M, CW), bf16),
        "hidden": ((M, CF), bf16),
        "d_pair": ((M, 2 * CF), bf16),
        "d_gu": ((M, 2 * CW), bf16),
        "d_pre": ((M, 2 * CW), bf16),
        "pair": ((M, 2 * CF), f32),
        "u": ((PLANE, T + 8, CW), f32),
        "state": ((PLANE, T + 8, CW), f32),
        "d_conv": ((PLANE, T + 8, CW), f32),
        **{name: ((M, CW), f32) for name in ("gated", "slope", "rgate", "igate", "decay", "work", "cum")},
        "x_one": ((T, D), f32),
        "d_one": ((T, D), f32),
        "carry_f": ((places, 2 * PLANE, CW), f32),
        "carry_b": ((places, 2 * PLANE, CW), f32),
        "into": ((8, CW), f32),
        "ends": ((8, CW), f32),
    }
    dims = SimpleNamespace(
        T=T, D=D, W=W, F=F, CW=CW, CF=CF, RD=RD, RW=RW, RF=RF, NL=NL, names=[*ins, *outs, *scratch, "ss", "rs"]
    )
    flops = 3 * 2 * M * (D * 2 * CW + W * 2 * CW + CW * D + 3 * D * CF)
    results = pl.pallas_call(
        partial(layer, dims),
        out_shape=[jax.ShapeDtypeStruct(shape, kind) for shape, kind in outs.values()],
        in_specs=[vmem] * 5 + [hbm] * len(WEIGHTS),
        out_specs=[vmem] * len(outs),
        scratch_shapes=[pltpu.VMEM(shape, kind) for shape, kind in scratch.values()]
        + [pltpu.SemaphoreType.DMA((SEMS,)), pltpu.SemaphoreType.DMA((SEMS,))],
        compiler_params=pltpu.CompilerParams(
            collective_id=0, has_side_effects=True, vmem_limit_bytes=62 * 2**20
        ),
        cost_estimate=pl.CostEstimate(flops=flops, bytes_accessed=8 * 2**20, transcendentals=M * CW * 16),
        name="griffin_layer",
    )(tokens, cotangent, gains, chan, masks, *[weights[name] for name in WEIGHTS])
    return dict(zip(outs, results, strict=True))


def local(
    sizes,
    tokens,
    cotangent,
    doc_lengths,
    decay_exponent,
    branch_weight,
    input_weight,
    decay_weight,
    inject_weight,
    output_weight,
    mlp_gate,
    mlp_up,
    mlp_down,
    first_gain,
    second_gain,
    conv_taps,
    conv_bias,
    decay_bias,
    inject_bias,
):
    devices = math.prod(sizes.values())
    width = branch_weight.shape[1]
    own_d, own_w = first_gain.shape[0], conv_bias.shape[0]
    NL = sizes["zl"]
    at = {name: lax.axis_index(name) for name in AXES}
    T = tokens.shape[1]

    small = jnp.concatenate(
        [
            jnp.stack([first_gain, second_gain]).reshape(-1),
            jnp.concatenate([conv_taps.T, jnp.stack([conv_bias, decay_bias, inject_bias])]).reshape(-1),
        ]
    ).astype(f32)
    small = jnp.concatenate([small, doc_lengths[0].astype(f32)])
    small = lax.all_gather(small, AXES)
    gains = small[:, : 2 * own_d].reshape(devices, 2, own_d).transpose(1, 0, 2).reshape(2, -1)
    chan = small[:, 2 * own_d : 2 * own_d + 7 * own_w].reshape(devices, 7, own_w).transpose(1, 0, 2).reshape(7, -1)
    scale = jnp.exp2(-decay_exponent.astype(f32))
    chan = jnp.concatenate([chan, scale[None]])
    mine = at["yl"] * 2 + at["xl"]
    chan = lax.dynamic_slice_in_dim(chan, mine * (width // PLANE), width // PLANE, 1)
    lengths = small[:, 2 * own_d + 7 * own_w :].astype(jnp.int32)
    across = sizes["xh"] * 2
    rows = (at["yh"] * 2 + jnp.arange(PLANE) // 2) * across + at["xh"] * 2 + jnp.arange(PLANE) % 2
    lengths = lengths[rows]

    ends = jnp.cumsum(lengths, axis=1)
    starts = ends - lengths
    index = (at["zh"] * NL + at["zl"]) * 2 + at["c"]
    count = T * RING * NL * 2
    where = index * T - 3 + jnp.arange(T + 6, dtype=jnp.int32)
    seg = jnp.sum((ends[:, None, :] <= where[None, :, None]).astype(jnp.int32), axis=2)
    seg = jnp.where((where < 0) | (where >= count), -1, seg)
    here = seg[:, 3 : 3 + T]
    first = jnp.any(starts[:, None, :] == where[None, 3 : 3 + T, None], axis=2)
    masks = [first]
    masks += [seg[:, 3 - k : 3 - k + T] == here for k in (1, 2, 3)]
    masks += [seg[:, 3 + k : 3 + k + T] == here for k in (1, 2, 3)]
    masks += [first]
    masks = jnp.stack(masks, axis=-1).astype(f32).reshape(PLANE * T, 8)

    weights = dict(
        zip(
            WEIGHTS,
            (branch_weight, input_weight, decay_weight, inject_weight, output_weight, mlp_gate, mlp_up, mlp_down),
            strict=True,
        )
    )
    groups = devices // SHARES
    if groups > 1:
        share = (at["zh"] * 2 + at["c"]) * PLANE + mine
        for name, value in weights.items():
            whole = lax.all_gather(value, AXES, axis=0, tiled=True)
            weights[name] = lax.dynamic_slice_in_dim(whole, share * (whole.shape[0] // SHARES), whole.shape[0] // SHARES)
    pad = jnp.zeros((6, gains.shape[1]), f32)
    got = run_layer(NL, tokens[0], cotangent[0], jnp.concatenate([gains, pad]), chan, masks, weights)
    grads = {name: got["grad_" + name] for name in WEIGHTS}
    if groups > 1:
        for name, value in grads.items():
            whole = jnp.zeros((value.shape[0] * SHARES, value.shape[1]), bf16)
            whole = lax.dynamic_update_slice_in_dim(whole, value.astype(bf16), share * value.shape[0], 0)
            grads[name] = lax.psum_scatter(whole, AXES, scatter_dimension=0, tiled=True).astype(f32)

    gain_grads = got["ggain"][:2].reshape(2, devices, own_d).transpose(1, 0, 2).reshape(devices, -1)
    chan_grads = jnp.zeros((7, width), f32)
    chan_grads = lax.dynamic_update_slice_in_dim(chan_grads, got["gchan"][:7], mine * (width // PLANE), 1)
    chan_grads = chan_grads.reshape(7, devices, own_w).transpose(1, 0, 2).reshape(devices, -1)
    sums = lax.psum_scatter(jnp.concatenate([gain_grads, chan_grads], 1), AXES, scatter_dimension=0, tiled=True)[0]
    gain_sum = sums[: 2 * own_d].reshape(2, own_d)
    chan_sum = sums[2 * own_d :].reshape(7, own_w)
    return (
        got["activations"][None],
        got["d_tokens"][None],
        *[grads[name] for name in WEIGHTS],
        gain_sum[0],
        gain_sum[1],
        chan_sum[:4].T,
        chan_sum[4],
        chan_sum[5],
        chan_sum[6],
    )


def solution(mesh):
    seq, dp = mesh.shape["seq"], mesh.shape["dp"]
    across = 1 << ((dp.bit_length() - 1) // 2)
    sizes = dict(zip(AXES, (RING, seq // (2 * RING), 2, dp // across // 2, 2, across // 2, 2), strict=True))
    split = Mesh(mesh.devices.reshape(tuple(sizes.values())), AXES)
    along_seq, along_dp = AXES[:3], AXES[3:]
    rows = P(along_dp, along_seq, None)
    in_specs = (rows, rows, P(along_dp, None), P(), *[P(AXES, None)] * 8, P(AXES), P(AXES), P(AXES, None), *[P(AXES)] * 3)
    out_specs = (rows, rows, *[P(AXES, None)] * 8, P(AXES), P(AXES), P(AXES, None), *[P(AXES)] * 3)
    return jax.shard_map(partial(local, sizes), mesh=split, in_specs=in_specs, out_specs=out_specs, check_vma=False)
```

time: 1420 us -> 407 us (0.29); the launches traced: 1400 us -> 406 us
  waiting for transfers between devices: 759 us -> 0 us
  Pallas kernels: 0 us -> 305 us
  local copies, waits for them, and re-layouts: 242 us -> 19.1 us
  blocking collectives: 187 us -> 79.7 us
  matrix products: 94.7 us -> 0 us
  other arithmetic: 93 us -> 1.62 us
  between operations: 18.8 us -> 0.93 us
    reduce_scatter x16 -> x0, waiting for transfers between devices: 522 us -> none  [the longest x1 70.3 us: local(): lax.psum_scatter(grad_gate.astype(jnp.bfloat16), 'seq', scatter_dimension...]
    pallas_call x0 -> x1, Pallas kernels: none -> 305 us  [run_layer(): pl.pallas_call(partial(layer, dims), out_shape=[jax.ShapeDtypeStruct(shap...]
    all_gather x8 -> x0, waiting for transfers between devices: 229 us -> none  [the longest x1 66.1 us: local(): lax.all_gather(mlp_down, ('seq', 'dp'), axis=0, tiled=True)]
    slice x97 -> x6, local copies, waits for them, and re-layouts: 162 us -> 1.74 us  [the longest x1 0.83 us: local(): got['ggain'][:2].reshape(2, devices, own_d).transpose(1, 0, 2)]
    all_gather x4 -> x0, blocking collectives: 108 us -> none  [the longest x1 66.2 us: local(): lax.all_gather(conv_taps, ('seq', 'dp'), axis=0, tiled=True)]
    dot_general x24 -> x0, matrix products: 94.7 us -> none  [the longest x8 32.6 us: matmul(): return jnp.dot(left, right, preferred_element_type=jnp.float32)]
    pad x48 -> x0, local copies, waits for them, and re-layouts: 38.7 us -> none  [the longest x24 25.9 us: local(): lax.associative_scan(combine, (next_decay, d_state), reverse=True, axis=0)]
    add x38 -> x1, other arithmetic: 29.6 us -> 0.01 us  [local(): where = index * T - 3 + jnp.arange(T + 6, dtype=jnp.int32)]
  transfers between devices with their start and end apart: 27 -> 0, of which waited for: 21 -> 0; matrix products, arithmetic and copies ran while one was open for 25% -> 0% of each run, Pallas kernels for 0% -> 0%
where the time goes in v1:
time: 407 us; the launch traced here: 406 us
  Pallas kernels  305 us (75%)
  blocking collectives  79.7 us (20%)
  local copies, waits for them, and re-layouts  19.1 us (5%)
    pallas_call x1, Pallas kernels, run_layer(): pl.pallas_call(partial(layer, dims), out_shape=[jax.ShapeDtypeStruct(shap...  305 us
    unnamed x2, blocking collectives  79.7 us
    unnamed x50, local copies, waits for them, and re-layouts  12.9 us

profile of v1, /device:TPU:0, one launch (start us, length us, event | category | flops | bytes accessed | tf_op | source)
XLA Modules:
  0.0 406.2 jit_solution(18255412360153643737)
XLA Ops:
  0.7 0.6 copy-done.14
  1.4 0.1 reshape.174
  1.5 0.7 copy-done.16
  2.2 0.1 reshape.173
  2.3 0.6 copy-done.18
  2.9 0.2 maximum_dynamic-update-slice_fusion
  3.1 42.5 %all-reduce.1 = f32[12928]{0:T(1024)S(1)} all-reduce(f32[12928]{0:T(1024)S(1)} %maximum_dynamic-update-slice_fusion), channel_id=2, replica_groups=mesh['zh'=4,'zl'=1,'c'=2,'yh'=1,'yl'=2,'xh'=1,'xl'=2] {'zh','zl','c','yh..., use_global_device_ids=true, to_apply=%add.1 | all-reduce | flops 12928 | bytes 103424
  45.6 0.1 reshape.191
  45.8 0.6 gather_fusion
  46.4 0.2 reduce_window_sum.11
  46.6 0.1 convert_reduce_fusion
  46.9 0.1 compare_reduce_fusion
  47.1 0.8 copy.61.refs_4_
  48.0 0.1 reshape.177
  48.1 0.1 reshape.178
  48.2 0.6 copy-done.11
  48.8 0.7 fusion.refs_3_
  49.5 0.1 reshape.175
  49.7 0.6 concatenate.22.refs_2_
  50.3 304.9 %griffin_layer.1 = (bf16[128,1024]{1,0:T(8,128)(2,1)}, f32[128,1024]{1,0:T(8,128)}, f32[32,1536]{1,0:T(8,128)}, f32[32,1536]{1,0:T(8,128)}, f32[48,1536]{1,0:T(8...) custom-call(bf16[128,1024]{1,0:T(8,128)(2,1)} %bitcast.87, ...), custom_call_target="tpu_custom_call" | custom-call | flops 14495514624 | bytes 8388608 | tf_op jit(solution)/shard_map/griffin_layer/pallas_call | solution.py:1072
  355.2 0.7 copy-done.10
  355.9 0.1 reshape.181
  356.1 0.1 reshape.182
  356.2 0.8 slice.86
  357.1 0.1 reshape.179
  357.2 0.1 reshape.180
  357.3 37.3 %all-reduce.2 = f32[32,400]{1,0:T(8,128)S(1)} all-reduce(f32[32,400]{1,0:T(8,128)S(1)} %pad_maximum_fusion), channel_id=3, replica_groups=mesh['zh'=4,'zl'=1,'c'=2,'yh'=1,'yl'=2,'xh'=1,'xl'=2] {'zh','zl','c','yh..., use_global_device_ids=true, to_apply=%region_3.4.clone | all-reduce | flops 12800 | bytes 102400
  394.6 0.1 dynamic-slice_reduce_fusion
  394.7 0.7 slice.91
  395.4 0.6 dynamic-slice_bitcast_fusion
  396.0 0.6 dynamic-slice_bitcast_fusion.3
  396.6 0.7 copy.93
  397.3 0.8 copy.94
  398.1 0.3 copy-done.9
  398.4 0.7 copy.95
  399.1 0.3 copy-done.8
  399.4 0.7 copy.96
  400.1 0.4 copy-done.5
  400.4 0.7 copy.97
  401.1 0.4 copy-done.4
  401.5 0.7 copy.98
  402.2 0.3 copy-done.7
  402.5 0.7 copy.99
  403.2 0.7 copy.100
  403.9 0.4 copy-done.2
  404.3 0.7 copy.101
  405.1 0.4 copy-done.1
  405.5 0.7 copy.102
  (58 shorter events, 1.0 us)
Async XLA Ops:
  0.7 0.7 copy-start.14
  0.7 0.7 copy-start.15
  0.7 0.7 copy-start.12
  0.7 0.7 copy-start.13
  1.5 0.7 copy-start.16
  1.5 0.7 copy-start.17
  2.3 0.7 copy-start.18
  48.1 0.7 copy-start.11
  355.2 0.7 copy-start.10
  356.2 40.4 %copy-start.6 = (bf16[128,1024]{1,0:T(8,128)(2,1)S(1)}, bf16[128,1024]{1,0:T(8,128)(2,1)}, u32[]{:S(2)}) copy-start(bf16[128,1024]{1,0:T(8,128)(2,1)} %get-tuple-element.28) | copy-start | bytes 786436
  356.2 41.1 %copy-start = (f32[128,1024]{1,0:T(8,128)S(1)}, f32[128,1024]{1,0:T(8,128)}, u32[]{:S(2)}) copy-start(f32[128,1024]{1,0:T(8,128)} %get-tuple-element.29) | copy-start | bytes 1572868
  397.3 1.1 copy-start.9
  398.4 1.0 copy-start.8
  399.4 1.0 copy-start.5
  400.4 1.1 copy-start.4
  401.5 1.0 copy-start.7
  401.5 1.7 copy-start.3
  403.2 1.1 copy-start.2
  404.3 1.1 copy-start.1

commit v2 on v1

--- a/solution.py
+++ b/solution.py
@@ -16,7 +16,7 @@
 RING = 4
 PLANE = 4
 SHARES = RING * 2 * PLANE
-SEMS = 512
+SEMS = 640
 
 eps_norm = 1e-06
 floor_gap = 1e-05
@@ -296,25 +296,24 @@
                 own = own + jnp.where(pred, part.astype(f32), 0.0)
             return own
 
-    class Columns:
-        def __init__(self, sources, w, R, C):
-            self.sources, self.w, self.R, self.C = sources, w, R, C
+    class Column:
+        def __init__(self, src, w, R, C, lane0):
+            self.src, self.w, self.R, self.C, self.lanes = src, w, R, C, pl.ds(lane0, C)
             self.ra, self.rz, self.rc = new(), new(4), new()
             self.out = []
 
         def spread(self):
-            R, C = self.R, self.C
-            for i, src in enumerate(self.sources):
-                dst = self.w.at[zh, c, ds(p * R, R, 16), pl.ds(i * C, C)]
-                for k, dev in plane_peers:
-                    self.out.append(push(src.at[:, ds(k * C, C, 128)], dst, dev, self.ra))
-                keep_local(src.at[:, ds(p * C, C, 128)], dst, self.ra)
+            R, C, src = self.R, self.C, self.src
+            dst = self.w.at[zh, c, ds(p * R, R, 16), self.lanes]
+            for k, dev in plane_peers:
+                self.out.append(push(src.at[:, ds(k * C, C, 128)], dst, dev, self.ra))
+            keep_local(src.at[:, ds(p * C, C, 128)], dst, self.ra)
 
         def block(self, z):
-            return self.w.at[z, c]
+            return self.w.at[z, c, :, self.lanes]
 
         def z_send(self):
-            arrived(self.w.at[zh, c], self.ra)
+            arrived(self.block(zh), self.ra)
             self.out += z_send(self.block(zh), self.block, self.rz)
 
         def z_forward(self):
@@ -322,11 +321,11 @@
 
         def z_wait(self):
             z_wait(self.block, self.rz)
-            half = self.w.at[:, c]
+            half = self.w.at[:, c, :, self.lanes]
             self.out.append(push(half, half, to_core, self.rc))
 
         def end(self):
-            arrived(self.w.at[:, 1 - c], self.rc)
+            arrived(self.w.at[:, 1 - c, :, self.lanes], self.rc)
             settle(*self.out)
 
     class Rows:
@@ -503,6 +502,108 @@
                 pl.when(pred)(take)
             settle(*self.out)
 
+    GL = PLANE * RD
+    ring = zh * 2 + c
+    home = {"yl": zh // 2, "xl": zh % 2}
+
+    def ring_place(at):
+        return {"zh": at // 2, "c": at % 2}
+
+    class Small:
+        def __init__(self):
+            self.rk, self.rc, self.rg, self.ra = new(), new(), new(2 * RING), new(2)
+            self.out = []
+
+        def one(self):
+            row = r.pack.at[:, pl.ds(0, GL + T)]
+            for _, dev in plane_peers:
+                self.out.append(push(row, r.pk.at[p], dev, self.rk))
+            keep_local(row, r.pk.at[p], self.rk)
+            chan = r.pack.at[:, pl.ds(GL + T, CW)]
+            self.out.append(push(chan, r.pc.at[p], home, self.rc, p != zh))
+            pl.when(p == zh)(lambda: keep_local(chan, r.pc.at[p], self.rc))
+
+        def two(self):
+            arrived(r.pk, self.rk)
+            r.g_all[ring] = (r.pk[0, :, 0:GL] + r.pk[1, :, 0:GL]) + (r.pk[2, :, 0:GL] + r.pk[3, :, 0:GL])
+
+            def chan():
+                arrived(r.pc, self.rc)
+                r.c_all[c] = (r.pc[0] + r.pc[1]) + (r.pc[2] + r.pc[3])
+
+            pl.when(p == zh)(chan)
+            for at in range(2 * RING):
+                own = r.g_all.at[ring]
+                self.out.append(push(own, own, ring_place(at), self.rg + ring, ring != at))
+            for at in range(2 * RING):
+                own = r.c_all.at[c]
+                self.out.append(push(own, own, ring_place(at), self.ra + c, (p == zh) & (ring != at)))
+
+        def three(self):
+            for at in range(2 * RING):
+                arrived(r.g_all.at[at], self.rg + at, ring != at)
+            for at in range(2):
+                arrived(r.c_all.at[at], self.ra + at, (p != zh) | (c != at))
+            for at in range(2 * RING):
+                r.gains[:, at * GL : (at + 1) * GL] = r.g_all[at]
+            r.chan[...] = r.c_all[0] + r.c_all[1]
+            r.chan[7:8] = r.scale[pl.ds(p, 1)]
+            lane = lax.broadcasted_iota(jnp.int32, (8, 128), 0)
+            for k in range(PLANE):
+                rows = r.pk[k, :, GL : GL + T]
+                for j in range(7):
+                    r.masks[j, k * T : (k + 1) * T] = dot_tn(rows, (lane == j).astype(f32))
+            settle(*self.out)
+
+    class SmallGrad:
+        def __init__(self):
+            self.rg, self.rc, self.rp, self.ro = new(2 * RING), new(2 * RING), new(PLANE), new()
+            self.out = []
+
+        def chan_one(self):
+            for cc in (0, 1):
+                self.out.append(
+                    push(r.gchan, r.gc.at[ring], {"zh": p, "c": cc}, self.rc + ring, (zh != p) | (c != cc))
+                )
+
+        def chan_two(self):
+            def total():
+                r.gc[ring] = r.gchan[...]
+                value = r.gchan[...]
+                for at in range(2 * RING):
+                    arrived(r.gc.at[at], self.rc + at, ring != at)
+                value = r.gc[0]
+                for at in range(1, 2 * RING):
+                    value = value + r.gc[at]
+                r.chan_out[...] = value
+
+            pl.when(p == zh)(total)
+            for _, dev in plane_peers:
+                self.out.append(push(r.chan_out, r.chan_out, dev, self.ro, p == zh))
+
+        def gain_one(self):
+            for at in range(2 * RING):
+                src = r.ggain.at[:, pl.ds(at * GL, GL)]
+                self.out.append(push(src, r.gg.at[ring], ring_place(at), self.rg + ring, ring != at))
+
+        def gain_two(self):
+            r.gg[ring] = r.ggain[:, ds(ring * GL, GL, 128)]
+            for at in range(2 * RING):
+                arrived(r.gg.at[at], self.rg + at, ring != at)
+            value = r.gg[0]
+            for at in range(1, 2 * RING):
+                value = value + r.gg[at]
+            r.gp[p] = value
+            for _, dev in plane_peers:
+                self.out.append(push(r.gp.at[p], r.gp.at[p], dev, self.rp + p))
+
+        def end(self):
+            for k, _ in plane_peers:
+                arrived(r.gp.at[k], self.rp + k)
+            r.gain_out[...] = (r.gp[0] + r.gp[1]) + (r.gp[2] + r.gp[3])
+            arrived(r.chan_out, self.ro, p != zh)
+            settle(*self.out)
+
     barrier = pltpu.get_barrier_semaphore()
     for _, dev in plane_peers:
         pl.semaphore_signal(barrier, 1, device_id=dev, device_id_type=MESH)
@@ -514,96 +615,125 @@
 
     pl.semaphore_wait(barrier, len(plane_peers) + places - 1)
 
-    in_branch = Columns((r.input_weight, r.branch_weight), r.w_ib, RD, CW)
-    dec_inj = Columns((r.decay_weight, r.inject_weight), r.w_di, RW, CW)
-    gate_up = Columns((r.mlp_gate, r.mlp_up), r.w_gu, RD, CF)
-    output = Rows(r.output_weight, r.w_o, r.st_o, RW)
-    down = Rows(r.mlp_down, r.w_dn, r.st_dn, RF)
-    ag_one, ag_conv, ag_two = Gather(r.n_one), Gather(r.conv), Gather(r.n_two)
+    w_i, w_b = Column(r.input_weight, r.w_ib, RD, CW, 0), Column(r.branch_weight, r.w_ib, RD, CW, CW)
+    w_d, w_j = Column(r.decay_weight, r.w_di, RW, CW, 0), Column(r.inject_weight, r.w_di, RW, CW, CW)
+    w_g, w_u = Column(r.mlp_gate, r.w_gu, RD, CF, 0), Column(r.mlp_up, r.w_gu, RD, CF, CF)
+    w_o, w_dn = Rows(r.output_weight, r.w_o, r.st_o, RW), Rows(r.mlp_down, r.w_dn, r.st_dn, RF)
+    ag_x, ag_conv, ag_two = Gather(r.x_all), Gather(r.conv), Gather(r.n_two)
     ag_cot, ag_out = Gather(r.cot_all), Gather(r.d_out)
-
-    in_branch.spread()
-    output.z_send()
-
-    def norm_one(o):
-        s = pl.ds(o, 16)
-        v = r.tokens[s].astype(f32)
-        r.n_one[p, s] = (v * inverse_rms(v) * r.gains[0:1]).astype(bf16)
-
-    loop(T, 16, norm_one)
-    ag_one.start()
-    dec_inj.spread()
-    gate_up.spread()
-    r.cot_all[p] = r.cotangent[...]
-    in_branch.z_send()
-    ag_one.mid()
-    ag_cot.start()
-    dec_inj.z_send()
-    gate_up.z_send()
-    down.z_send()
-    output.z_forward()
-    in_branch.z_forward()
-    in_branch.z_wait()
-    ag_one.end()
-    in_branch.end()
-
-    n_one = r.n_one[...].reshape(M, D)
-    r.pair[:, 0 : 2 * CW] = dot(n_one, r.w_ib[...].reshape(D, 2 * CW))
-    for k in range(PLANE):
-        r.u[k, 8 : 8 + T] = r.pair[k * T : (k + 1) * T, 0:CW].astype(bf16).astype(f32)
-    halo_f = new()
+    small, small_grad = Small(), SmallGrad()
     after, before = flat_z + c, flat_z - (1 - c)
     to_next = {"zh": after // NL, "zl": after % NL, "c": 1 - c}
     to_prev = {"zh": before // NL, "zl": before % NL, "c": 1 - c}
-    sent_f = push(r.u.at[:, pl.ds(T, 8)], r.u.at[:, pl.ds(0, 8)], to_next, halo_f, pos < places - 1)
-
-    def gates_one(o):
-        s = pl.ds(o, 16)
-        r.gated[s], r.slope[s] = gelu_parts(r.pair[s, CW : 2 * CW])
-
-    loop(M, 16, gates_one)
+    step = 256
+    chunk = PLANE * RD * 2
+
+    small.one()
+    halo_x = new()
+    sent_x = push(r.tokens.at[pl.ds(T - 16, 16)], r.x_halo.at[p], to_next, halo_x, pos < places - 1)
+    w_i.spread()
+    w_o.z_send()
+    r.x_all[p] = r.tokens[...]
+    r.cot_all[p] = r.cotangent[...]
+    ag_x.start()
+    w_d.spread()
+    w_j.spread()
+    w_i.z_send()
+    small.two()
 
     @pl.when(pos == 0)
     def _():
-        r.u[:, 0:8] = jnp.zeros((PLANE, 8, CW), f32)
-
-    arrived(r.u.at[:, pl.ds(0, 8)], halo_f, pos > 0)
-    settle(sent_f)
-
+        r.x_halo[p] = jnp.zeros((16, D), bf16)
+
+    arrived(r.x_halo.at[p], halo_x, pos > 0)
+    halo_p = new(PLANE)
+    sent_p = [push(r.x_halo.at[p], r.x_halo.at[p], dev, halo_p + p) for _, dev in plane_peers]
+    ag_x.mid()
+    w_b.spread()
+    small.three()
+
+    def norm_block(k):
+        def norm_one(o):
+            s = pl.ds(o, 32)
+            v = r.x_all[k, s].astype(f32)
+            r.n_one[k, s] = (v * inverse_rms(v) * r.gains[0:1]).astype(bf16)
+
+        loop(T, 32, norm_one)
+
+    norm_block(p)
+    w_d.z_send()
+    w_o.z_forward()
+    ag_x.wait_x()
+    norm_block(px)
+    ag_x.wait_y()
+    norm_block(py)
+    for k, _ in plane_peers:
+        arrived(r.x_halo.at[k], halo_p + k)
+    v = r.x_halo[...].reshape(PLANE * 16, D).astype(f32)
+    r.n_halo[...] = (v * inverse_rms(v) * r.gains[0:1]).astype(bf16).reshape(PLANE, 16, D)
+    ag_x.wait_d()
+    norm_block(pd)
+    settle(*ag_x.out, sent_x, *sent_p)
+    w_g.spread()
+    w_u.spread()
+    w_i.z_forward()
+    w_i.z_wait()
+    w_o.z_wait()
+    w_j.z_send()
+    w_i.end()
+
+    def weight_ib(lanes):
+        return r.w_ib[:, :, :, lanes].reshape(D, CW)
+
+    lanes_a, lanes_b = pl.ds(0, CW), pl.ds(CW, CW)
+    halo = dot(r.n_halo[...].reshape(PLANE * 16, D), weight_ib(lanes_a)).astype(bf16).astype(f32)
+    body = dot(r.n_one[...].reshape(M, D), weight_ib(lanes_a)).astype(bf16).astype(f32)
     for k in range(PLANE):
-
-        def convolve(o, k=k):
+        r.u[k, 0:8] = halo[k * 16 + 8 : (k + 1) * 16]
+        r.u[k, 8 : 8 + T] = body[k * T : (k + 1) * T]
+
+    def wide(j, rows):
+        return jnp.concatenate([r.masks[j, rows]] * (CW // 128), axis=1) > 0.5
+
+    def convolve(o):
+        for k in range(PLANE):
             ext = r.u[k, pl.ds(o, 24)]
             rows = ds(k * T + o, 16, 16)
-            keep = r.masks[rows]
             total = r.chan[4:5] + r.chan[0:1] * ext[8:24]
             for j in range(1, 4):
-                total = total + jnp.where(keep[:, j : j + 1] > 0.5, r.chan[j : j + 1] * ext[8 - j : 24 - j], 0.0)
+                total = total + jnp.where(wide(j, rows), r.chan[j : j + 1] * ext[8 - j : 24 - j], 0.0)
             r.conv[p, rows] = total.astype(bf16)
 
-        loop(T, 16, convolve)
+    loop(T, 16, convolve)
     ag_conv.start()
-    ag_cot.mid()
-    dec_inj.z_forward()
+    w_o.plane_wait()
+    w_d.z_forward()
+    w_d.z_wait()
+    w_b.z_send()
     ag_conv.mid()
-    output.z_wait()
-    dec_inj.z_wait()
-    output.plane_wait()
-    dec_inj.end()
-
-    def pre(q):
-        return dot(r.conv[q], r.w_di[q].reshape(W // RING, 2 * CW))
-
-    r.pair[:, 0 : 2 * CW] = pre(p)
+    w_d.end()
+
+    def pre(q, lanes):
+        return dot(r.conv[q], r.w_di[q, :, :, lanes].reshape(W // RING, CW))
+
+    r.pair[:, 0:CW] = pre(p, lanes_a)
     for q, wait in ((px, ag_conv.wait_x), (py, ag_conv.wait_y), (pd, ag_conv.wait_d)):
         wait()
-        r.pair[:, 0 : 2 * CW] += pre(q)
+        r.pair[:, 0:CW] += pre(q, lanes_a)
     settle(*ag_conv.out)
+    ag_cot.start()
+    w_j.z_forward()
+    w_j.z_wait()
+    w_g.z_send()
+    w_j.end()
+    r.pair[:, CW : 2 * CW] = pre(0, lanes_b)
+    for q in range(1, PLANE):
+        r.pair[:, CW : 2 * CW] += pre(q, lanes_b)
 
     def decay_terms(s, rg):
         log_a = -rate_scale * rg * r.chan[7:8]
         gap = minus_expm1(2.0 * log_a)
-        first = r.masks[s][:, 0:1] > 0.5
+        first = wide(0, s)
         return log_a, gap, jnp.where(first, 1.0, jnp.sqrt(jnp.maximum(gap, floor_gap))), first
 
     def gates_two(o):
@@ -641,22 +771,30 @@
         r.carry_f[pos, PLANE + k : PLANE + k + 1] = ends[2 * k]
         r.ends[k : k + 1] = ends[2 * k + 1]
     carry_f.send()
-    output.end()
+    ag_cot.mid()
+    w_b.z_forward()
+    w_b.z_wait()
+    w_b.end()
+    r.work[...] = dot(r.n_one[...].reshape(M, D), weight_ib(lanes_b))
+
+    def gates_one(o):
+        s = pl.ds(o, 16)
+        r.gated[s], r.slope[s] = gelu_parts(r.work[s])
+
+    loop(M, 16, gates_one)
+    w_o.end()
     carry_f.fold(r.into)
-
     for k in range(PLANE):
-        into = r.into[k : k + 1]
-        r.state[k, 0:8] = jnp.broadcast_to(into, (8, CW))
-
-        def mix(o, k=k, into=into):
+        r.state[k, 0:8] = jnp.broadcast_to(r.into[k : k + 1], (8, CW))
+
+    def mix(o):
+        for k in range(PLANE):
             s, t = ds(k * T + o, 16, 16), ds(8 + o, 16, 8)
-            state = r.state[k, t] + r.cum[s] * into
+            state = r.state[k, t] + r.cum[s] * r.into[k : k + 1]
             r.state[k, t] = state
             r.mixed[s] = (state * r.gated[s]).astype(bf16)
 
-        loop(T, 16, mix)
-
-    step = 256
+    loop(T, 16, mix)
 
     def out_part(o):
         q = pl.ds(o, step)
@@ -665,9 +803,10 @@
     loop(D, step, out_part)
     rs_one = Scatter(r.part, r.got_one)
     rs_one.start()
+    w_u.z_send()
     ag_cot.end()
-    gate_up.z_forward()
     rs_one.mid()
+    w_g.z_forward()
     rs_one.end()
 
     def norm_two(o, summed):
@@ -678,18 +817,21 @@
 
     rs_one.each(16, norm_two)
     ag_two.start()
-    gate_up.z_wait()
-    down.z_forward()
+    w_g.z_wait()
+    w_dn.z_send()
     ag_two.mid()
-    gate_up.end()
+    w_g.end()
+    w_u.z_forward()
     ag_two.end()
 
     def mlp_in(o):
         q = pl.ds(o, step)
         r.pair[:, q] = dot(r.n_two[...].reshape(M, D), r.w_gu[:, :, :, q].reshape(D, step))
 
-    loop(2 * CF, step, mlp_in)
-    down.z_wait()
+    loop(CF, step, mlp_in)
+    w_u.z_wait()
+    w_u.end()
+    loop(CF, step, lambda o: mlp_in(pl.multiple_of(CF + o, step)))
 
     def gates_mlp(o):
         s = pl.ds(o, 16)
@@ -700,8 +842,20 @@
         r.pair[s, CF : 2 * CF] = value
 
     loop(M, 16, gates_mlp)
-    down.plane_wait()
-    down.end()
+
+    def grad_down(o):
+        q = pl.ds(o, step)
+        r.g_dn[q] = dot_tn(r.hidden[:, q], r.cot_all[...].reshape(M, D)).astype(bf16)
+
+    loop(CF, step, grad_down)
+    g_dn = RowsGrad(r.g_dn, r.h_dn, r.sg_dn, r.z_dn, RF, r.grad_mlp_down)
+    g_dn.core_send()
+    w_dn.z_forward()
+    g_dn.plane_send()
+    w_dn.z_wait()
+    g_dn.z_send()
+    w_dn.plane_wait()
+    w_dn.end()
 
     for k in range(CF // step):
         q = pl.ds(k * step, step)
@@ -710,7 +864,6 @@
         r.d_pair[:, CF + k * step : CF + (k + 1) * step] = (
             back * r.pair[:, CF + k * step : CF + (k + 1) * step]
         ).astype(bf16)
-    chunk = PLANE * RD * 2
 
     def d_two_part(z, _):
         q = ds(z * chunk, chunk, chunk)
@@ -723,38 +876,35 @@
     rs_two = Scatter(r.part, r.got_two)
     rs_two.start()
 
+    def grad_gate_up(lane0):
+        lanes = pl.ds(lane0, CF)
+
+        def run(z, _):
+            q = ds(z * chunk, chunk, chunk)
+            value = dot_tn(r.n_two[:, :, q].reshape(M, chunk), r.d_pair[:, lanes])
+            r.w_gu[z, :, :, lanes] = value.astype(bf16).reshape(2, chunk // 2, CF)
+            return 0
+
+        lax.fori_loop(0, RING, run, 0)
+
+    grad_gate_up(0)
+    g_g = ColumnsGrad(r.w_gu, r.h_gu, r.z_gu, r.l_gu, RD, 0, CF, ((0, CF, r.grad_mlp_gate),))
+    g_g.core_send()
+    rs_two.mid()
+    grad_gate_up(CF)
+    g_u = ColumnsGrad(r.w_gu, r.h_gu, r.z_gu, r.l_gu, RD, CF, CF, ((CF, CF, r.grad_mlp_up),))
+    g_u.core_send()
+    g_dn.z_forward()
+    g_g.z_send()
+
     def act_part(o):
         q = pl.ds(o, step)
         r.part_act[:, :, q] = dot(r.hidden[...], r.w_dn[:, q]).astype(bf16).reshape(PLANE, T, step)
 
     loop(D, step, act_part)
-    rs_act = Scatter(r.part_act, r.got_act)
-    rs_act.start()
-
-    def grad_down(o):
-        q = pl.ds(o, step)
-        r.w_dn[q] = dot_tn(r.hidden[:, q], r.cot_all[...].reshape(M, D)).astype(bf16)
-
-    loop(CF, step, grad_down)
-    g_down = RowsGrad(r.w_dn, r.h_dn, r.sg_dn, r.z_dn, RF, r.grad_mlp_down)
-    g_down.core_send()
-    rs_two.mid()
-    g_down.plane_send()
-
-    def grad_gate_up(z, _):
-        q = ds(z * chunk, chunk, chunk)
-        value = dot_tn(r.n_two[:, :, q].reshape(M, chunk), r.d_pair[...])
-        r.w_gu[z] = value.astype(bf16).reshape(2, chunk // 2, 2 * CF)
-        return 0
-
-    lax.fori_loop(0, RING, grad_gate_up, 0)
-    g_gu = ColumnsGrad(
-        r.w_gu, r.h_gu, r.z_gu, r.l_gu, RD, 0, 2 * CF, ((0, CF, r.grad_mlp_gate), (CF, CF, r.grad_mlp_up))
-    )
-    g_gu.core_send()
-    rs_two.end()
     r.ggain[...] = jnp.zeros_like(r.ggain)
     r.gchan[...] = jnp.zeros_like(r.gchan)
+    rs_two.end()
 
     def norm_two_back(o, d_two):
         s = pl.ds(o, 16)
@@ -769,30 +919,24 @@
 
     rs_two.each(16, norm_two_back)
     ag_out.start()
-    g_down.z_send()
-    rs_act.mid()
-    g_gu.z_send()
+    g_dn.end()
+    g_u.z_send()
     ag_out.mid()
-    g_down.z_forward()
-    rs_act.end()
-
-    def finish_act(o, summed):
-        s = pl.ds(o, 16)
-        r.activations[s] = (r.x_one[s] + summed).astype(bf16)
-
-    rs_act.each(16, finish_act)
+    g_g.z_forward()
     ag_out.end()
+    rs_act = Scatter(r.part_act, r.got_act)
+    rs_act.start()
 
     r.work[...] = dot_nt(r.d_out[...].reshape(M, D), r.w_o[...])
-    for k in range(PLANE):
-
-        def split(o, k=k):
+
+    def split(o):
+        for k in range(PLANE):
             s = ds(k * T + o, 16, 16)
             d_mixed = r.work[s]
             r.d_gu[s, CW : 2 * CW] = (d_mixed * r.state[k, ds(8 + o, 16, 8)] * r.slope[s]).astype(bf16)
             r.work[s] = d_mixed * r.gated[s]
 
-        loop(T, 16, split)
+    loop(T, 16, split)
 
     def scan_backward(i, carry):
         j = T // 8 - 1 - i
@@ -822,76 +966,89 @@
         r.w_o[q] = dot_tn(r.mixed[:, q], r.d_out[...].reshape(M, D)).astype(bf16)
 
     loop(CW, 128, grad_out)
-    g_out = RowsGrad(r.w_o, r.h_o, r.sg_o, r.z_o, RW, r.grad_output_weight)
-    g_out.core_send()
+    g_o = RowsGrad(r.w_o, r.h_o, r.sg_o, r.z_o, RW, r.grad_output_weight)
+    g_o.core_send()
+    rs_act.mid()
+
+    def d_branch_part(z, _):
+        q = ds(z * chunk, chunk, chunk)
+        r.part[:, :, q] = (
+            dot_nt(r.d_gu[:, lanes_b], r.w_ib[z, :, :, lanes_b].reshape(chunk, CW))
+            .astype(bf16)
+            .reshape(PLANE, T, chunk)
+        )
+        value = dot_tn(r.n_one[:, :, q].reshape(M, chunk), r.d_gu[:, lanes_b])
+        r.w_ib[z, :, :, lanes_b] = value.astype(bf16).reshape(2, chunk // 2, CW)
+        return 0
+
+    lax.fori_loop(0, RING, d_branch_part, 0)
+    g_b = ColumnsGrad(r.w_ib, r.h_ib, r.z_ib, r.l_ib, RD, CW, CW, ((CW, CW, r.grad_branch_weight),))
+    g_b.core_send()
+    g_g.plane_send()
     carry_b.fold(r.into)
 
-    for k in range(PLANE):
-        into = r.into[k : k + 1]
-
-        def back(o, k=k, into=into):
+    def back(o):
+        sums = [jnp.zeros((1, CW), f32)] * 2
+        for k in range(PLANE):
             s = ds(k * T + o, 16, 16)
-            adjoint = r.work[s] + r.cum[s] * into
+            adjoint = r.work[s] + r.cum[s] * r.into[k : k + 1]
             previous = r.state[k, pl.ds(o, 24)][7:23]
             rg, ig, decay, conv = r.rgate[s], r.igate[s], r.decay[s], r.conv[p, s].astype(f32)
             _, gap, mult, first = decay_terms(s, rg)
             d_mult = jnp.where(first, 0.0, adjoint * ig * conv)
-            d_log = adjoint * previous * decay - jnp.where(
-                gap > floor_gap, (1.0 - gap) * d_mult / mult, 0.0
-            )
+            d_log = adjoint * previous * decay - jnp.where(gap > floor_gap, (1.0 - gap) * d_mult / mult, 0.0)
             d_decay = (-rate_scale * r.chan[7:8] * d_log * rg * (1.0 - rg)).astype(bf16)
             d_inject = (adjoint * mult * conv * ig * (1.0 - ig)).astype(bf16)
             r.d_pre[s, 0:CW] = d_decay
             r.d_pre[s, CW : 2 * CW] = d_inject
-            r.gchan[5:6] += jnp.sum(d_decay.astype(f32), axis=0, keepdims=True)
-            r.gchan[6:7] += jnp.sum(d_inject.astype(f32), axis=0, keepdims=True)
+            sums[0] = sums[0] + jnp.sum(d_decay.astype(f32), axis=0, keepdims=True)
+            sums[1] = sums[1] + jnp.sum(d_inject.astype(f32), axis=0, keepdims=True)
             r.d_conv[k, pl.ds(o, 16)] = adjoint * mult * ig
-
-        loop(T, 16, back)
+        r.gchan[5:6] += sums[0]
+        r.gchan[6:7] += sums[1]
+
+    loop(T, 16, back)
 
     def conv_part(q, _):
         r.part_conv[q] = dot_nt(r.d_pre[...], r.w_di[q].reshape(W // RING, 2 * CW)).astype(bf16)
         return 0
 
     lax.fori_loop(0, RING, conv_part, 0)
+    rs_act.end()
     rs_conv = Scatter(r.part_conv, r.got_conv)
     rs_conv.start()
-    g_gu.z_forward()
-    g_out.plane_send()
-
-    def grad_dec_inj(q, _):
-        value = dot_tn(r.conv[q], r.d_pre[...])
-        r.w_di[q] = value.astype(bf16).reshape(2, W // SHARES * PLANE, 2 * CW)
-        return 0
-
-    lax.fori_loop(0, RING, grad_dec_inj, 0)
-    g_di = ColumnsGrad(
-        r.w_di, r.h_di, r.z_di, r.l_di, RW, 0, 2 * CW, ((0, CW, r.grad_decay_weight), (CW, CW, r.grad_inject_weight))
-    )
-    g_di.core_send()
+
+    def finish_act(o, summed):
+        s = pl.ds(o, 16)
+        r.activations[s] = (r.x_one[s] + summed).astype(bf16)
+
+    rs_act.each(16, finish_act)
+    g_u.z_forward()
+    g_b.z_send()
+
+    def grad_dec_inj(lanes):
+        def run(q, _):
+            value = dot_tn(r.conv[q], r.d_pre[:, lanes])
+            r.w_di[q, :, :, lanes] = value.astype(bf16).reshape(2, W // SHARES * PLANE, CW)
+            return 0
+
+        lax.fori_loop(0, RING, run, 0)
+
+    grad_dec_inj(lanes_a)
+    g_d = ColumnsGrad(r.w_di, r.h_di, r.z_di, r.l_di, RW, 0, CW, ((0, CW, r.grad_decay_weight),))
+    g_d.core_send()
+    g_o.plane_send()
     rs_conv.mid()
-
-    def d_branch_part(z, _):
-        q = ds(z * chunk, chunk, chunk)
-        r.part[:, :, q] = (
-            dot_nt(r.d_gu[:, CW : 2 * CW], r.w_ib[z, :, :, CW : 2 * CW].reshape(chunk, CW))
-            .astype(bf16)
-            .reshape(PLANE, T, chunk)
-        )
-        value = dot_tn(r.n_one[:, :, q].reshape(M, chunk), r.d_gu[:, CW : 2 * CW])
-        r.w_ib[z, :, :, CW : 2 * CW] = value.astype(bf16).reshape(2, chunk // 2, CW)
-        return 0
-
-    lax.fori_loop(0, RING, d_branch_part, 0)
-    g_branch = ColumnsGrad(r.w_ib, r.h_ib, r.z_ib, r.l_ib, RD, CW, CW, ((CW, CW, r.grad_branch_weight),))
-    g_branch.core_send()
-    g_out.z_send()
-    g_di.z_send()
-    g_branch.z_send()
+    grad_dec_inj(lanes_b)
+    g_j = ColumnsGrad(r.w_di, r.h_di, r.z_di, r.l_di, RW, CW, CW, ((CW, CW, r.grad_inject_weight),))
+    g_j.core_send()
+    g_u.plane_send()
+    g_o.z_send()
+    g_b.z_forward()
+    g_d.z_send()
     rs_conv.end()
 
     for half in (0, 1):
-        rows = M // 2
 
         def add_conv(o, half=half):
             for k in (2 * half, 2 * half + 1):
@@ -901,19 +1058,23 @@
         loop(T, 16, add_conv)
     halo_b = new()
     sent_b = push(r.d_conv.at[:, pl.ds(0, 8)], r.d_conv.at[:, pl.ds(T, 8)], to_prev, halo_b, pos > 0)
-    for k in range(PLANE):
-
-        def taps_back(o, k=k):
+
+    def taps_back(o):
+        sums = [jnp.zeros((1, CW), f32)] * 5
+        for k in range(PLANE):
             ext = r.u[k, pl.ds(o, 24)]
-            keep = r.masks[ds(k * T + o, 16, 16)]
+            rows = ds(k * T + o, 16, 16)
             dc = r.d_conv[k, pl.ds(o, 16)]
-            r.gchan[4:5] += jnp.sum(dc, axis=0, keepdims=True)
-            r.gchan[0:1] += jnp.sum(dc * ext[8:24], axis=0, keepdims=True)
+            sums[4] = sums[4] + jnp.sum(dc, axis=0, keepdims=True)
+            sums[0] = sums[0] + jnp.sum(dc * ext[8:24], axis=0, keepdims=True)
             for j in range(1, 4):
-                term = jnp.where(keep[:, j : j + 1] > 0.5, dc * ext[8 - j : 24 - j], 0.0)
-                r.gchan[j : j + 1] += jnp.sum(term, axis=0, keepdims=True)
-
-        loop(T, 16, taps_back)
+                term = jnp.where(wide(j, rows), dc * ext[8 - j : 24 - j], 0.0)
+                sums[j] = sums[j] + jnp.sum(term, axis=0, keepdims=True)
+        for j in range(5):
+            r.gchan[j : j + 1] += sums[j]
+
+    loop(T, 16, taps_back)
+    small_grad.chan_one()
 
     @pl.when(pos == places - 1)
     def _():
@@ -921,22 +1082,21 @@
 
     arrived(r.d_conv.at[:, pl.ds(T, 8)], halo_b, pos < places - 1)
     settle(sent_b)
-    for k in range(PLANE):
-
-        def conv_back(o, k=k):
+
+    def conv_back(o):
+        for k in range(PLANE):
             ext = r.d_conv[k, pl.ds(o, 24)]
             rows = ds(k * T + o, 16, 16)
-            keep = r.masks[rows]
             total = r.chan[0:1] * ext[0:16]
             for j in range(1, 4):
-                total = total + jnp.where(keep[:, 3 + j : 4 + j] > 0.5, r.chan[j : j + 1] * ext[j : 16 + j], 0.0)
+                total = total + jnp.where(wide(3 + j, rows), r.chan[j : j + 1] * ext[j : 16 + j], 0.0)
             r.d_gu[rows, 0:CW] = total.astype(bf16)
 
-        loop(T, 16, conv_back)
+    loop(T, 16, conv_back)
 
     def d_input_part(z, _):
         q = ds(z * chunk, chunk, chunk)
-        value = dot_nt(r.d_gu[:, 0:CW], r.w_ib[z, :, :, 0:CW].reshape(chunk, CW)).reshape(PLANE, T, chunk)
+        value = dot_nt(r.d_gu[:, lanes_a], r.w_ib[z, :, :, lanes_a].reshape(chunk, CW)).reshape(PLANE, T, chunk)
         r.part[:, :, q] = (r.part[:, :, q].astype(f32) + value).astype(bf16)
         return 0
 
@@ -946,21 +1106,23 @@
 
     def grad_input(z, _):
         q = ds(z * chunk, chunk, chunk)
-        value = dot_tn(r.n_one[:, :, q].reshape(M, chunk), r.d_gu[:, 0:CW])
-        r.w_ib[z, :, :, 0:CW] = value.astype(bf16).reshape(2, chunk // 2, CW)
+        value = dot_tn(r.n_one[:, :, q].reshape(M, chunk), r.d_gu[:, lanes_a])
+        r.w_ib[z, :, :, lanes_a] = value.astype(bf16).reshape(2, chunk // 2, CW)
         return 0
 
     lax.fori_loop(0, RING, grad_input, 0)
-    g_input = ColumnsGrad(r.w_ib, r.h_ib, r.z_ib, r.l_ib, RD, 0, CW, ((0, CW, r.grad_input_weight),))
-    g_input.core_send()
+    g_i = ColumnsGrad(r.w_ib, r.h_ib, r.z_ib, r.l_ib, RD, 0, CW, ((0, CW, r.grad_input_weight),))
+    g_i.core_send()
+    g_o.z_forward()
+    g_b.plane_send()
+    g_d.z_forward()
     rs_three.mid()
-    g_input.z_send()
-    g_down.end()
-    g_out.z_forward()
-    g_di.z_forward()
-    g_branch.z_forward()
-    g_gu.plane_send()
-    g_input.z_forward()
+    small_grad.chan_two()
+    g_j.z_send()
+    g_i.z_send()
+    g_o.end()
+    g_g.end()
+    g_u.end()
     rs_three.end()
 
     def norm_one_back(o, d_n):
@@ -973,14 +1135,18 @@
         r.d_tokens[s] = r.d_one[s] + rs * (dz - z * jnp.mean(dz * z, axis=-1, keepdims=True))
 
     rs_three.each(16, norm_one_back)
-    g_out.end()
-    g_di.plane_send()
-    g_branch.plane_send()
-    g_gu.end()
-    g_input.plane_send()
-    g_di.end()
-    g_branch.end()
-    g_input.end()
+    small_grad.gain_one()
+    g_d.plane_send()
+    g_j.z_forward()
+    g_i.z_forward()
+    small_grad.gain_two()
+    g_b.end()
+    g_j.plane_send()
+    g_i.plane_send()
+    g_d.end()
+    small_grad.end()
+    g_j.end()
+    g_i.end()
     assert not sent
 
 
@@ -996,22 +1162,21 @@
 )
 
 
-def run_layer(NL, tokens, cotangent, gains, chan, masks, weights):
+def run_layer(NL, tokens, cotangent, pack, scale, weights):
     T, D = tokens.shape
     W, F = weights["branch_weight"].shape[1], weights["mlp_gate"].shape[1]
     CW, CF = W // PLANE, F // PLANE
     RD, RW, RF = D // SHARES, W // SHARES, F // SHARES
-    M, places = PLANE * T, RING * NL * 2
+    GL, M, places = PLANE * RD, PLANE * T, RING * NL * 2
     vmem, hbm = pl.BlockSpec(memory_space=pltpu.VMEM), pl.BlockSpec(memory_space=pl.ANY)
-    ins = ["tokens", "cotangent", "gains", "chan", "masks", *WEIGHTS]
+    ins = ["tokens", "cotangent", "pack", "scale", *WEIGHTS]
     outs = {
         "activations": ((T, D), bf16),
         "d_tokens": ((T, D), f32),
         **{"grad_" + name: (weights[name].shape, f32) for name in WEIGHTS},
-        "ggain": ((8, D), f32),
-        "gchan": ((8, CW), f32),
+        "gain_out": ((8, GL), f32),
+        "chan_out": ((8, CW), f32),
     }
-    outs = {name if name[:5] != "grad_" else name: spec for name, spec in outs.items()}
     scratch = {
         "w_ib": ((RING, 2, PLANE * RD, 2 * CW), bf16),
         "w_di": ((RING, 2, PLANE * RW, 2 * CW), bf16),
@@ -1063,6 +1228,22 @@
         "carry_f": ((places, 2 * PLANE, CW), f32),
         "carry_b": ((places, 2 * PLANE, CW), f32),
         "into": ((8, CW), f32),
+        "x_all": ((PLANE, T, D), bf16),
+        "x_halo": ((PLANE, 16, D), bf16),
+        "n_halo": ((PLANE, 16, D), bf16),
+        "g_dn": ((CF, D), bf16),
+        "masks": ((7, M, 128), f32),
+        "pk": ((PLANE, 8, GL + T), f32),
+        "pc": ((PLANE, 8, CW), f32),
+        "g_all": ((2 * RING, 8, GL), f32),
+        "c_all": ((2, 8, CW), f32),
+        "gains": ((8, D), f32),
+        "chan": ((8, CW), f32),
+        "ggain": ((8, D), f32),
+        "gchan": ((8, CW), f32),
+        "gg": ((2 * RING, 8, GL), f32),
+        "gp": ((PLANE, 8, GL), f32),
+        "gc": ((2 * RING, 8, CW), f32),
         "ends": ((8, CW), f32),
     }
     dims = SimpleNamespace(
@@ -1072,7 +1253,7 @@
     results = pl.pallas_call(
         partial(layer, dims),
         out_shape=[jax.ShapeDtypeStruct(shape, kind) for shape, kind in outs.values()],
-        in_specs=[vmem] * 5 + [hbm] * len(WEIGHTS),
+        in_specs=[vmem] * 4 + [hbm] * len(WEIGHTS),
         out_specs=[vmem] * len(outs),
         scratch_shapes=[pltpu.VMEM(shape, kind) for shape, kind in scratch.values()]
         + [pltpu.SemaphoreType.DMA((SEMS,)), pltpu.SemaphoreType.DMA((SEMS,))],
@@ -1081,7 +1262,7 @@
         ),
         cost_estimate=pl.CostEstimate(flops=flops, bytes_accessed=8 * 2**20, transcendentals=M * CW * 16),
         name="griffin_layer",
-    )(tokens, cotangent, gains, chan, masks, *[weights[name] for name in WEIGHTS])
+    )(tokens, cotangent, pack, scale, *[weights[name] for name in WEIGHTS])
     return dict(zip(outs, results, strict=True))
 
 
@@ -1108,44 +1289,47 @@
 ):
     devices = math.prod(sizes.values())
     width = branch_weight.shape[1]
-    own_d, own_w = first_gain.shape[0], conv_bias.shape[0]
     NL = sizes["zl"]
     at = {name: lax.axis_index(name) for name in AXES}
     T = tokens.shape[1]
 
-    small = jnp.concatenate(
-        [
-            jnp.stack([first_gain, second_gain]).reshape(-1),
-            jnp.concatenate([conv_taps.T, jnp.stack([conv_bias, decay_bias, inject_bias])]).reshape(-1),
-        ]
-    ).astype(f32)
-    small = jnp.concatenate([small, doc_lengths[0].astype(f32)])
-    small = lax.all_gather(small, AXES)
-    gains = small[:, : 2 * own_d].reshape(devices, 2, own_d).transpose(1, 0, 2).reshape(2, -1)
-    chan = small[:, 2 * own_d : 2 * own_d + 7 * own_w].reshape(devices, 7, own_w).transpose(1, 0, 2).reshape(7, -1)
-    scale = jnp.exp2(-decay_exponent.astype(f32))
-    chan = jnp.concatenate([chan, scale[None]])
     mine = at["yl"] * 2 + at["xl"]
-    chan = lax.dynamic_slice_in_dim(chan, mine * (width // PLANE), width // PLANE, 1)
-    lengths = small[:, 2 * own_d + 7 * own_w :].astype(jnp.int32)
-    across = sizes["xh"] * 2
-    rows = (at["yh"] * 2 + jnp.arange(PLANE) // 2) * across + at["xh"] * 2 + jnp.arange(PLANE) % 2
-    lengths = lengths[rows]
-
-    ends = jnp.cumsum(lengths, axis=1)
+    ring = at["zh"] * 2 + at["c"]
+    share = ring * PLANE + mine
+    groups = devices // SHARES
+
+    def pooled(value, axis=0):
+        if groups == 1:
+            return value
+        whole = lax.all_gather(value, AXES, axis=axis, tiled=True)
+        size = whole.shape[axis] // SHARES
+        return lax.dynamic_slice_in_dim(whole, share * size, size, axis)
+
+    gains = pooled(jnp.stack([first_gain, second_gain]).astype(f32), 1)
+    chan = pooled(jnp.concatenate([conv_taps.T, jnp.stack([conv_bias, decay_bias, inject_bias])]).astype(f32), 1)
+    RD, RW = gains.shape[1], chan.shape[1]
+    gain_pack = lax.dynamic_update_slice(jnp.zeros((8, PLANE * RD), f32), gains, (0, mine * RD))
+    chan_pack = lax.dynamic_update_slice(
+        jnp.zeros((8, 2 * PLANE * RW), f32), chan, (0, (at["c"] * PLANE + mine) * RW)
+    )
+    scale = jnp.exp2(-decay_exponent.astype(f32)).reshape(PLANE, width // PLANE)
+    scale = jnp.concatenate([scale, scale])
+
+    lengths = doc_lengths[0]
+    ends = jnp.cumsum(lengths)
     starts = ends - lengths
     index = (at["zh"] * NL + at["zl"]) * 2 + at["c"]
     count = T * RING * NL * 2
     where = index * T - 3 + jnp.arange(T + 6, dtype=jnp.int32)
-    seg = jnp.sum((ends[:, None, :] <= where[None, :, None]).astype(jnp.int32), axis=2)
+    seg = jnp.sum((ends[:, None] <= where[None, :]).astype(jnp.int32), axis=0)
     seg = jnp.where((where < 0) | (where >= count), -1, seg)
-    here = seg[:, 3 : 3 + T]
-    first = jnp.any(starts[:, None, :] == where[None, 3 : 3 + T, None], axis=2)
+    here = seg[3 : 3 + T]
+    first = jnp.any(starts[:, None] == where[None, 3 : 3 + T], axis=0)
     masks = [first]
-    masks += [seg[:, 3 - k : 3 - k + T] == here for k in (1, 2, 3)]
-    masks += [seg[:, 3 + k : 3 + k + T] == here for k in (1, 2, 3)]
-    masks += [first]
-    masks = jnp.stack(masks, axis=-1).astype(f32).reshape(PLANE * T, 8)
+    masks += [seg[3 - k : 3 - k + T] == here for k in (1, 2, 3)]
+    masks += [seg[3 + k : 3 + k + T] == here for k in (1, 2, 3)]
+    masks = jnp.stack([*masks, first]).astype(f32)
+    pack = jnp.concatenate([gain_pack, masks, chan_pack], axis=1)
 
     weights = dict(
         zip(
@@ -1154,32 +1338,26 @@
             strict=True,
         )
     )
-    groups = devices // SHARES
-    if groups > 1:
-        share = (at["zh"] * 2 + at["c"]) * PLANE + mine
-        for name, value in weights.items():
-            whole = lax.all_gather(value, AXES, axis=0, tiled=True)
-            weights[name] = lax.dynamic_slice_in_dim(whole, share * (whole.shape[0] // SHARES), whole.shape[0] // SHARES)
-    pad = jnp.zeros((6, gains.shape[1]), f32)
-    got = run_layer(NL, tokens[0], cotangent[0], jnp.concatenate([gains, pad]), chan, masks, weights)
-    grads = {name: got["grad_" + name] for name in WEIGHTS}
-    if groups > 1:
-        for name, value in grads.items():
-            whole = jnp.zeros((value.shape[0] * SHARES, value.shape[1]), bf16)
-            whole = lax.dynamic_update_slice_in_dim(whole, value.astype(bf16), share * value.shape[0], 0)
-            grads[name] = lax.psum_scatter(whole, AXES, scatter_dimension=0, tiled=True).astype(f32)
-
-    gain_grads = got["ggain"][:2].reshape(2, devices, own_d).transpose(1, 0, 2).reshape(devices, -1)
-    chan_grads = jnp.zeros((7, width), f32)
-    chan_grads = lax.dynamic_update_slice_in_dim(chan_grads, got["gchan"][:7], mine * (width // PLANE), 1)
-    chan_grads = chan_grads.reshape(7, devices, own_w).transpose(1, 0, 2).reshape(devices, -1)
-    sums = lax.psum_scatter(jnp.concatenate([gain_grads, chan_grads], 1), AXES, scatter_dimension=0, tiled=True)[0]
-    gain_sum = sums[: 2 * own_d].reshape(2, own_d)
-    chan_sum = sums[2 * own_d :].reshape(7, own_w)
+    weights = {name: pooled(value) for name, value in weights.items()}
+    got = run_layer(NL, tokens[0], cotangent[0], pack, scale, weights)
+
+    def returned(value, axis=0):
+        if groups == 1:
+            return value
+        shape = list(value.shape)
+        size = shape[axis]
+        shape[axis] = size * SHARES
+        whole = lax.dynamic_update_slice_in_dim(jnp.zeros(shape, bf16), value.astype(bf16), share * size, axis)
+        return lax.psum_scatter(whole, AXES, scatter_dimension=axis, tiled=True).astype(f32)
+
+    grads = [returned(got["grad_" + name]) for name in WEIGHTS]
+    gain_sum = returned(lax.dynamic_slice_in_dim(got["gain_out"], mine * RD, RD, 1)[:2], 1)
+    chan_sum = lax.dynamic_slice_in_dim(got["chan_out"], (at["c"] * PLANE + mine) * RW, RW, 1)
+    chan_sum = returned(chan_sum[:7], 1)
     return (
         got["activations"][None],
         got["d_tokens"][None],
-        *[grads[name] for name in WEIGHTS],
+        *grads,
         gain_sum[0],
         gain_sum[1],
         chan_sum[:4].T,

time: 407 us -> 264 us (0.65)
  blocking collectives: 79.7 us -> 0 us
  Pallas kernels: 305 us -> 245 us
    unnamed x2 -> x0, blocking collectives: 79.7 us -> none
    pallas_call x1, Pallas kernels: 305 us -> 245 us  [run_layer(): pl.pallas_call(partial(layer, dims), out_shape=[jax.ShapeDtypeStruct(shap...]
    unnamed x50 -> x44, local copies, waits for them, and re-layouts: 12.9 us -> 12.3 us
where the time goes in v2:
time: 264 us
  Pallas kernels  245 us (93%)
  local copies, waits for them, and re-layouts  16.2 us (6%)
    pallas_call x1, Pallas kernels, run_layer(): pl.pallas_call(partial(layer, dims), out_shape=[jax.ShapeDtypeStruct(shap...  245 us
    unnamed x44, local copies, waits for them, and re-layouts  12.3 us

profile of v2, /device:TPU:0, one launch (start us, length us, event | category | flops | bytes accessed | tf_op | source)
XLA Modules:
  0.0 263.6 jit_solution(11679590579319605439)
XLA Ops:
  0.7 0.0 copy-start.16
  0.7 0.6 copy-done.16
  1.3 0.2 reduce-window.7
  1.5 0.1 convert_reduce_fusion
  1.6 0.1 slice.50
  1.7 0.1 compare_reduce_fusion
  1.8 0.0 copy-start.12
  1.8 0.6 copy-done.11
  2.4 0.0 copy-done.12
  2.4 0.1 compare_bitcast_fusion
  2.6 0.0 copy-start.13
  2.6 0.0 copy-start.14
  2.6 0.0 copy-start.15
  2.6 0.6 copy-done.10
  3.2 0.0 copy-done.13
  3.2 0.0 copy-done.14
  3.2 0.0 copy-done.15
  3.3 0.3 dynamic_update_slice.6
  3.6 0.3 copy-done.9
  4.0 0.6 pad_maximum_fusion.1.refs_3_
  4.6 0.3 dynamic_update_slice.7
  4.9 0.6 pad_maximum_fusion.refs_2_
  5.5 245.0 %griffin_layer.1 = (bf16[128,1024]{1,0:T(8,128)(2,1)}, f32[128,1024]{1,0:T(8,128)}, f32[32,1536]{1,0:T(8,128)}, f32[32,1536]{1,0:T(8,128)}, f32[48,1536]{1,0:T(8...) custom-call(bf16[128,1024]{1,0:T(8,128)(2,1)} %bitcast.51, ...), custom_call_target="tpu_custom_call" | custom-call | flops 14495514624 | bytes 8388608 | tf_op jit(solution)/shard_map/griffin_layer/pallas_call | solution.py:1253
  250.5 0.0 copy-start
  250.5 0.8 constant_dynamic-slice_fusion
  251.3 0.5 slice_bitcast_fusion.1
  251.9 0.6 slice_bitcast_fusion
  252.4 0.7 constant_dynamic-slice_fusion.1
  253.2 0.5 slice_bitcast_fusion.4
  253.7 1.7 copy.46
  255.4 0.0 copy-done
  255.4 0.8 copy.47
  256.2 0.3 copy-done.8
  256.5 0.7 copy.48
  257.2 0.0 copy-done.7
  257.2 0.7 copy.49
  257.8 0.0 copy-done.5
  257.8 0.7 copy.50
  258.6 0.4 copy-done.4
  258.9 0.7 copy.51
  259.6 0.3 copy-done.6
  259.9 0.7 copy.52
  260.6 0.0 copy-done.3
  260.6 0.7 copy.53
  261.4 0.4 copy-done.2
  261.8 0.7 copy.54
  262.5 0.4 copy-done.1
  262.9 0.7 copy.55
  (22 shorter events, 0.1 us)
Async XLA Ops:
  0.7 0.7 copy-start.16
  1.8 0.7 copy-start.11
  1.8 0.7 copy-start.12
  2.6 0.7 copy-start.10
  2.6 0.7 copy-start.13
  2.6 0.7 copy-start.14
  2.6 0.7 copy-start.15
  3.3 0.7 copy-start.9
  250.5 4.9 %copy-start = (f32[128,1024]{1,0:T(8,128)S(1)}, f32[128,1024]{1,0:T(8,128)}, u32[]{:S(2)}) copy-start(f32[128,1024]{1,0:T(8,128)} %get-tuple-element.29) | copy-start | bytes 1572868
  255.4 1.1 copy-start.8
  255.4 1.8 copy-start.7
  256.5 1.4 copy-start.5
  257.8 1.1 copy-start.4
  258.9 1.0 copy-start.6
  258.9 1.7 copy-start.3
  260.6 1.1 copy-start.2
  261.8 1.1 copy-start.1

commit v3 on v2

--- a/solution.py
+++ b/solution.py
@@ -16,7 +16,8 @@
 RING = 4
 PLANE = 4
 SHARES = RING * 2 * PLANE
-SEMS = 640
+SENDS = 72
+RECEIVES = 181
 
 eps_norm = 1e-06
 floor_gap = 1e-05
@@ -90,13 +91,14 @@
         first = next(count)
         for _ in range(n - 1):
             next(count)
-        assert first + n <= SEMS
+        assert first + n <= dims.receives
         return first
 
+    spare = list(range(SENDS))
     sent = []
 
     def push(src, dst, dev, rsem, pred=None):
-        i = new()
+        i = spare.pop(0)
 
         def make():
             return pltpu.make_async_remote_copy(
@@ -107,18 +109,19 @@
             make().start()
         else:
             pl.when(pred)(lambda: make().start())
-        entry = (make, pred)
+        entry = (make, pred, i)
         sent.append(entry)
         return entry
 
     def settle(*entries):
         for entry in entries:
-            make, pred = entry
+            make, pred, i = entry
             if pred is None:
                 make().wait_send()
             else:
                 pl.when(pred)(lambda make=make: make().wait_send())
             sent.remove(entry)
+            spare.append(i)
 
     def arrived(dst, rsem, pred=None):
         def wait():
@@ -134,7 +137,15 @@
     def keep_local(src, dst, rsem):
         pltpu.make_async_copy(src, dst, r.rs.at[rsem]).start()
 
-    new()
+    def local_wait(src, dst, rsem):
+        pltpu.make_async_copy(src, dst, r.rs.at[rsem]).wait()
+
+    results = []
+
+    def deliver(src, dst):
+        sem = new()
+        keep_local(src, dst, sem)
+        results.append((src, dst, sem))
 
     def ds(start, size, unit):
         return pl.ds(pl.multiple_of(start, unit), size)
@@ -143,7 +154,7 @@
         def __init__(self, buf):
             self.buf, half = buf, buf.shape[1] // 2
             self.h0, self.h1 = pl.ds(0, half), pl.ds(half, half)
-            self.rx0, self.rx1, self.ry0, self.ry1, self.rd0, self.rd1 = (new() for _ in range(6))
+            self.rx0, self.rx1, self.ry0, self.ry1, self.rd = (new() for _ in range(5))
             self.out = []
 
         def start(self):
@@ -158,9 +169,9 @@
             b = self.buf
             got0, got1 = b.at[px, self.h0], b.at[py, self.h1]
             arrived(got0, self.rx0)
-            self.out.append(push(got0, got0, to_y, self.rd0))
+            self.out.append(push(got0, got0, to_y, self.rd))
             arrived(got1, self.ry1)
-            self.out.append(push(got1, got1, to_x, self.rd1))
+            self.out.append(push(got1, got1, to_x, self.rd))
 
         def wait_x(self):
             arrived(self.buf.at[px, self.h1], self.rx1)
@@ -169,8 +180,7 @@
             arrived(self.buf.at[py, self.h0], self.ry0)
 
         def wait_d(self):
-            arrived(self.buf.at[pd, self.h0], self.rd0)
-            arrived(self.buf.at[pd, self.h1], self.rd1)
+            arrived(self.buf.at[pd], self.rd)
 
         def end(self):
             self.wait_x()
@@ -183,7 +193,7 @@
             self.buf, self.recv = buf, recv
             self.half = buf.shape[1] // 2
             self.h0, self.h1 = pl.ds(0, self.half), pl.ds(self.half, self.half)
-            self.sems = [new() for _ in range(6)]
+            self.sems = [new(), new(), *[new()] * 4]
             self.out = []
 
         def start(self):
@@ -213,8 +223,7 @@
             self.out.append(push(b.at[px, self.h1], v.at[5], to_x, s[5]))
 
         def end(self):
-            for k in (2, 3, 4, 5):
-                arrived(self.recv.at[k], self.sems[k])
+            arrived(self.recv.at[pl.ds(2, 4)], self.sems[2])
             settle(*self.out)
 
         def total(self, half, o, step):
@@ -229,7 +238,7 @@
 
     def z_send(src, block, rz):
         out = []
-        for s in (1, 2):
+        for s in (2, 1):
             out.append(push(src, block(zh), {"zh": zh + s}, rz + zh, zh + s < RING))
             out.append(push(src, block(zh), {"zh": zh - s}, rz + zh, zh - s >= 0))
         return out
@@ -331,27 +340,42 @@
     class Rows:
         def __init__(self, src, w, stage, R):
             self.src, self.w, self.stage, self.R = src, w, stage, R
-            self.rl, self.rz, self.rp, self.rc = new(), new(4), new(), new()
+            self.rz, self.rp, self.rc = new(4), new(), new()
             self.out = []
 
         def block(self, z):
             return self.stage.at[z]
 
         def z_send(self):
-            keep_local(self.src, self.block(zh), self.rl)
             self.out += z_send(self.src, self.block, self.rz)
 
         def z_forward(self):
             self.out += z_forward(self.block, self.rz)
 
-        def z_wait(self):
+        def hand(self, src, k, pred):
             R = self.R
-            pltpu.make_async_copy(self.src, self.block(zh), r.rs.at[self.rl]).wait()
-            z_wait(self.block, self.rz)
             dst = self.w.at[ds((c * PLANE + p) * R, R, 16)]
-            for k, dev in plane_peers:
-                self.out.append(push(self.stage.at[k], dst, dev, self.rp))
-            keep_local(self.stage.at[p], dst, self.rp)
+            self.out.append(push(src, dst, {"yl": k // 2, "xl": k % 2}, self.rp, pred & (k != p)))
+            pl.when(pred & (k == p))(lambda: keep_local(src, dst, self.rp))
+
+        def hand_from(self, k, pred, waited=False):
+            if not waited:
+                arrived(self.block(k), self.rz + k, pred)
+            self.hand(self.block(k), k, pred)
+
+        def near(self):
+            self.hand(self.src, zh, zh >= 0)
+            self.hand_from(zh - 1, zh >= 1)
+            self.hand_from(zh + 1, zh <= RING - 2)
+
+        def far(self):
+            last = RING - 1
+            self.hand_from(zh - 2, (zh >= 2) & (zh != last - 1))
+            self.hand_from(zh - 2, zh == last - 1, True)
+            self.hand_from(zh + 2, (zh <= last - 2) & (zh != 1))
+            self.hand_from(zh + 2, zh == 1, True)
+            self.hand_from(0, zh == last)
+            self.hand_from(last, zh == 0)
 
         def plane_wait(self):
             H = PLANE * self.R
@@ -365,9 +389,9 @@
             settle(*self.out)
 
     class ColumnsGrad:
-        def __init__(self, g, other, slots, land, R, lane0, lanes, outs):
+        def __init__(self, g, other, slots, land, R, lane0, lanes, result):
             self.g, self.other, self.slots, self.land = g, other, slots, land
-            self.R, self.lanes, self.outs = R, pl.ds(lane0, lanes), outs
+            self.R, self.lanes, self.result = R, pl.ds(lane0, lanes), result
             self.rc, self.rl = new(), new()
             self.zsum = ZSum(
                 lambda z: g.at[z, c, :, self.lanes], lambda k: slots.at[k, :, self.lanes], self.add_slot
@@ -421,13 +445,12 @@
         def end(self):
             arrived(self.land.at[:, :, self.lanes], self.rl)
             settle(*self.out)
-            for lane0, C, out in self.outs:
-                for k in range(PLANE):
-                    out[:, k * C : (k + 1) * C] = self.land[k, :, lane0 : lane0 + C].astype(f32)
+            deliver(self.land.at[:, :, self.lanes], self.result.at[:, :, self.lanes])
 
     class RowsGrad:
-        def __init__(self, g, other, stage, slots, R, out):
-            self.g, self.other, self.stage, self.slots, self.R, self.result = g, other, stage, slots, R, out
+        def __init__(self, g, other, stage, slots, R, total, result):
+            self.g, self.other, self.stage, self.slots, self.R = g, other, stage, slots, R
+            self.sum, self.result = total, result
             self.rc, self.rl = new(), new()
             self.zsum = ZSum(lambda z: stage.at[z], lambda k: slots.at[k], self.add_slot)
 
@@ -471,35 +494,52 @@
 
             def add(o):
                 s = pl.ds(o, 16)
-                self.result[s] = self.zsum.total(self.stage[zh, s].astype(f32), [self.slots[k, s] for k in range(4)])
+                self.sum[s] = self.zsum.total(self.stage[zh, s].astype(f32), [self.slots[k, s] for k in range(4)])
 
             loop(self.R, 16, add)
+            deliver(self.sum, self.result)
 
     class Carry:
-        def __init__(self, buf, later):
-            self.buf, self.later = buf, later
-            self.sems = new(places)
+        def __init__(self, own, sib, buf, later):
+            self.own, self.sib, self.buf, self.later = own, sib, buf, later
+            self.rc, self.rz = new(), new(RING * NL)
             self.out = []
 
+        def order(self):
+            return range(RING * NL) if self.later else reversed(range(RING * NL))
+
+        def send_core(self):
+            self.out.append(push(self.own, self.sib, to_core, self.rc))
+
         def send(self):
-            own = self.buf.at[pos]
-            order = range(places) if self.later else reversed(range(places))
-            for at in order:
-                pred = (pos < at) if self.later else (pos > at)
-                self.out.append(push(own, own, place(at), self.sems + pos, pred))
+            arrived(self.sib, self.rc)
+            own, sib = self.own[...], self.sib[...]
+            near = (c == 0) if self.later else (c == 1)
+            head, tail = jnp.where(near, own, sib), jnp.where(near, sib, own)
+            self.buf[flat_z, 0:PLANE] = tail[0:PLANE] * head[0:PLANE]
+            self.buf[flat_z, PLANE : 2 * PLANE] = (
+                tail[0:PLANE] * head[PLANE : 2 * PLANE] + tail[PLANE : 2 * PLANE]
+            )
+            part = self.buf.at[flat_z]
+            for at in self.order():
+                pred = (flat_z < at) if self.later else (flat_z > at)
+                self.out.append(push(part, part, {"zh": at // NL, "zl": at % NL}, self.rz + flat_z, pred))
 
         def fold(self, into):
             into[...] = jnp.zeros_like(into)
-            order = range(places) if self.later else reversed(range(places))
-            for at in order:
-                pred = (pos > at) if self.later else (pos < at)
-
-                def take(at=at):
-                    arrived(self.buf.at[at], self.sems + at)
-                    part = self.buf[at]
-                    into[0:PLANE] = part[0:PLANE] * into[0:PLANE] + part[PLANE : 2 * PLANE]
-
-                pl.when(pred)(take)
+
+            def take(part):
+                into[0:PLANE] = part[0:PLANE] * into[0:PLANE] + part[PLANE : 2 * PLANE]
+
+            for at in self.order():
+                pred = (flat_z > at) if self.later else (flat_z < at)
+
+                def chip(at=at):
+                    arrived(self.buf.at[at], self.rz + at)
+                    take(self.buf[at])
+
+                pl.when(pred)(chip)
+            pl.when((c == 1) if self.later else (c == 0))(lambda: take(self.sib[...]))
             settle(*self.out)
 
     GL = PLANE * RD
@@ -511,48 +551,69 @@
 
     class Small:
         def __init__(self):
-            self.rk, self.rc, self.rg, self.ra = new(), new(), new(2 * RING), new(2)
+            self.rr, self.rk = new(), new()
             self.out = []
 
         def one(self):
-            row = r.pack.at[:, pl.ds(0, GL + T)]
+            for at in range(2 * RING):
+                self.out.append(push(r.pack, r.pr.at[ring], ring_place(at), self.rr, ring != at))
+            keep_local(r.pack, r.pr.at[ring], self.rr)
+
+        def two(self):
+            arrived(r.pr, self.rr)
             for _, dev in plane_peers:
-                self.out.append(push(row, r.pk.at[p], dev, self.rk))
-            keep_local(row, r.pk.at[p], self.rk)
-            chan = r.pack.at[:, pl.ds(GL + T, CW)]
-            self.out.append(push(chan, r.pc.at[p], home, self.rc, p != zh))
-            pl.when(p == zh)(lambda: keep_local(chan, r.pc.at[p], self.rc))
-
-        def two(self):
-            arrived(r.pk, self.rk)
-            r.g_all[ring] = (r.pk[0, :, 0:GL] + r.pk[1, :, 0:GL]) + (r.pk[2, :, 0:GL] + r.pk[3, :, 0:GL])
-
-            def chan():
-                arrived(r.pc, self.rc)
-                r.c_all[c] = (r.pc[0] + r.pc[1]) + (r.pc[2] + r.pc[3])
-
-            pl.when(p == zh)(chan)
+                self.out.append(push(r.pr, r.pp.at[p], dev, self.rk))
+            keep_local(r.pr, r.pp.at[p], self.rk)
+
+        def three(self):
+            arrived(r.pp, self.rk)
+            from_row = lax.broadcasted_iota(jnp.int32, (128, GL), 0)
+            to_lane = lax.broadcasted_iota(jnp.int32, (128, GL), 1)
+            whole = jnp.zeros((2 * RING * 16, GL), f32)
+            for k in range(PLANE):
+                move = ((to_lane == from_row + k * RD) & (from_row < RD)).astype(bf16)
+                whole = whole + dot(r.pp[k].reshape(2 * RING * 16, 128), move)
             for at in range(2 * RING):
-                own = r.g_all.at[ring]
-                self.out.append(push(own, own, ring_place(at), self.rg + ring, ring != at))
-            for at in range(2 * RING):
-                own = r.c_all.at[c]
-                self.out.append(push(own, own, ring_place(at), self.ra + c, (p == zh) & (ring != at)))
-
-        def three(self):
-            for at in range(2 * RING):
-                arrived(r.g_all.at[at], self.rg + at, ring != at)
-            for at in range(2):
-                arrived(r.c_all.at[at], self.ra + at, (p != zh) | (c != at))
-            for at in range(2 * RING):
-                r.gains[:, at * GL : (at + 1) * GL] = r.g_all[at]
-            r.chan[...] = r.c_all[0] + r.c_all[1]
-            r.chan[7:8] = r.scale[pl.ds(p, 1)]
-            lane = lax.broadcasted_iota(jnp.int32, (8, 128), 0)
+                r.gains[0:2, at * GL : (at + 1) * GL] = whole[at * 16 : at * 16 + 2]
+            from_row = lax.broadcasted_iota(jnp.int32, (128, CW), 0)
+            to_lane = lax.broadcasted_iota(jnp.int32, (128, CW), 1)
+            whole = jnp.zeros((16, CW), f32)
             for k in range(PLANE):
-                rows = r.pk[k, :, GL : GL + T]
-                for j in range(7):
-                    r.masks[j, k * T : (k + 1) * T] = dot_tn(rows, (lane == j).astype(f32))
+                for cc in (0, 1):
+                    move = ((to_lane == from_row + (cc * PLANE + k) * RW) & (from_row < RW)).astype(bf16)
+                    whole = whole + dot(r.pp[k, 2 * p + cc], move)
+            r.chan[...] = whole[2:10]
+            rate = r.pack[...].astype(f32)
+            for k in range(CW // 128):
+                r.chan[7:8, k * 128 : (k + 1) * 128] = jnp.exp2(-rate[11 + k : 12 + k])
+
+        def four(self):
+            where = lax.broadcasted_iota(jnp.int32, (T, 128), 0).astype(f32) + (pos * T).astype(f32)
+            for k in range(PLANE):
+                part = r.pp[k, 0].astype(f32)
+                starts, ends = [], []
+                total = jnp.zeros((1, 1), f32)
+                for j in range(dims.SEGS):
+                    starts.append(total)
+                    total = total + part[9:10, j : j + 1] * 256.0 + part[10:11, j : j + 1]
+                    ends.append(total)
+
+                def seg(shift):
+                    at = where + float(shift)
+                    value = jnp.zeros((T, 128), f32)
+                    for end in ends:
+                        value = value + jnp.where(at >= end, 1.0, 0.0)
+                    return jnp.where((at < 0.0) | (at >= float(T * places)), -1.0, value)
+
+                here = seg(0)
+                rows = pl.ds(k * T, T)
+                first = jnp.zeros((T, 128), f32)
+                for start in starts:
+                    first = jnp.where(where == start, 1.0, first)
+                r.masks[0, rows] = first
+                for j in (1, 2, 3):
+                    r.masks[j, rows] = jnp.where(seg(-j) == here, 1.0, 0.0)
+                    r.masks[3 + j, rows] = jnp.where(seg(j) == here, 1.0, 0.0)
             settle(*self.out)
 
     class SmallGrad:
@@ -575,11 +636,11 @@
                 value = r.gc[0]
                 for at in range(1, 2 * RING):
                     value = value + r.gc[at]
-                r.chan_out[...] = value
+                r.chan_sum[...] = value
 
             pl.when(p == zh)(total)
             for _, dev in plane_peers:
-                self.out.append(push(r.chan_out, r.chan_out, dev, self.ro, p == zh))
+                self.out.append(push(r.chan_sum, r.chan_sum, dev, self.ro, p == zh))
 
         def gain_one(self):
             for at in range(2 * RING):
@@ -600,8 +661,17 @@
         def end(self):
             for k, _ in plane_peers:
                 arrived(r.gp.at[k], self.rp + k)
-            r.gain_out[...] = (r.gp[0] + r.gp[1]) + (r.gp[2] + r.gp[3])
-            arrived(r.chan_out, self.ro, p != zh)
+            gains = (r.gp[0] + r.gp[1]) + (r.gp[2] + r.gp[3])
+            from_lane = lax.broadcasted_iota(jnp.int32, (GL, 128), 0)
+            to_lane = lax.broadcasted_iota(jnp.int32, (GL, 128), 1)
+            move = (from_lane == to_lane + p * RD).astype(f32)
+            r.small_sum[0:8] = jnp.dot(gains, move, precision=lax.Precision.HIGHEST)
+            arrived(r.chan_sum, self.ro, p != zh)
+            from_lane = lax.broadcasted_iota(jnp.int32, (CW, 128), 0)
+            to_lane = lax.broadcasted_iota(jnp.int32, (CW, 128), 1)
+            move = (from_lane == to_lane + (c * PLANE + p) * RW).astype(f32)
+            r.small_sum[8:16] = jnp.dot(r.chan_sum[...], move, precision=lax.Precision.HIGHEST)
+            deliver(r.small_sum, r.small_out)
             settle(*self.out)
 
     barrier = pltpu.get_barrier_semaphore()
@@ -613,7 +683,16 @@
         def _(at=at):
             pl.semaphore_signal(barrier, 1, device_id=place(at), device_id_type=MESH)
 
-    pl.semaphore_wait(barrier, len(plane_peers) + places - 1)
+    first_loads = [
+        (src, dst, new())
+        for src, dst in (
+            (r.pack_in, r.pack),
+            (r.tokens, r.x_all.at[p]),
+            (r.cotangent, r.cot_all.at[p]),
+        )
+    ]
+    for load in first_loads:
+        keep_local(*load)
 
     w_i, w_b = Column(r.input_weight, r.w_ib, RD, CW, 0), Column(r.branch_weight, r.w_ib, RD, CW, CW)
     w_d, w_j = Column(r.decay_weight, r.w_di, RW, CW, 0), Column(r.inject_weight, r.w_di, RW, CW, CW)
@@ -628,18 +707,18 @@
     step = 256
     chunk = PLANE * RD * 2
 
+    pl.semaphore_wait(barrier, len(plane_peers) + places - 1)
+    local_wait(*first_loads[0])
     small.one()
+    w_i.spread()
+    local_wait(*first_loads[1])
+    ag_x.start()
     halo_x = new()
-    sent_x = push(r.tokens.at[pl.ds(T - 16, 16)], r.x_halo.at[p], to_next, halo_x, pos < places - 1)
-    w_i.spread()
+    sent_x = push(r.x_all.at[p, pl.ds(T - 16, 16)], r.x_halo.at[p], to_next, halo_x, pos < places - 1)
     w_o.z_send()
-    r.x_all[p] = r.tokens[...]
-    r.cot_all[p] = r.cotangent[...]
-    ag_x.start()
+    small.two()
+    w_i.z_send()
     w_d.spread()
-    w_j.spread()
-    w_i.z_send()
-    small.two()
 
     @pl.when(pos == 0)
     def _():
@@ -649,7 +728,9 @@
     halo_p = new(PLANE)
     sent_p = [push(r.x_halo.at[p], r.x_halo.at[p], dev, halo_p + p) for _, dev in plane_peers]
     ag_x.mid()
+    w_j.spread()
     w_b.spread()
+    local_wait(*first_loads[2])
     small.three()
 
     def norm_block(k):
@@ -661,12 +742,14 @@
         loop(T, 32, norm_one)
 
     norm_block(p)
+    w_o.z_forward()
     w_d.z_send()
-    w_o.z_forward()
     ag_x.wait_x()
     norm_block(px)
     ag_x.wait_y()
     norm_block(py)
+    w_i.z_forward()
+    small.four()
     for k, _ in plane_peers:
         arrived(r.x_halo.at[k], halo_p + k)
     v = r.x_halo[...].reshape(PLANE * 16, D).astype(f32)
@@ -674,12 +757,8 @@
     ag_x.wait_d()
     norm_block(pd)
     settle(*ag_x.out, sent_x, *sent_p)
+    w_i.z_wait()
     w_g.spread()
-    w_u.spread()
-    w_i.z_forward()
-    w_i.z_wait()
-    w_o.z_wait()
-    w_j.z_send()
     w_i.end()
 
     def weight_ib(lanes):
@@ -706,25 +785,31 @@
 
     loop(T, 16, convolve)
     ag_conv.start()
-    w_o.plane_wait()
     w_d.z_forward()
+    w_j.z_send()
+    ag_conv.mid()
     w_d.z_wait()
     w_b.z_send()
-    ag_conv.mid()
     w_d.end()
 
     def pre(q, lanes):
         return dot(r.conv[q], r.w_di[q, :, :, lanes].reshape(W // RING, CW))
 
     r.pair[:, 0:CW] = pre(p, lanes_a)
-    for q, wait in ((px, ag_conv.wait_x), (py, ag_conv.wait_y), (pd, ag_conv.wait_d)):
-        wait()
-        r.pair[:, 0:CW] += pre(q, lanes_a)
+    ag_conv.wait_x()
+    r.pair[:, 0:CW] += pre(px, lanes_a)
+    ag_conv.wait_y()
+    r.pair[:, 0:CW] += pre(py, lanes_a)
+    w_j.z_forward()
+    w_g.z_send()
+    ag_conv.wait_d()
+    r.pair[:, 0:CW] += pre(pd, lanes_a)
     settle(*ag_conv.out)
+    w_u.spread()
+    w_o.near()
+    w_o.far()
+    w_j.z_wait()
     ag_cot.start()
-    w_j.z_forward()
-    w_j.z_wait()
-    w_g.z_send()
     w_j.end()
     r.pair[:, CW : 2 * CW] = pre(0, lanes_b)
     for q in range(1, PLANE):
@@ -765,15 +850,16 @@
 
     zero, one = jnp.zeros((1, CW), f32), jnp.ones((1, CW), f32)
     ends = lax.fori_loop(0, T // 8, scan_forward, (zero, one) * PLANE)
-    carry_f = Carry(r.carry_f, True)
+    carry_f = Carry(r.own_f, r.sib_f, r.carry_f, True)
     for k in range(PLANE):
-        r.carry_f[pos, k : k + 1] = ends[2 * k + 1]
-        r.carry_f[pos, PLANE + k : PLANE + k + 1] = ends[2 * k]
-        r.ends[k : k + 1] = ends[2 * k + 1]
-    carry_f.send()
-    ag_cot.mid()
+        r.own_f[k : k + 1] = ends[2 * k + 1]
+        r.own_f[PLANE + k : PLANE + k + 1] = ends[2 * k]
+    carry_f.send_core()
     w_b.z_forward()
     w_b.z_wait()
+    carry_f.send()
+    w_o.plane_wait()
+    ag_cot.mid()
     w_b.end()
     r.work[...] = dot(r.n_one[...].reshape(M, D), weight_ib(lanes_b))
 
@@ -803,15 +889,15 @@
     loop(D, step, out_part)
     rs_one = Scatter(r.part, r.got_one)
     rs_one.start()
+    w_g.z_forward()
     w_u.z_send()
     ag_cot.end()
     rs_one.mid()
-    w_g.z_forward()
     rs_one.end()
 
     def norm_two(o, summed):
         s = pl.ds(o, 16)
-        v = r.tokens[s].astype(f32) + summed
+        v = r.x_all[p, s].astype(f32) + summed
         r.x_one[s] = v
         r.n_two[p, s] = (v * inverse_rms(v) * r.gains[1:2]).astype(bf16)
 
@@ -820,8 +906,8 @@
     w_g.z_wait()
     w_dn.z_send()
     ag_two.mid()
+    w_u.z_forward()
     w_g.end()
-    w_u.z_forward()
     ag_two.end()
 
     def mlp_in(o):
@@ -842,19 +928,19 @@
         r.pair[s, CF : 2 * CF] = value
 
     loop(M, 16, gates_mlp)
+    w_dn.near()
 
     def grad_down(o):
         q = pl.ds(o, step)
         r.g_dn[q] = dot_tn(r.hidden[:, q], r.cot_all[...].reshape(M, D)).astype(bf16)
 
     loop(CF, step, grad_down)
-    g_dn = RowsGrad(r.g_dn, r.h_dn, r.sg_dn, r.z_dn, RF, r.grad_mlp_down)
+    g_dn = RowsGrad(r.g_dn, r.h_dn, r.sg_dn, r.z_dn, RF, r.t_dn, r.grad_mlp_down)
     g_dn.core_send()
     w_dn.z_forward()
+    w_dn.far()
+    w_dn.plane_wait()
     g_dn.plane_send()
-    w_dn.z_wait()
-    g_dn.z_send()
-    w_dn.plane_wait()
     w_dn.end()
 
     for k in range(CF // step):
@@ -888,13 +974,13 @@
         lax.fori_loop(0, RING, run, 0)
 
     grad_gate_up(0)
-    g_g = ColumnsGrad(r.w_gu, r.h_gu, r.z_gu, r.l_gu, RD, 0, CF, ((0, CF, r.grad_mlp_gate),))
+    g_g = ColumnsGrad(r.w_gu, r.h_gu, r.z_gu, r.l_gu, RD, 0, CF, r.grads_gu)
     g_g.core_send()
     rs_two.mid()
     grad_gate_up(CF)
-    g_u = ColumnsGrad(r.w_gu, r.h_gu, r.z_gu, r.l_gu, RD, CF, CF, ((CF, CF, r.grad_mlp_up),))
+    g_u = ColumnsGrad(r.w_gu, r.h_gu, r.z_gu, r.l_gu, RD, CF, CF, r.grads_gu)
     g_u.core_send()
-    g_dn.z_forward()
+    g_dn.z_send()
     g_g.z_send()
 
     def act_part(o):
@@ -913,16 +999,15 @@
         z = v * rs
         dz = d_two * r.gains[1:2]
         r.ggain[1:2] += jnp.sum(d_two * z, axis=0, keepdims=True)
-        d_one = r.cotangent[s].astype(f32) + rs * (dz - z * jnp.mean(dz * z, axis=-1, keepdims=True))
+        d_one = r.cot_all[p, s].astype(f32) + rs * (dz - z * jnp.mean(dz * z, axis=-1, keepdims=True))
         r.d_one[s] = d_one
         r.d_out[p, s] = d_one.astype(bf16)
 
     rs_two.each(16, norm_two_back)
     ag_out.start()
-    g_dn.end()
     g_u.z_send()
     ag_out.mid()
-    g_g.z_forward()
+    g_dn.z_forward()
     ag_out.end()
     rs_act = Scatter(r.part_act, r.got_act)
     rs_act.start()
@@ -955,19 +1040,20 @@
         return tuple(out)
 
     heads = lax.fori_loop(0, T // 8, scan_backward, (zero, one, one) * PLANE)
-    carry_b = Carry(r.carry_b, False)
+    carry_b = Carry(r.own_b, r.sib_b, r.carry_b, False)
     for k in range(PLANE):
-        r.carry_b[pos, k : k + 1] = r.ends[k : k + 1]
-        r.carry_b[pos, PLANE + k : PLANE + k + 1] = heads[3 * k] * heads[3 * k + 2]
-    carry_b.send()
+        r.own_b[k : k + 1] = r.own_f[k : k + 1]
+        r.own_b[PLANE + k : PLANE + k + 1] = heads[3 * k] * heads[3 * k + 2]
+    carry_b.send_core()
 
     def grad_out(o):
         q = pl.ds(o, 128)
         r.w_o[q] = dot_tn(r.mixed[:, q], r.d_out[...].reshape(M, D)).astype(bf16)
 
     loop(CW, 128, grad_out)
-    g_o = RowsGrad(r.w_o, r.h_o, r.sg_o, r.z_o, RW, r.grad_output_weight)
+    g_o = RowsGrad(r.w_o, r.h_o, r.sg_o, r.z_o, RW, r.t_o, r.grad_output_weight)
     g_o.core_send()
+    carry_b.send()
     rs_act.mid()
 
     def d_branch_part(z, _):
@@ -982,9 +1068,11 @@
         return 0
 
     lax.fori_loop(0, RING, d_branch_part, 0)
-    g_b = ColumnsGrad(r.w_ib, r.h_ib, r.z_ib, r.l_ib, RD, CW, CW, ((CW, CW, r.grad_branch_weight),))
+    g_b = ColumnsGrad(r.w_ib, r.h_ib, r.z_ib, r.l_ib, RD, CW, CW, r.grads_ib)
     g_b.core_send()
-    g_g.plane_send()
+    g_o.plane_send()
+    g_b.z_send()
+    g_g.z_forward()
     carry_b.fold(r.into)
 
     def back(o):
@@ -1020,11 +1108,13 @@
 
     def finish_act(o, summed):
         s = pl.ds(o, 16)
-        r.activations[s] = (r.x_one[s] + summed).astype(bf16)
+        r.act[s] = (r.x_one[s] + summed).astype(bf16)
 
     rs_act.each(16, finish_act)
+    deliver(r.act, r.activations)
+    g_o.z_send()
     g_u.z_forward()
-    g_b.z_send()
+    g_dn.end()
 
     def grad_dec_inj(lanes):
         def run(q, _):
@@ -1035,17 +1125,15 @@
         lax.fori_loop(0, RING, run, 0)
 
     grad_dec_inj(lanes_a)
-    g_d = ColumnsGrad(r.w_di, r.h_di, r.z_di, r.l_di, RW, 0, CW, ((0, CW, r.grad_decay_weight),))
+    g_d = ColumnsGrad(r.w_di, r.h_di, r.z_di, r.l_di, RW, 0, CW, r.grads_di)
     g_d.core_send()
-    g_o.plane_send()
     rs_conv.mid()
     grad_dec_inj(lanes_b)
-    g_j = ColumnsGrad(r.w_di, r.h_di, r.z_di, r.l_di, RW, CW, CW, ((CW, CW, r.grad_inject_weight),))
+    g_j = ColumnsGrad(r.w_di, r.h_di, r.z_di, r.l_di, RW, CW, CW, r.grads_di)
     g_j.core_send()
-    g_u.plane_send()
-    g_o.z_send()
+    g_d.z_send()
     g_b.z_forward()
-    g_d.z_send()
+    g_g.plane_send()
     rs_conv.end()
 
     for half in (0, 1):
@@ -1057,7 +1145,10 @@
 
         loop(T, 16, add_conv)
     halo_b = new()
-    sent_b = push(r.d_conv.at[:, pl.ds(0, 8)], r.d_conv.at[:, pl.ds(T, 8)], to_prev, halo_b, pos > 0)
+    for k in range(PLANE):
+        r.halo_out[4 * k : 4 * k + 4] = r.d_conv[k, 0:4]
+    sent_b = push(r.halo_out, r.halo_in, to_prev, halo_b, pos > 0)
+    g_j.z_send()
 
     def taps_back(o):
         sums = [jnp.zeros((1, CW), f32)] * 5
@@ -1078,10 +1169,11 @@
 
     @pl.when(pos == places - 1)
     def _():
-        r.d_conv[:, T : T + 8] = jnp.zeros((PLANE, 8, CW), f32)
-
-    arrived(r.d_conv.at[:, pl.ds(T, 8)], halo_b, pos < places - 1)
-    settle(sent_b)
+        r.halo_in[...] = jnp.zeros((16, CW), f32)
+
+    arrived(r.halo_in, halo_b, pos < places - 1)
+    for k in range(PLANE):
+        r.d_conv[k, T : T + 8] = jnp.concatenate([r.halo_in[4 * k : 4 * k + 4], jnp.zeros((4, CW), f32)], axis=0)
 
     def conv_back(o):
         for k in range(PLANE):
@@ -1111,34 +1203,36 @@
         return 0
 
     lax.fori_loop(0, RING, grad_input, 0)
-    g_i = ColumnsGrad(r.w_ib, r.h_ib, r.z_ib, r.l_ib, RD, 0, CW, ((0, CW, r.grad_input_weight),))
+    g_i = ColumnsGrad(r.w_ib, r.h_ib, r.z_ib, r.l_ib, RD, 0, CW, r.grads_ib)
     g_i.core_send()
+    rs_three.mid()
     g_o.z_forward()
+    g_i.z_send()
+    g_u.plane_send()
+    g_d.z_forward()
     g_b.plane_send()
-    g_d.z_forward()
-    rs_three.mid()
     small_grad.chan_two()
-    g_j.z_send()
-    g_i.z_send()
-    g_o.end()
-    g_g.end()
-    g_u.end()
     rs_three.end()
 
     def norm_one_back(o, d_n):
         s = pl.ds(o, 16)
-        v = r.tokens[s].astype(f32)
+        v = r.x_all[p, s].astype(f32)
         rs = inverse_rms(v)
         z = v * rs
         dz = d_n * r.gains[0:1]
         r.ggain[0:1] += jnp.sum(d_n * z, axis=0, keepdims=True)
-        r.d_tokens[s] = r.d_one[s] + rs * (dz - z * jnp.mean(dz * z, axis=-1, keepdims=True))
+        r.d_x[s] = r.d_one[s] + rs * (dz - z * jnp.mean(dz * z, axis=-1, keepdims=True))
 
     rs_three.each(16, norm_one_back)
+    deliver(r.d_x, r.d_tokens)
     small_grad.gain_one()
-    g_d.plane_send()
+    settle(sent_b)
     g_j.z_forward()
     g_i.z_forward()
+    g_g.end()
+    g_u.end()
+    g_d.plane_send()
+    g_o.end()
     small_grad.gain_two()
     g_b.end()
     g_j.plane_send()
@@ -1148,6 +1242,8 @@
     g_j.end()
     g_i.end()
     assert not sent
+    for result in results:
+        local_wait(*result)
 
 
 WEIGHTS = (
@@ -1162,20 +1258,23 @@
 )
 
 
-def run_layer(NL, tokens, cotangent, pack, scale, weights):
+def run_layer(NL, SEGS, tokens, cotangent, pack, weights):
     T, D = tokens.shape
     W, F = weights["branch_weight"].shape[1], weights["mlp_gate"].shape[1]
     CW, CF = W // PLANE, F // PLANE
     RD, RW, RF = D // SHARES, W // SHARES, F // SHARES
     GL, M, places = PLANE * RD, PLANE * T, RING * NL * 2
-    vmem, hbm = pl.BlockSpec(memory_space=pltpu.VMEM), pl.BlockSpec(memory_space=pl.ANY)
-    ins = ["tokens", "cotangent", "pack", "scale", *WEIGHTS]
+    hbm = pl.BlockSpec(memory_space=pl.ANY)
+    ins = ["tokens", "cotangent", "pack_in", *WEIGHTS]
     outs = {
         "activations": ((T, D), bf16),
         "d_tokens": ((T, D), f32),
-        **{"grad_" + name: (weights[name].shape, f32) for name in WEIGHTS},
-        "gain_out": ((8, GL), f32),
-        "chan_out": ((8, CW), f32),
+        "grads_ib": ((PLANE, RD, 2 * CW), bf16),
+        "grads_di": ((PLANE, RW, 2 * CW), bf16),
+        "grads_gu": ((PLANE, RD, 2 * CF), bf16),
+        "grad_output_weight": ((RW, D), f32),
+        "grad_mlp_down": ((RF, D), f32),
+        "small_out": ((16, 128), f32),
     }
     scratch = {
         "w_ib": ((RING, 2, PLANE * RD, 2 * CW), bf16),
@@ -1225,18 +1324,26 @@
         **{name: ((M, CW), f32) for name in ("gated", "slope", "rgate", "igate", "decay", "work", "cum")},
         "x_one": ((T, D), f32),
         "d_one": ((T, D), f32),
-        "carry_f": ((places, 2 * PLANE, CW), f32),
-        "carry_b": ((places, 2 * PLANE, CW), f32),
+        "carry_f": ((RING * NL, 2 * PLANE, CW), f32),
+        "carry_b": ((RING * NL, 2 * PLANE, CW), f32),
+        **{name: ((2 * PLANE, CW), f32) for name in ("own_f", "sib_f", "own_b", "sib_b")},
+        "halo_out": ((16, CW), f32),
+        "halo_in": ((16, CW), f32),
         "into": ((8, CW), f32),
         "x_all": ((PLANE, T, D), bf16),
         "x_halo": ((PLANE, 16, D), bf16),
         "n_halo": ((PLANE, 16, D), bf16),
         "g_dn": ((CF, D), bf16),
         "masks": ((7, M, 128), f32),
-        "pk": ((PLANE, 8, GL + T), f32),
-        "pc": ((PLANE, 8, CW), f32),
-        "g_all": ((2 * RING, 8, GL), f32),
-        "c_all": ((2, 8, CW), f32),
+        "pack": ((16, 128), bf16),
+        "pr": ((2 * RING, 16, 128), bf16),
+        "pp": ((PLANE, 2 * RING, 16, 128), bf16),
+        "act": ((T, D), bf16),
+        "d_x": ((T, D), f32),
+        "t_o": ((RW, D), f32),
+        "t_dn": ((RF, D), f32),
+        "small_sum": ((16, 128), f32),
+        "chan_sum": ((8, CW), f32),
         "gains": ((8, D), f32),
         "chan": ((8, CW), f32),
         "ggain": ((8, D), f32),
@@ -1244,26 +1351,80 @@
         "gg": ((2 * RING, 8, GL), f32),
         "gp": ((PLANE, 8, GL), f32),
         "gc": ((2 * RING, 8, CW), f32),
-        "ends": ((8, CW), f32),
     }
     dims = SimpleNamespace(
-        T=T, D=D, W=W, F=F, CW=CW, CF=CF, RD=RD, RW=RW, RF=RF, NL=NL, names=[*ins, *outs, *scratch, "ss", "rs"]
+        T=T, D=D, W=W, F=F, CW=CW, CF=CF, RD=RD, RW=RW, RF=RF, NL=NL, SEGS=SEGS, receives=RECEIVES + 2 * RING * NL, names=[*ins, *outs, *scratch, "ss", "rs"]
     )
     flops = 3 * 2 * M * (D * 2 * CW + W * 2 * CW + CW * D + 3 * D * CF)
     results = pl.pallas_call(
         partial(layer, dims),
         out_shape=[jax.ShapeDtypeStruct(shape, kind) for shape, kind in outs.values()],
-        in_specs=[vmem] * 4 + [hbm] * len(WEIGHTS),
-        out_specs=[vmem] * len(outs),
+        in_specs=[hbm] * (3 + len(WEIGHTS)),
+        out_specs=[hbm] * len(outs),
         scratch_shapes=[pltpu.VMEM(shape, kind) for shape, kind in scratch.values()]
-        + [pltpu.SemaphoreType.DMA((SEMS,)), pltpu.SemaphoreType.DMA((SEMS,))],
+        + [pltpu.SemaphoreType.DMA((SENDS,)), pltpu.SemaphoreType.DMA((dims.receives,))],
         compiler_params=pltpu.CompilerParams(
             collective_id=0, has_side_effects=True, vmem_limit_bytes=62 * 2**20
         ),
         cost_estimate=pl.CostEstimate(flops=flops, bytes_accessed=8 * 2**20, transcendentals=M * CW * 16),
         name="griffin_layer",
-    )(tokens, cotangent, pack, scale, *[weights[name] for name in WEIGHTS])
-    return dict(zip(outs, results, strict=True))
+    )(tokens, cotangent, pack, *[weights[name] for name in WEIGHTS])
+    return finish(dict(zip(outs, results, strict=True)), PLANE, CW, CF)
+
+
+def finish(got, blocks, CW, CF):
+    hbm = pl.BlockSpec(memory_space=pl.ANY)
+    pairs = (
+        ("grads_ib", ("grad_input_weight", "grad_branch_weight"), CW),
+        ("grads_di", ("grad_decay_weight", "grad_inject_weight"), CW),
+        ("grads_gu", ("grad_mlp_gate", "grad_mlp_up"), CF),
+    )
+    plain = ("d_tokens", "activations", "grad_output_weight", "grad_mlp_down")
+    names = [*[name for name, _, _ in pairs], *plain]
+    shapes = {name: got[name] for name in plain}
+    for name, outs, C in pairs:
+        for out in outs:
+            shapes[out] = jax.ShapeDtypeStruct((got[name].shape[1], blocks * C), f32)
+    scratch = [pltpu.VMEM(got[name].shape, got[name].dtype) for name in names]
+    scratch += [pltpu.VMEM(shapes[out].shape, f32) for _, outs, _ in pairs for out in outs]
+    count = 2 * len(plain) + 3 * len(pairs)
+
+    def body(*refs):
+        ins = dict(zip(names, refs[: len(names)], strict=True))
+        outs = dict(zip(shapes, refs[len(names) : len(names) + len(shapes)], strict=True))
+        held, sems = refs[len(names) + len(shapes) : -1], refs[-1]
+        copies = []
+
+        def copy(src, dst):
+            copies.append(pltpu.make_async_copy(src, dst, sems.at[len(copies)]))
+            copies[-1].start()
+            return copies[-1]
+
+        loads = [copy(ins[name], held[i]) for i, name in enumerate(names)]
+        stores = []
+        for i, (_, targets, C) in enumerate(pairs):
+            loads[i].wait()
+            for j, target in enumerate(targets):
+                wide = held[len(names) + 2 * i + j]
+                for k in range(blocks):
+                    wide[:, k * C : (k + 1) * C] = held[i][k, :, j * C : (j + 1) * C].astype(f32)
+                stores.append(copy(wide, outs[target]))
+        for i, name in enumerate(plain):
+            loads[len(pairs) + i].wait()
+            stores.append(copy(held[len(pairs) + i], outs[name]))
+        for store in stores:
+            store.wait()
+
+    results = pl.pallas_call(
+        body,
+        out_shape=[jax.ShapeDtypeStruct(like.shape, like.dtype) for like in shapes.values()],
+        in_specs=[hbm] * len(names),
+        out_specs=[hbm] * len(shapes),
+        scratch_shapes=[*scratch, pltpu.SemaphoreType.DMA((count,))],
+        compiler_params=pltpu.CompilerParams(vmem_limit_bytes=62 * 2**20),
+        name="finish",
+    )(*[got[name] for name in names])
+    return {**got, **dict(zip(shapes, results, strict=True))}
 
 
 def local(
@@ -1289,10 +1450,7 @@
 ):
     devices = math.prod(sizes.values())
     width = branch_weight.shape[1]
-    NL = sizes["zl"]
     at = {name: lax.axis_index(name) for name in AXES}
-    T = tokens.shape[1]
-
     mine = at["yl"] * 2 + at["xl"]
     ring = at["zh"] * 2 + at["c"]
     share = ring * PLANE + mine
@@ -1305,31 +1463,17 @@
         size = whole.shape[axis] // SHARES
         return lax.dynamic_slice_in_dim(whole, share * size, size, axis)
 
-    gains = pooled(jnp.stack([first_gain, second_gain]).astype(f32), 1)
-    chan = pooled(jnp.concatenate([conv_taps.T, jnp.stack([conv_bias, decay_bias, inject_bias])]).astype(f32), 1)
+    def rows(value):
+        value = value.astype(bf16)
+        return jnp.pad(value, ((0, 0), (0, 128 - value.shape[1])))
+
+    gains = pooled(jnp.stack([first_gain, second_gain]), 1)
+    chan = pooled(jnp.concatenate([conv_taps.T, jnp.stack([conv_bias, decay_bias, inject_bias])]), 1)
     RD, RW = gains.shape[1], chan.shape[1]
-    gain_pack = lax.dynamic_update_slice(jnp.zeros((8, PLANE * RD), f32), gains, (0, mine * RD))
-    chan_pack = lax.dynamic_update_slice(
-        jnp.zeros((8, 2 * PLANE * RW), f32), chan, (0, (at["c"] * PLANE + mine) * RW)
-    )
-    scale = jnp.exp2(-decay_exponent.astype(f32)).reshape(PLANE, width // PLANE)
-    scale = jnp.concatenate([scale, scale])
-
-    lengths = doc_lengths[0]
-    ends = jnp.cumsum(lengths)
-    starts = ends - lengths
-    index = (at["zh"] * NL + at["zl"]) * 2 + at["c"]
-    count = T * RING * NL * 2
-    where = index * T - 3 + jnp.arange(T + 6, dtype=jnp.int32)
-    seg = jnp.sum((ends[:, None] <= where[None, :]).astype(jnp.int32), axis=0)
-    seg = jnp.where((where < 0) | (where >= count), -1, seg)
-    here = seg[3 : 3 + T]
-    first = jnp.any(starts[:, None] == where[None, 3 : 3 + T], axis=0)
-    masks = [first]
-    masks += [seg[3 - k : 3 - k + T] == here for k in (1, 2, 3)]
-    masks += [seg[3 + k : 3 + k + T] == here for k in (1, 2, 3)]
-    masks = jnp.stack([*masks, first]).astype(f32)
-    pack = jnp.concatenate([gain_pack, masks, chan_pack], axis=1)
+    rates = lax.dynamic_slice_in_dim(decay_exponent, mine * (width // PLANE), width // PLANE).reshape(-1, 128)
+    lengths = jnp.concatenate([doc_lengths // 256, doc_lengths % 256])
+    pack = jnp.concatenate([rows(gains), rows(chan), rows(lengths), rows(rates)])
+    pack = jnp.pad(pack, ((0, 16 - pack.shape[0]), (0, 0)))
 
     weights = dict(
         zip(
@@ -1339,7 +1483,7 @@
         )
     )
     weights = {name: pooled(value) for name, value in weights.items()}
-    got = run_layer(NL, tokens[0], cotangent[0], pack, scale, weights)
+    got = run_layer(sizes["zl"], doc_lengths.shape[1], tokens[0], cotangent[0], pack, weights)
 
     def returned(value, axis=0):
         if groups == 1:
@@ -1351,9 +1495,8 @@
         return lax.psum_scatter(whole, AXES, scatter_dimension=axis, tiled=True).astype(f32)
 
     grads = [returned(got["grad_" + name]) for name in WEIGHTS]
-    gain_sum = returned(lax.dynamic_slice_in_dim(got["gain_out"], mine * RD, RD, 1)[:2], 1)
-    chan_sum = lax.dynamic_slice_in_dim(got["chan_out"], (at["c"] * PLANE + mine) * RW, RW, 1)
-    chan_sum = returned(chan_sum[:7], 1)
+    gain_sum = returned(got["small_out"][:2, :RD], 1)
+    chan_sum = returned(got["small_out"][8:15, :RW], 1)
     return (
         got["activations"][None],
         got["d_tokens"][None],

time: 264 us -> 224 us (0.85)
  Pallas kernels: 245 us -> 218 us
  local copies, waits for them, and re-layouts: 16.2 us -> 3.65 us
    pallas_call x1, Pallas kernels: 245 us -> 215 us  [run_layer(): pl.pallas_call(partial(layer, dims), out_shape=[jax.ShapeDtypeStruct(shap...]
    unnamed x44 -> x16, local copies, waits for them, and re-layouts: 12.3 us -> 2.04 us
    pallas_call x0 -> x1, Pallas kernels: none -> 2.75 us  [finish(): pl.pallas_call(body, out_shape=[jax.ShapeDtypeStruct(like.shape, like.dty...]
where the time goes in v3:
time: 224 us
  Pallas kernels  218 us (97%)
  local copies, waits for them, and re-layouts  3.65 us (2%)
    pallas_call x1, Pallas kernels, run_layer(): pl.pallas_call(partial(layer, dims), out_shape=[jax.ShapeDtypeStruct(shap...  215 us

profile of v3, /device:TPU:0, one launch (start us, length us, event | category | flops | bytes accessed | tf_op | source)
XLA Modules:
  0.0 223.7 jit_solution(14774423249560702734)
XLA Ops:
  0.7 0.0 copy-start.7
  0.7 0.8 fusion.14
  1.4 0.0 copy-done.7
  1.5 0.0 copy-start.5
  1.5 0.0 copy-start.6
  1.5 0.6 copy-done.5
  2.1 0.0 copy-done.6
  2.1 0.0 copy-start.3
  2.2 0.0 copy-start.4
  2.2 0.0 copy-start.1
  2.2 0.0 copy-start.2
  2.2 0.6 copy-done.3
  2.8 0.0 copy-done.4
  2.8 0.0 copy-done.1
  2.9 0.0 copy-done.2
  2.9 0.6 fusion.6.refs_2_
  3.5 215.0 %griffin_layer.1 = (bf16[128,1024]{1,0:T(8,128)(2,1)}, f32[128,1024]{1,0:T(8,128)}, bf16[4,32,768]{2,1,0:T(8,128)(2,1)}, bf16[4,48,768]{2,1,0:T(8,128)(2,1)}, bf...) custom-call(bf16[128,1024]{1,0:T(8,128)(2,1)} %bitcast.31, ...), custom_call_target="tpu_custom_call" | custom-call | flops 14495514624 | bytes 8388608 | tf_op jit(solution)/shard_map/griffin_layer/pallas_call | solution.py:1359
  218.5 0.0 copy-start
  218.5 0.7 copy-done
  219.2 0.5 slice_bitcast_fusion.4
  219.7 0.5 slice_bitcast_fusion.1
  220.2 0.6 slice_bitcast_fusion
  220.8 2.8 %finish.1 = (f32[128,1024]{1,0:T(8,128)}, bf16[128,1024]{1,0:T(8,128)(2,1)}, f32[48,1024]{1,0:T(8,128)}, f32[96,1024]{1,0:T(8,128)}, f32[32,1536]{1,0:T(8,128)},...) custom-call(bf16[4,32,768]{2,1,0:T(8,128)(2,1)} %get-tuple-element.3, ...), custom_call_target="tpu_custom_call" | custom-call | tf_op jit(solution)/shard_map/finish/pallas_call | solution.py:1418
  (3 shorter events, 0.0 us)
Async XLA Ops:
  0.7 0.8 copy-start.7
  1.5 0.7 copy-start.5
  1.5 0.7 copy-start.6
  2.1 0.7 copy-start.3
  2.2 0.7 copy-start.4
  2.2 0.7 copy-start.1
  2.2 0.7 copy-start.2
  218.5 0.7 copy-start

commit v4 on v3

--- a/solution.py
+++ b/solution.py
@@ -306,17 +306,27 @@
             return own
 
     class Column:
-        def __init__(self, src, w, R, C, lane0):
-            self.src, self.w, self.R, self.C, self.lanes = src, w, R, C, pl.ds(lane0, C)
-            self.ra, self.rz, self.rc = new(), new(4), new()
+        def __init__(self, src, raw, sorted_, w, R, C, lane0):
+            self.src, self.raw, self.sorted = src, raw, sorted_
+            self.w, self.R, self.C, self.lanes = w, R, C, pl.ds(lane0, C)
+            self.rl, self.ra, self.rz, self.rc = new(), new(), new(4), new()
             self.out = []
 
+        def load(self):
+            keep_local(self.src, self.raw, self.rl)
+
+        def prepare(self):
+            local_wait(self.src, self.raw, self.rl)
+            value, part = self.raw[...], self.C // (2 * RING)
+            for k in range(PLANE):
+                first = [(g * PLANE + k) * part for g in range(2 * RING)]
+                self.sorted[k] = jnp.concatenate([value[:, at : at + part] for at in first], axis=1)
+
         def spread(self):
-            R, C, src = self.R, self.C, self.src
-            dst = self.w.at[zh, c, ds(p * R, R, 16), self.lanes]
+            dst = self.w.at[zh, c, ds(p * self.R, self.R, 16), self.lanes]
             for k, dev in plane_peers:
-                self.out.append(push(src.at[:, ds(k * C, C, 128)], dst, dev, self.ra))
-            keep_local(src.at[:, ds(p * C, C, 128)], dst, self.ra)
+                self.out.append(push(self.sorted.at[k], dst, dev, self.ra))
+            keep_local(self.sorted.at[p], dst, self.ra)
 
         def block(self, z):
             return self.w.at[z, c, :, self.lanes]
@@ -337,61 +347,25 @@
             arrived(self.w.at[:, 1 - c, :, self.lanes], self.rc)
             settle(*self.out)
 
-    class Rows:
-        def __init__(self, src, w, stage, R):
-            self.src, self.w, self.stage, self.R = src, w, stage, R
-            self.rz, self.rp, self.rc = new(4), new(), new()
+    class Row(Column):
+        def __init__(self, src, w):
+            self.src, self.w, self.lanes = src, w, pl.ds(0, w.shape[3])
+            self.ra, self.rz, self.rc = new(), new(4), new()
             self.out = []
 
-        def block(self, z):
-            return self.stage.at[z]
-
         def z_send(self):
+            keep_local(self.src, self.block(zh), self.ra)
             self.out += z_send(self.src, self.block, self.rz)
 
-        def z_forward(self):
-            self.out += z_forward(self.block, self.rz)
-
-        def hand(self, src, k, pred):
-            R = self.R
-            dst = self.w.at[ds((c * PLANE + p) * R, R, 16)]
-            self.out.append(push(src, dst, {"yl": k // 2, "xl": k % 2}, self.rp, pred & (k != p)))
-            pl.when(pred & (k == p))(lambda: keep_local(src, dst, self.rp))
-
-        def hand_from(self, k, pred, waited=False):
-            if not waited:
-                arrived(self.block(k), self.rz + k, pred)
-            self.hand(self.block(k), k, pred)
-
-        def near(self):
-            self.hand(self.src, zh, zh >= 0)
-            self.hand_from(zh - 1, zh >= 1)
-            self.hand_from(zh + 1, zh <= RING - 2)
-
-        def far(self):
-            last = RING - 1
-            self.hand_from(zh - 2, (zh >= 2) & (zh != last - 1))
-            self.hand_from(zh - 2, zh == last - 1, True)
-            self.hand_from(zh + 2, (zh <= last - 2) & (zh != 1))
-            self.hand_from(zh + 2, zh == 1, True)
-            self.hand_from(0, zh == last)
-            self.hand_from(last, zh == 0)
-
-        def plane_wait(self):
-            H = PLANE * self.R
-            half = self.w.at[ds(c * H, H, 16)]
-            arrived(half, self.rp)
-            self.out.append(push(half, half, to_core, self.rc))
-
-        def end(self):
-            H = PLANE * self.R
-            arrived(self.w.at[ds((1 - c) * H, H, 16)], self.rc)
-            settle(*self.out)
+        def z_wait(self):
+            local_wait(self.src, self.block(zh), self.ra)
+            super().z_wait()
 
     class ColumnsGrad:
         def __init__(self, g, other, slots, land, R, lane0, lanes, result):
             self.g, self.other, self.slots, self.land = g, other, slots, land
             self.R, self.lanes, self.result = R, pl.ds(lane0, lanes), result
+            self.rows = PLANE * R
             self.rc, self.rl = new(), new()
             self.zsum = ZSum(
                 lambda z: g.at[z, c, :, self.lanes], lambda k: slots.at[k, :, self.lanes], self.add_slot
@@ -404,7 +378,7 @@
                 s = pl.ds(o, 16)
                 g[z, c, s, q] = (g[z, c, s, q].astype(f32) + self.slots[k, s, q].astype(f32)).astype(bf16)
 
-            loop(PLANE * self.R, 16, add)
+            loop(self.rows, 16, add)
 
         def core_send(self):
             self.pushed = push(
@@ -420,7 +394,7 @@
                     s = pl.ds(o, 16)
                     g[z, c, s, q] = (g[z, c, s, q].astype(f32) + self.other[z, s, q].astype(f32)).astype(bf16)
 
-                loop(PLANE * self.R, 16, add)
+                loop(self.rows, 16, add)
             self.zsum.send()
 
         def z_forward(self):
@@ -447,56 +421,20 @@
             settle(*self.out)
             deliver(self.land.at[:, :, self.lanes], self.result.at[:, :, self.lanes])
 
-    class RowsGrad:
-        def __init__(self, g, other, stage, slots, R, total, result):
-            self.g, self.other, self.stage, self.slots, self.R = g, other, stage, slots, R
-            self.sum, self.result = total, result
-            self.rc, self.rl = new(), new()
-            self.zsum = ZSum(lambda z: stage.at[z], lambda k: slots.at[k], self.add_slot)
-
-        def add_slot(self, z, k):
-            g = self.stage
+    class RowsGrad(ColumnsGrad):
+        def __init__(self, g, other, slots, total, result):
+            super().__init__(g, other, slots, None, 0, 0, g.shape[3], result)
+            self.rows, self.sum = g.shape[2], total
+
+        def end(self):
+            self.zsum.end()
+            settle(self.pushed)
 
             def add(o):
                 s = pl.ds(o, 16)
-                g[z, s] = (g[z, s].astype(f32) + self.slots[k, s].astype(f32)).astype(bf16)
-
-            loop(self.R, 16, add)
-
-        def core_send(self):
-            H = PLANE * self.R
-            self.out = [push(self.g.at[ds((1 - c) * H, H, 16)], self.other, to_core, self.rc)]
-
-        def plane_send(self):
-            R, H, g = self.R, PLANE * self.R, self.g
-            arrived(self.other, self.rc)
-
-            def add(o):
-                s = ds(c * H + o, 16, 16)
-                g[s] = (g[s].astype(f32) + self.other[pl.ds(o, 16)].astype(f32)).astype(bf16)
-
-            loop(H, 16, add)
-            dst = self.stage.at[p]
-            for k, dev in plane_peers:
-                self.out.append(push(g.at[ds(c * H + k * R, R, 16)], dst, dev, self.rl))
-            keep_local(g.at[ds(c * H + p * R, R, 16)], dst, self.rl)
-
-        def z_send(self):
-            arrived(self.stage, self.rl)
-            self.zsum.send()
-
-        def z_forward(self):
-            self.zsum.forward()
-
-        def end(self):
-            self.zsum.end()
-            settle(*self.out)
-
-            def add(o):
-                s = pl.ds(o, 16)
-                self.sum[s] = self.zsum.total(self.stage[zh, s].astype(f32), [self.slots[k, s] for k in range(4)])
-
-            loop(self.R, 16, add)
+                self.sum[s] = self.zsum.total(self.g[zh, c, s].astype(f32), [self.slots[k, s] for k in range(4)])
+
+            loop(self.rows, 16, add)
             deliver(self.sum, self.result)
 
     class Carry:
@@ -544,7 +482,6 @@
 
     GL = PLANE * RD
     ring = zh * 2 + c
-    home = {"yl": zh // 2, "xl": zh % 2}
 
     def ring_place(at):
         return {"zh": at // 2, "c": at % 2}
@@ -575,13 +512,7 @@
                 whole = whole + dot(r.pp[k].reshape(2 * RING * 16, 128), move)
             for at in range(2 * RING):
                 r.gains[0:2, at * GL : (at + 1) * GL] = whole[at * 16 : at * 16 + 2]
-            from_row = lax.broadcasted_iota(jnp.int32, (128, CW), 0)
-            to_lane = lax.broadcasted_iota(jnp.int32, (128, CW), 1)
-            whole = jnp.zeros((16, CW), f32)
-            for k in range(PLANE):
-                for cc in (0, 1):
-                    move = ((to_lane == from_row + (cc * PLANE + k) * RW) & (from_row < RW)).astype(bf16)
-                    whole = whole + dot(r.pp[k, 2 * p + cc], move)
+            whole = jnp.concatenate([r.pr[at, :, 0:RW].astype(f32) for at in range(2 * RING)], axis=1)
             r.chan[...] = whole[2:10]
             rate = r.pack[...].astype(f32)
             for k in range(CW // 128):
@@ -618,43 +549,25 @@
 
     class SmallGrad:
         def __init__(self):
-            self.rg, self.rc, self.rp, self.ro = new(2 * RING), new(2 * RING), new(PLANE), new()
+            self.rg, self.rp = new(2 * RING), new(PLANE)
             self.out = []
 
-        def chan_one(self):
-            for cc in (0, 1):
-                self.out.append(
-                    push(r.gchan, r.gc.at[ring], {"zh": p, "c": cc}, self.rc + ring, (zh != p) | (c != cc))
-                )
-
-        def chan_two(self):
-            def total():
-                r.gc[ring] = r.gchan[...]
-                value = r.gchan[...]
-                for at in range(2 * RING):
-                    arrived(r.gc.at[at], self.rc + at, ring != at)
-                value = r.gc[0]
-                for at in range(1, 2 * RING):
-                    value = value + r.gc[at]
-                r.chan_sum[...] = value
-
-            pl.when(p == zh)(total)
-            for _, dev in plane_peers:
-                self.out.append(push(r.chan_sum, r.chan_sum, dev, self.ro, p == zh))
-
-        def gain_one(self):
+        def one(self):
             for at in range(2 * RING):
-                src = r.ggain.at[:, pl.ds(at * GL, GL)]
-                self.out.append(push(src, r.gg.at[ring], ring_place(at), self.rg + ring, ring != at))
-
-        def gain_two(self):
-            r.gg[ring] = r.ggain[:, ds(ring * GL, GL, 128)]
+                own = jnp.concatenate([r.gchan[:, at * RW : (at + 1) * RW], jnp.zeros((8, 128 - RW), f32)], axis=1)
+                r.gs[at, 0:8], r.gs[at, 8:16] = r.ggain[:, at * GL : (at + 1) * GL], own
+            for at in range(2 * RING):
+                self.out.append(push(r.gs.at[at], r.gg.at[ring], ring_place(at), self.rg + ring, ring != at))
+
+        def two(self):
+            r.gg[ring] = r.gs[ring]
             for at in range(2 * RING):
                 arrived(r.gg.at[at], self.rg + at, ring != at)
             value = r.gg[0]
             for at in range(1, 2 * RING):
                 value = value + r.gg[at]
-            r.gp[p] = value
+            r.small_sum[...] = value
+            r.gp[p] = value[0:8]
             for _, dev in plane_peers:
                 self.out.append(push(r.gp.at[p], r.gp.at[p], dev, self.rp + p))
 
@@ -666,11 +579,6 @@
             to_lane = lax.broadcasted_iota(jnp.int32, (GL, 128), 1)
             move = (from_lane == to_lane + p * RD).astype(f32)
             r.small_sum[0:8] = jnp.dot(gains, move, precision=lax.Precision.HIGHEST)
-            arrived(r.chan_sum, self.ro, p != zh)
-            from_lane = lax.broadcasted_iota(jnp.int32, (CW, 128), 0)
-            to_lane = lax.broadcasted_iota(jnp.int32, (CW, 128), 1)
-            move = (from_lane == to_lane + (c * PLANE + p) * RW).astype(f32)
-            r.small_sum[8:16] = jnp.dot(r.chan_sum[...], move, precision=lax.Precision.HIGHEST)
             deliver(r.small_sum, r.small_out)
             settle(*self.out)
 
@@ -694,10 +602,13 @@
     for load in first_loads:
         keep_local(*load)
 
-    w_i, w_b = Column(r.input_weight, r.w_ib, RD, CW, 0), Column(r.branch_weight, r.w_ib, RD, CW, CW)
-    w_d, w_j = Column(r.decay_weight, r.w_di, RW, CW, 0), Column(r.inject_weight, r.w_di, RW, CW, CW)
-    w_g, w_u = Column(r.mlp_gate, r.w_gu, RD, CF, 0), Column(r.mlp_up, r.w_gu, RD, CF, CF)
-    w_o, w_dn = Rows(r.output_weight, r.w_o, r.st_o, RW), Rows(r.mlp_down, r.w_dn, r.st_dn, RF)
+    w_i = Column(r.input_weight, r.raw_i, r.sort_i, r.w_ib, RD, CW, 0)
+    w_b = Column(r.branch_weight, r.raw_b, r.sort_b, r.w_ib, RD, CW, CW)
+    w_d = Column(r.decay_weight, r.raw_d, r.sort_d, r.w_di, RW, CW, 0)
+    w_j = Column(r.inject_weight, r.raw_j, r.sort_j, r.w_di, RW, CW, CW)
+    w_g = Column(r.mlp_gate, r.raw_g, r.sort_g, r.w_gu, RD, CF, 0)
+    w_u = Column(r.mlp_up, r.raw_u, r.sort_u, r.w_gu, RD, CF, CF)
+    w_o, w_dn = Row(r.output_weight, r.w_o), Row(r.mlp_down, r.w_dn)
     ag_x, ag_conv, ag_two = Gather(r.x_all), Gather(r.conv), Gather(r.n_two)
     ag_cot, ag_out = Gather(r.cot_all), Gather(r.d_out)
     small, small_grad = Small(), SmallGrad()
@@ -707,6 +618,9 @@
     step = 256
     chunk = PLANE * RD * 2
 
+    for w in (w_i, w_d, w_j, w_b, w_g, w_u):
+        w.load()
+    w_i.prepare()
     pl.semaphore_wait(barrier, len(plane_peers) + places - 1)
     local_wait(*first_loads[0])
     small.one()
@@ -715,10 +629,13 @@
     ag_x.start()
     halo_x = new()
     sent_x = push(r.x_all.at[p, pl.ds(T - 16, 16)], r.x_halo.at[p], to_next, halo_x, pos < places - 1)
+    w_d.prepare()
+    w_d.spread()
+    w_i.z_send()
     w_o.z_send()
     small.two()
-    w_i.z_send()
-    w_d.spread()
+    w_j.prepare()
+    w_b.prepare()
 
     @pl.when(pos == 0)
     def _():
@@ -730,6 +647,7 @@
     ag_x.mid()
     w_j.spread()
     w_b.spread()
+    w_g.prepare()
     local_wait(*first_loads[2])
     small.three()
 
@@ -742,13 +660,12 @@
         loop(T, 32, norm_one)
 
     norm_block(p)
-    w_o.z_forward()
-    w_d.z_send()
+    w_i.z_forward()
     ag_x.wait_x()
     norm_block(px)
     ag_x.wait_y()
     norm_block(py)
-    w_i.z_forward()
+    w_d.z_send()
     small.four()
     for k, _ in plane_peers:
         arrived(r.x_halo.at[k], halo_p + k)
@@ -757,8 +674,10 @@
     ag_x.wait_d()
     norm_block(pd)
     settle(*ag_x.out, sent_x, *sent_p)
+    w_g.spread()
+    w_o.z_forward()
     w_i.z_wait()
-    w_g.spread()
+    w_u.prepare()
     w_i.end()
 
     def weight_ib(lanes):
@@ -793,7 +712,7 @@
     w_d.end()
 
     def pre(q, lanes):
-        return dot(r.conv[q], r.w_di[q, :, :, lanes].reshape(W // RING, CW))
+        return dot(r.conv[q], r.w_di[:, :, ds(q * RW, RW, 16), lanes].reshape(CW, CW))
 
     r.pair[:, 0:CW] = pre(p, lanes_a)
     ag_conv.wait_x()
@@ -801,15 +720,15 @@
     ag_conv.wait_y()
     r.pair[:, 0:CW] += pre(py, lanes_a)
     w_j.z_forward()
-    w_g.z_send()
     ag_conv.wait_d()
     r.pair[:, 0:CW] += pre(pd, lanes_a)
     settle(*ag_conv.out)
     w_u.spread()
-    w_o.near()
-    w_o.far()
+    ag_cot.start()
+    w_b.z_forward()
+    w_g.z_send()
     w_j.z_wait()
-    ag_cot.start()
+    w_o.z_wait()
     w_j.end()
     r.pair[:, CW : 2 * CW] = pre(0, lanes_b)
     for q in range(1, PLANE):
@@ -855,11 +774,10 @@
         r.own_f[k : k + 1] = ends[2 * k + 1]
         r.own_f[PLANE + k : PLANE + k + 1] = ends[2 * k]
     carry_f.send_core()
-    w_b.z_forward()
+    ag_cot.mid()
+    carry_f.send()
     w_b.z_wait()
-    carry_f.send()
-    w_o.plane_wait()
-    ag_cot.mid()
+    w_g.z_forward()
     w_b.end()
     r.work[...] = dot(r.n_one[...].reshape(M, D), weight_ib(lanes_b))
 
@@ -870,6 +788,7 @@
     loop(M, 16, gates_one)
     w_o.end()
     carry_f.fold(r.into)
+    w_u.z_send()
     for k in range(PLANE):
         r.state[k, 0:8] = jnp.broadcast_to(r.into[k : k + 1], (8, CW))
 
@@ -884,15 +803,16 @@
 
     def out_part(o):
         q = pl.ds(o, step)
-        r.part[:, :, q] = dot(r.mixed[...], r.w_o[:, q]).astype(bf16).reshape(PLANE, T, step)
+        r.part[:, :, q] = dot(r.mixed[...], r.w_o[:, :, :, q].reshape(CW, step)).astype(bf16).reshape(PLANE, T, step)
 
     loop(D, step, out_part)
     rs_one = Scatter(r.part, r.got_one)
     rs_one.start()
-    w_g.z_forward()
-    w_u.z_send()
     ag_cot.end()
+    w_g.z_wait()
     rs_one.mid()
+    w_u.z_forward()
+    w_dn.z_send()
     rs_one.end()
 
     def norm_two(o, summed):
@@ -903,11 +823,10 @@
 
     rs_one.each(16, norm_two)
     ag_two.start()
-    w_g.z_wait()
-    w_dn.z_send()
     ag_two.mid()
-    w_u.z_forward()
+    w_u.z_wait()
     w_g.end()
+    w_dn.z_forward()
     ag_two.end()
 
     def mlp_in(o):
@@ -915,7 +834,6 @@
         r.pair[:, q] = dot(r.n_two[...].reshape(M, D), r.w_gu[:, :, :, q].reshape(D, step))
 
     loop(CF, step, mlp_in)
-    w_u.z_wait()
     w_u.end()
     loop(CF, step, lambda o: mlp_in(pl.multiple_of(CF + o, step)))
 
@@ -928,24 +846,21 @@
         r.pair[s, CF : 2 * CF] = value
 
     loop(M, 16, gates_mlp)
-    w_dn.near()
-
-    def grad_down(o):
-        q = pl.ds(o, step)
-        r.g_dn[q] = dot_tn(r.hidden[:, q], r.cot_all[...].reshape(M, D)).astype(bf16)
-
-    loop(CF, step, grad_down)
-    g_dn = RowsGrad(r.g_dn, r.h_dn, r.sg_dn, r.z_dn, RF, r.t_dn, r.grad_mlp_down)
+    w_dn.z_wait()
+
+    half = CF // 2
+    for k in (0, 1):
+        for o in range(0, D, D // 2):
+            value = dot_tn(r.hidden[:, k * half : (k + 1) * half], r.cot_all[:, :, o : o + D // 2].reshape(M, D // 2))
+            r.g_dn[k * RING // 2 : (k + 1) * RING // 2, :, :, o : o + D // 2] = value.astype(bf16).reshape(
+                RING // 2, 2, RF, D // 2
+            )
+    g_dn = RowsGrad(r.g_dn, r.h_dn, r.z_dn, r.t_dn, r.grad_mlp_down)
     g_dn.core_send()
-    w_dn.z_forward()
-    w_dn.far()
-    w_dn.plane_wait()
-    g_dn.plane_send()
     w_dn.end()
 
     for k in range(CF // step):
-        q = pl.ds(k * step, step)
-        back = dot_nt(r.cot_all[...].reshape(M, D), r.w_dn[q])
+        back = dot_nt(r.cot_all[...].reshape(M, D), r.w_dn[...].reshape(CF, D)[k * step : (k + 1) * step])
         r.d_pair[:, k * step : (k + 1) * step] = (back * r.pair[:, k * step : (k + 1) * step]).astype(bf16)
         r.d_pair[:, CF + k * step : CF + (k + 1) * step] = (
             back * r.pair[:, CF + k * step : CF + (k + 1) * step]
@@ -961,6 +876,7 @@
     lax.fori_loop(0, RING, d_two_part, 0)
     rs_two = Scatter(r.part, r.got_two)
     rs_two.start()
+    g_dn.z_send()
 
     def grad_gate_up(lane0):
         lanes = pl.ds(lane0, CF)
@@ -980,12 +896,12 @@
     grad_gate_up(CF)
     g_u = ColumnsGrad(r.w_gu, r.h_gu, r.z_gu, r.l_gu, RD, CF, CF, r.grads_gu)
     g_u.core_send()
-    g_dn.z_send()
+    g_dn.z_forward()
     g_g.z_send()
 
     def act_part(o):
         q = pl.ds(o, step)
-        r.part_act[:, :, q] = dot(r.hidden[...], r.w_dn[:, q]).astype(bf16).reshape(PLANE, T, step)
+        r.part_act[:, :, q] = dot(r.hidden[...], r.w_dn[:, :, :, q].reshape(CF, step)).astype(bf16).reshape(PLANE, T, step)
 
     loop(D, step, act_part)
     r.ggain[...] = jnp.zeros_like(r.ggain)
@@ -1005,14 +921,13 @@
 
     rs_two.each(16, norm_two_back)
     ag_out.start()
-    g_u.z_send()
     ag_out.mid()
-    g_dn.z_forward()
+    g_g.z_forward()
     ag_out.end()
     rs_act = Scatter(r.part_act, r.got_act)
     rs_act.start()
 
-    r.work[...] = dot_nt(r.d_out[...].reshape(M, D), r.w_o[...])
+    r.work[...] = dot_nt(r.d_out[...].reshape(M, D), r.w_o[...].reshape(CW, D))
 
     def split(o):
         for k in range(PLANE):
@@ -1047,11 +962,12 @@
     carry_b.send_core()
 
     def grad_out(o):
-        q = pl.ds(o, 128)
-        r.w_o[q] = dot_tn(r.mixed[:, q], r.d_out[...].reshape(M, D)).astype(bf16)
-
-    loop(CW, 128, grad_out)
-    g_o = RowsGrad(r.w_o, r.h_o, r.sg_o, r.z_o, RW, r.t_o, r.grad_output_weight)
+        q = pl.ds(o, D // 2)
+        value = dot_tn(r.mixed[...], r.d_out[:, :, q].reshape(M, D // 2))
+        r.w_o[:, :, :, q] = value.astype(bf16).reshape(RING, 2, RW, D // 2)
+
+    loop(D, D // 2, grad_out)
+    g_o = RowsGrad(r.w_o, r.h_o, r.z_o, r.t_o, r.grad_output_weight)
     g_o.core_send()
     carry_b.send()
     rs_act.mid()
@@ -1070,10 +986,9 @@
     lax.fori_loop(0, RING, d_branch_part, 0)
     g_b = ColumnsGrad(r.w_ib, r.h_ib, r.z_ib, r.l_ib, RD, CW, CW, r.grads_ib)
     g_b.core_send()
-    g_o.plane_send()
-    g_b.z_send()
-    g_g.z_forward()
+    g_g.plane_send()
     carry_b.fold(r.into)
+    g_u.z_send()
 
     def back(o):
         sums = [jnp.zeros((1, CW), f32)] * 2
@@ -1098,7 +1013,7 @@
     loop(T, 16, back)
 
     def conv_part(q, _):
-        r.part_conv[q] = dot_nt(r.d_pre[...], r.w_di[q].reshape(W // RING, 2 * CW)).astype(bf16)
+        r.part_conv[q] = dot_nt(r.d_pre[...], r.w_di[:, :, ds(q * RW, RW, 16), :].reshape(CW, 2 * CW)).astype(bf16)
         return 0
 
     lax.fori_loop(0, RING, conv_part, 0)
@@ -1113,13 +1028,14 @@
     rs_act.each(16, finish_act)
     deliver(r.act, r.activations)
     g_o.z_send()
+    g_b.z_send()
     g_u.z_forward()
     g_dn.end()
 
     def grad_dec_inj(lanes):
         def run(q, _):
             value = dot_tn(r.conv[q], r.d_pre[:, lanes])
-            r.w_di[q, :, :, lanes] = value.astype(bf16).reshape(2, W // SHARES * PLANE, CW)
+            r.w_di[:, :, ds(q * RW, RW, 16), lanes] = value.astype(bf16).reshape(RING, 2, RW, CW)
             return 0
 
         lax.fori_loop(0, RING, run, 0)
@@ -1131,9 +1047,7 @@
     grad_dec_inj(lanes_b)
     g_j = ColumnsGrad(r.w_di, r.h_di, r.z_di, r.l_di, RW, CW, CW, r.grads_di)
     g_j.core_send()
-    g_d.z_send()
     g_b.z_forward()
-    g_g.plane_send()
     rs_conv.end()
 
     for half in (0, 1):
@@ -1148,7 +1062,7 @@
     for k in range(PLANE):
         r.halo_out[4 * k : 4 * k + 4] = r.d_conv[k, 0:4]
     sent_b = push(r.halo_out, r.halo_in, to_prev, halo_b, pos > 0)
-    g_j.z_send()
+    g_d.z_send()
 
     def taps_back(o):
         sums = [jnp.zeros((1, CW), f32)] * 5
@@ -1165,13 +1079,13 @@
             r.gchan[j : j + 1] += sums[j]
 
     loop(T, 16, taps_back)
-    small_grad.chan_one()
 
     @pl.when(pos == places - 1)
     def _():
         r.halo_in[...] = jnp.zeros((16, CW), f32)
 
     arrived(r.halo_in, halo_b, pos < places - 1)
+    g_j.z_send()
     for k in range(PLANE):
         r.d_conv[k, T : T + 8] = jnp.concatenate([r.halo_in[4 * k : 4 * k + 4], jnp.zeros((4, CW), f32)], axis=0)
 
@@ -1211,7 +1125,6 @@
     g_u.plane_send()
     g_d.z_forward()
     g_b.plane_send()
-    small_grad.chan_two()
     rs_three.end()
 
     def norm_one_back(o, d_n):
@@ -1225,7 +1138,7 @@
 
     rs_three.each(16, norm_one_back)
     deliver(r.d_x, r.d_tokens)
-    small_grad.gain_one()
+    small_grad.one()
     settle(sent_b)
     g_j.z_forward()
     g_i.z_forward()
@@ -1233,7 +1146,7 @@
     g_u.end()
     g_d.plane_send()
     g_o.end()
-    small_grad.gain_two()
+    small_grad.two()
     g_b.end()
     g_j.plane_send()
     g_i.plane_send()
@@ -1276,19 +1189,20 @@
         "grad_mlp_down": ((RF, D), f32),
         "small_out": ((16, 128), f32),
     }
+    columns = (("i", RD, CW), ("b", RD, CW), ("d", RW, CW), ("j", RW, CW), ("g", RD, CF), ("u", RD, CF))
     scratch = {
         "w_ib": ((RING, 2, PLANE * RD, 2 * CW), bf16),
         "w_di": ((RING, 2, PLANE * RW, 2 * CW), bf16),
         "w_gu": ((RING, 2, PLANE * RD, 2 * CF), bf16),
-        "w_o": ((CW, D), bf16),
-        "w_dn": ((CF, D), bf16),
-        "st_o": ((RING, RW, D), bf16),
-        "st_dn": ((RING, RF, D), bf16),
+        "w_o": ((RING, 2, RW, D), bf16),
+        "w_dn": ((RING, 2, RF, D), bf16),
+        **{"raw_" + n: ((R, PLANE * C), bf16) for n, R, C in columns},
+        **{"sort_" + n: ((PLANE, R, C), bf16) for n, R, C in columns},
         "h_ib": ((RING, PLANE * RD, 2 * CW), bf16),
         "h_di": ((RING, PLANE * RW, 2 * CW), bf16),
         "h_gu": ((RING, PLANE * RD, 2 * CF), bf16),
-        "h_o": ((CW // 2, D), bf16),
-        "h_dn": ((CF // 2, D), bf16),
+        "h_o": ((RING, RW, D), bf16),
+        "h_dn": ((RING, RF, D), bf16),
         "z_ib": ((4, PLANE * RD, 2 * CW), bf16),
         "z_di": ((4, PLANE * RW, 2 * CW), bf16),
         "z_gu": ((4, PLANE * RD, 2 * CF), bf16),
@@ -1297,8 +1211,6 @@
         "l_ib": ((PLANE, RD, 2 * CW), bf16),
         "l_di": ((PLANE, RW, 2 * CW), bf16),
         "l_gu": ((PLANE, RD, 2 * CF), bf16),
-        "sg_o": ((RING, RW, D), bf16),
-        "sg_dn": ((RING, RF, D), bf16),
         "n_one": ((PLANE, T, D), bf16),
         "n_two": ((PLANE, T, D), bf16),
         "cot_all": ((PLANE, T, D), bf16),
@@ -1333,7 +1245,7 @@
         "x_all": ((PLANE, T, D), bf16),
         "x_halo": ((PLANE, 16, D), bf16),
         "n_halo": ((PLANE, 16, D), bf16),
-        "g_dn": ((CF, D), bf16),
+        "g_dn": ((RING, 2, RF, D), bf16),
         "masks": ((7, M, 128), f32),
         "pack": ((16, 128), bf16),
         "pr": ((2 * RING, 16, 128), bf16),
@@ -1343,14 +1255,13 @@
         "t_o": ((RW, D), f32),
         "t_dn": ((RF, D), f32),
         "small_sum": ((16, 128), f32),
-        "chan_sum": ((8, CW), f32),
         "gains": ((8, D), f32),
         "chan": ((8, CW), f32),
         "ggain": ((8, D), f32),
         "gchan": ((8, CW), f32),
-        "gg": ((2 * RING, 8, GL), f32),
+        "gs": ((2 * RING, 16, 128), f32),
+        "gg": ((2 * RING, 16, 128), f32),
         "gp": ((PLANE, 8, GL), f32),
-        "gc": ((2 * RING, 8, CW), f32),
     }
     dims = SimpleNamespace(
         T=T, D=D, W=W, F=F, CW=CW, CF=CF, RD=RD, RW=RW, RF=RF, NL=NL, SEGS=SEGS, receives=RECEIVES + 2 * RING * NL, names=[*ins, *outs, *scratch, "ss", "rs"]
@@ -1406,8 +1317,11 @@
             loads[i].wait()
             for j, target in enumerate(targets):
                 wide = held[len(names) + 2 * i + j]
-                for k in range(blocks):
-                    wide[:, k * C : (k + 1) * C] = held[i][k, :, j * C : (j + 1) * C].astype(f32)
+                part = C // (2 * RING)
+                values = [held[i][k, :, j * C : (j + 1) * C].astype(f32) for k in range(blocks)]
+                wide[...] = jnp.concatenate(
+                    [value[:, g * part : (g + 1) * part] for g in range(2 * RING) for value in values], axis=1
+                )
                 stores.append(copy(wide, outs[target]))
         for i, name in enumerate(plain):
             loads[len(pairs) + i].wait()
@@ -1470,7 +1384,8 @@
     gains = pooled(jnp.stack([first_gain, second_gain]), 1)
     chan = pooled(jnp.concatenate([conv_taps.T, jnp.stack([conv_bias, decay_bias, inject_bias])]), 1)
     RD, RW = gains.shape[1], chan.shape[1]
-    rates = lax.dynamic_slice_in_dim(decay_exponent, mine * (width // PLANE), width // PLANE).reshape(-1, 128)
+    rates = decay_exponent.reshape(2 * RING, PLANE, width // SHARES)
+    rates = lax.dynamic_index_in_dim(rates, mine, 1, keepdims=False).reshape(-1, 128)
     lengths = jnp.concatenate([doc_lengths // 256, doc_lengths % 256])
     pack = jnp.concatenate([rows(gains), rows(chan), rows(lengths), rows(rates)])
     pack = jnp.pad(pack, ((0, 16 - pack.shape[0]), (0, 0)))

time: 224 us -> 199 us (0.89)
  Pallas kernels: 218 us -> 193 us
    pallas_call x1, Pallas kernels: 215 us -> 190 us  [run_layer(): pl.pallas_call(partial(layer, dims), out_shape=[jax.ShapeDtypeStruct(shap...]
where the time goes in v4:
time: 199 us
  Pallas kernels  193 us (97%)
  local copies, waits for them, and re-layouts  4.46 us (2%)
    pallas_call x1, Pallas kernels, run_layer(): pl.pallas_call(partial(layer, dims), out_shape=[jax.ShapeDtypeStruct(shap...  190 us

profile of v4, /device:TPU:0, one launch (start us, length us, event | category | flops | bytes accessed | tf_op | source)
XLA Modules:
  0.0 198.6 jit_solution(10646571459052919071)
XLA Ops:
  0.7 0.0 copy-start.8
  0.7 0.6 copy-done.8
  1.3 0.0 copy-start.6
  1.3 0.0 copy-start.7
  1.3 0.0 copy-start
  1.3 0.6 copy-done.6
  2.0 0.0 copy-done.7
  2.0 0.0 copy-start.4
  2.0 0.0 copy-start.5
  2.0 0.0 copy-start.2
  2.0 0.0 copy-start.3
  2.0 0.6 copy-done.4
  2.7 0.0 copy-done.5
  2.7 0.0 copy-done.2
  2.7 0.0 copy-done.3
  2.7 0.0 copy-done
  2.7 0.1 reshape.38
  2.9 0.1 convert_element_type.16
  2.9 0.6 fusion.6.refs_2_
  3.5 189.5 %griffin_layer.1 = (bf16[128,1024]{1,0:T(8,128)(2,1)}, f32[128,1024]{1,0:T(8,128)}, bf16[4,32,768]{2,1,0:T(8,128)(2,1)}, bf16[4,48,768]{2,1,0:T(8,128)(2,1)}, bf...) custom-call(bf16[128,1024]{1,0:T(8,128)(2,1)} %bitcast.29, ...), custom_call_target="tpu_custom_call" | custom-call | flops 14495514624 | bytes 8388608 | tf_op jit(solution)/shard_map/griffin_layer/pallas_call | solution.py:1270
  193.1 0.0 copy-start.1
  193.1 0.7 copy-done.1
  193.8 0.5 slice_bitcast_fusion.4
  194.3 0.5 slice_bitcast_fusion.1
  194.8 0.6 slice_bitcast_fusion
  195.4 3.1 %finish.1 = (f32[128,1024]{1,0:T(8,128)}, bf16[128,1024]{1,0:T(8,128)(2,1)}, f32[48,1024]{1,0:T(8,128)}, f32[96,1024]{1,0:T(8,128)}, f32[32,1536]{1,0:T(8,128)},...) custom-call(bf16[4,32,768]{2,1,0:T(8,128)(2,1)} %get-tuple-element.3, ...), custom_call_target="tpu_custom_call" | custom-call | tf_op jit(solution)/shard_map/finish/pallas_call | solution.py:1332
  (4 shorter events, 0.1 us)
Async XLA Ops:
  0.7 0.7 copy-start.8
  1.3 0.7 copy-start.6
  1.3 0.7 copy-start.7
  1.3 1.4 copy-start
  2.0 0.7 copy-start.4
  2.0 0.7 copy-start.5
  2.0 0.7 copy-start.2
  2.0 0.7 copy-start.3
  193.1 0.7 copy-start.1

commit v5 on v4

--- a/solution.py
+++ b/solution.py
@@ -16,8 +16,8 @@
 RING = 4
 PLANE = 4
 SHARES = RING * 2 * PLANE
-SENDS = 72
-RECEIVES = 181
+SENDS = 60
+RECEIVES = 188
 
 eps_norm = 1e-06
 floor_gap = 1e-05
@@ -45,12 +45,11 @@
     return v * half, slope
 
 
-def minus_expm1(y):
-    poly = jnp.full_like(y, 1.0 / 8.0)
-    poly = 1.0 + y * poly
-    for k in (7, 6, 5, 4, 3, 2):
+def minus_expm1(y, root):
+    poly = 1.0 + y * (1.0 / 7.0)
+    for k in (6, 5, 4, 3, 2):
         poly = 1.0 + y * poly * (1.0 / k)
-    return jnp.where(y > -0.35, -y * poly, 1.0 - jnp.exp(y))
+    return jnp.where(y > -0.35, -y * poly, 1.0 - root * root)
 
 
 def inverse_rms(v):
@@ -97,8 +96,8 @@
     spare = list(range(SENDS))
     sent = []
 
-    def push(src, dst, dev, rsem, pred=None):
-        i = spare.pop(0)
+    def push(src, dst, dev, rsem, pred=None, instead=None):
+        i = spare.pop(0) if instead is None else instead[2]
 
         def make():
             return pltpu.make_async_remote_copy(
@@ -109,19 +108,20 @@
             make().start()
         else:
             pl.when(pred)(lambda: make().start())
-        entry = (make, pred, i)
+        entry = (make, pred, i, instead is None)
         sent.append(entry)
         return entry
 
     def settle(*entries):
         for entry in entries:
-            make, pred, i = entry
+            make, pred, i, owner = entry
             if pred is None:
                 make().wait_send()
             else:
                 pl.when(pred)(lambda make=make: make().wait_send())
             sent.remove(entry)
-            spare.append(i)
+            if owner:
+                spare.append(i)
 
     def arrived(dst, rsem, pred=None):
         def wait():
@@ -197,9 +197,16 @@
             self.out = []
 
         def start(self):
+            self.start_far()
+            self.start_near()
+
+        def start_far(self):
             b, v, s = self.buf, self.recv, self.sems
             self.out.append(push(b.at[pd, self.h0], v.at[0], to_x, s[0]))
             self.out.append(push(b.at[pd, self.h1], v.at[1], to_y, s[1]))
+
+        def start_near(self):
+            b, v, s = self.buf, self.recv, self.sems
             self.out.append(push(b.at[px, self.h0], v.at[2], to_x, s[2]))
             self.out.append(push(b.at[py, self.h1], v.at[3], to_y, s[3]))
 
@@ -232,15 +239,22 @@
             q = pl.ds(o, step)
             return own + v[2 + half, q].astype(f32) + v[4 + half, q].astype(f32)
 
-        def each(self, step, body):
+        def each(self, step, body, init=None):
             for half in (0, 1):
-                loop(self.half, step, lambda o: body(pl.multiple_of(half * self.half + o, step), self.total(half, o, step)))
+
+                def run(j, carry, half=half):
+                    o = pl.multiple_of(j * step, step)
+                    return body(pl.multiple_of(half * self.half + o, step), self.total(half, o, step), carry)
+
+                init = lax.fori_loop(0, self.half // step, run, init)
+            return init
 
     def z_send(src, block, rz):
         out = []
-        for s in (2, 1):
-            out.append(push(src, block(zh), {"zh": zh + s}, rz + zh, zh + s < RING))
-            out.append(push(src, block(zh), {"zh": zh - s}, rz + zh, zh - s >= 0))
+        out.append(push(src, block(zh), {"zh": zh + 2}, rz + zh, zh + 2 < RING))
+        out.append(push(src, block(zh), {"zh": zh - 2}, rz + zh, zh - 2 >= 0, out[-1]))
+        out.append(push(src, block(zh), {"zh": zh + 1}, rz + zh, zh + 1 < RING))
+        out.append(push(src, block(zh), {"zh": zh - 1}, rz + zh, zh - 1 >= 0))
         return out
 
     def z_forward(block, rz):
@@ -248,7 +262,7 @@
         arrived(block(0), rz, zh == last - 1)
         one = push(block(0), block(0), {"zh": zh + 1}, rz, zh == last - 1)
         arrived(block(last), rz + last, zh == 1)
-        two = push(block(last), block(last), {"zh": zh - 1}, rz + last, zh == 1)
+        two = push(block(last), block(last), {"zh": zh - 1}, rz + last, zh == 1, one)
         return [one, two]
 
     def z_wait(block, rz):
@@ -269,9 +283,9 @@
             last = RING - 1
             o = self.out
             o.append(push(b(last), v(1), {"zh": zh + 1}, s + 1, zh == 0))
-            o.append(push(b(0), v(3), {"zh": zh - 1}, s + 3, zh == last))
+            o.append(push(b(0), v(3), {"zh": zh - 1}, s + 3, zh == last, o[-1]))
             o.append(push(b(zh + 2), v(1), {"zh": zh + 2}, s + 1, zh == 0))
-            o.append(push(b(zh - 2), v(3), {"zh": zh - 2}, s + 3, zh == last))
+            o.append(push(b(zh - 2), v(3), {"zh": zh - 2}, s + 3, zh == last, o[-1]))
             o.append(push(b(zh + 1), v(0), {"zh": zh + 1}, s + 0, zh < last))
             o.append(push(b(zh - 1), v(2), {"zh": zh - 1}, s + 2, zh > 0))
 
@@ -290,7 +304,7 @@
             pl.when(zh == 1)(up)
             self.out.append(push(b(last), v(1), {"zh": zh + 2}, s + 1, zh == 1))
             pl.when(zh == last - 1)(down)
-            self.out.append(push(b(0), v(3), {"zh": zh - 2}, s + 3, zh == last - 1))
+            self.out.append(push(b(0), v(3), {"zh": zh - 2}, s + 3, zh == last - 1, self.out[-1]))
 
         def end(self):
             v, s = self.slot, self.sems
@@ -312,6 +326,19 @@
             self.rl, self.ra, self.rz, self.rc = new(), new(), new(4), new()
             self.out = []
 
+        def halves(self):
+            out = []
+            for k in (0, 1):
+                part = Column(self.src, self.raw, self.sorted, self.w, self.R, self.C, 0)
+                part.lanes = pl.ds(self.lanes.start + k * self.C // 2, self.C // 2)
+                out.append(part)
+            return out
+
+        def spread_wait(self):
+            arrived(self.block(zh), self.ra)
+            settle(*self.out)
+            self.out = []
+
         def load(self):
             keep_local(self.src, self.raw, self.rl)
 
@@ -331,8 +358,9 @@
         def block(self, z):
             return self.w.at[z, c, :, self.lanes]
 
-        def z_send(self):
-            arrived(self.block(zh), self.ra)
+        def z_send(self, spread=True):
+            if spread:
+                arrived(self.block(zh), self.ra)
             self.out += z_send(self.block(zh), self.block, self.rz)
 
         def z_forward(self):
@@ -498,20 +526,23 @@
 
         def two(self):
             arrived(r.pr, self.rr)
+            lines = []
+            for at in range(2 * RING):
+                tile = r.pr[at].astype(f32)
+                lines.append(jnp.concatenate([tile[row : row + 1, 0:32] for row in (0, 1, 9, 10)], axis=1))
+            r.line[...] = jnp.concatenate([*lines, jnp.zeros((16 - 2 * RING, 128), f32)], axis=0).astype(bf16)
             for _, dev in plane_peers:
-                self.out.append(push(r.pr, r.pp.at[p], dev, self.rk))
-            keep_local(r.pr, r.pp.at[p], self.rk)
+                self.out.append(push(r.line, r.pp.at[p], dev, self.rk))
+            keep_local(r.line, r.pp.at[p], self.rk)
 
         def three(self):
             arrived(r.pp, self.rk)
-            from_row = lax.broadcasted_iota(jnp.int32, (128, GL), 0)
-            to_lane = lax.broadcasted_iota(jnp.int32, (128, GL), 1)
-            whole = jnp.zeros((2 * RING * 16, GL), f32)
-            for k in range(PLANE):
-                move = ((to_lane == from_row + k * RD) & (from_row < RD)).astype(bf16)
-                whole = whole + dot(r.pp[k].reshape(2 * RING * 16, 128), move)
-            for at in range(2 * RING):
-                r.gains[0:2, at * GL : (at + 1) * GL] = whole[at * 16 : at * 16 + 2]
+            parts = [r.pp[k].astype(f32) for k in range(PLANE)]
+            for row in (0, 1):
+                lanes = slice(row * 32, row * 32 + RD)
+                wide = jnp.concatenate([part[:, lanes] for part in parts], axis=1)
+                for at in range(2 * RING):
+                    r.gains[row : row + 1, at * GL : (at + 1) * GL] = wide[at : at + 1]
             whole = jnp.concatenate([r.pr[at, :, 0:RW].astype(f32) for at in range(2 * RING)], axis=1)
             r.chan[...] = whole[2:10]
             rate = r.pack[...].astype(f32)
@@ -521,12 +552,12 @@
         def four(self):
             where = lax.broadcasted_iota(jnp.int32, (T, 128), 0).astype(f32) + (pos * T).astype(f32)
             for k in range(PLANE):
-                part = r.pp[k, 0].astype(f32)
+                part = r.pp[k].astype(f32)
                 starts, ends = [], []
                 total = jnp.zeros((1, 1), f32)
                 for j in range(dims.SEGS):
                     starts.append(total)
-                    total = total + part[9:10, j : j + 1] * 256.0 + part[10:11, j : j + 1]
+                    total = total + part[0:1, 64 + j : 65 + j] * 256.0 + part[0:1, 96 + j : 97 + j]
                     ends.append(total)
 
                 def seg(shift):
@@ -549,36 +580,23 @@
 
     class SmallGrad:
         def __init__(self):
-            self.rg, self.rp = new(2 * RING), new(PLANE)
+            self.rg = new()
             self.out = []
 
         def one(self):
             for at in range(2 * RING):
                 own = jnp.concatenate([r.gchan[:, at * RW : (at + 1) * RW], jnp.zeros((8, 128 - RW), f32)], axis=1)
-                r.gs[at, 0:8], r.gs[at, 8:16] = r.ggain[:, at * GL : (at + 1) * GL], own
+                r.gs[at] = own
             for at in range(2 * RING):
-                self.out.append(push(r.gs.at[at], r.gg.at[ring], ring_place(at), self.rg + ring, ring != at))
+                self.out.append(push(r.gs.at[at], r.gg.at[ring], ring_place(at), self.rg, ring != at))
+            keep_local(r.gs.at[ring], r.gg.at[ring], self.rg)
 
         def two(self):
-            r.gg[ring] = r.gs[ring]
-            for at in range(2 * RING):
-                arrived(r.gg.at[at], self.rg + at, ring != at)
+            arrived(r.gg, self.rg)
             value = r.gg[0]
             for at in range(1, 2 * RING):
                 value = value + r.gg[at]
             r.small_sum[...] = value
-            r.gp[p] = value[0:8]
-            for _, dev in plane_peers:
-                self.out.append(push(r.gp.at[p], r.gp.at[p], dev, self.rp + p))
-
-        def end(self):
-            for k, _ in plane_peers:
-                arrived(r.gp.at[k], self.rp + k)
-            gains = (r.gp[0] + r.gp[1]) + (r.gp[2] + r.gp[3])
-            from_lane = lax.broadcasted_iota(jnp.int32, (GL, 128), 0)
-            to_lane = lax.broadcasted_iota(jnp.int32, (GL, 128), 1)
-            move = (from_lane == to_lane + p * RD).astype(f32)
-            r.small_sum[0:8] = jnp.dot(gains, move, precision=lax.Precision.HIGHEST)
             deliver(r.small_sum, r.small_out)
             settle(*self.out)
 
@@ -608,6 +626,7 @@
     w_j = Column(r.inject_weight, r.raw_j, r.sort_j, r.w_di, RW, CW, CW)
     w_g = Column(r.mlp_gate, r.raw_g, r.sort_g, r.w_gu, RD, CF, 0)
     w_u = Column(r.mlp_up, r.raw_u, r.sort_u, r.w_gu, RD, CF, CF)
+    w_g1, w_g2 = w_g.halves()
     w_o, w_dn = Row(r.output_weight, r.w_o), Row(r.mlp_down, r.w_dn)
     ag_x, ag_conv, ag_two = Gather(r.x_all), Gather(r.conv), Gather(r.n_two)
     ag_cot, ag_out = Gather(r.cot_all), Gather(r.d_out)
@@ -621,20 +640,20 @@
     for w in (w_i, w_d, w_j, w_b, w_g, w_u):
         w.load()
     w_i.prepare()
+    w_d.prepare()
     pl.semaphore_wait(barrier, len(plane_peers) + places - 1)
     local_wait(*first_loads[0])
     small.one()
+    w_o.z_send()
     w_i.spread()
+    w_d.spread()
     local_wait(*first_loads[1])
     ag_x.start()
     halo_x = new()
     sent_x = push(r.x_all.at[p, pl.ds(T - 16, 16)], r.x_halo.at[p], to_next, halo_x, pos < places - 1)
-    w_d.prepare()
-    w_d.spread()
+    w_j.prepare()
     w_i.z_send()
-    w_o.z_send()
     small.two()
-    w_j.prepare()
     w_b.prepare()
 
     @pl.when(pos == 0)
@@ -645,8 +664,7 @@
     halo_p = new(PLANE)
     sent_p = [push(r.x_halo.at[p], r.x_halo.at[p], dev, halo_p + p) for _, dev in plane_peers]
     ag_x.mid()
-    w_j.spread()
-    w_b.spread()
+    w_i.z_forward()
     w_g.prepare()
     local_wait(*first_loads[2])
     small.three()
@@ -660,12 +678,12 @@
         loop(T, 32, norm_one)
 
     norm_block(p)
-    w_i.z_forward()
+    w_d.z_send()
     ag_x.wait_x()
     norm_block(px)
     ag_x.wait_y()
     norm_block(py)
-    w_d.z_send()
+    w_j.spread()
     small.four()
     for k, _ in plane_peers:
         arrived(r.x_halo.at[k], halo_p + k)
@@ -674,10 +692,12 @@
     ag_x.wait_d()
     norm_block(pd)
     settle(*ag_x.out, sent_x, *sent_p)
+    w_b.spread()
     w_g.spread()
     w_o.z_forward()
     w_i.z_wait()
     w_u.prepare()
+    w_j.z_send()
     w_i.end()
 
     def weight_ib(lanes):
@@ -705,10 +725,10 @@
     loop(T, 16, convolve)
     ag_conv.start()
     w_d.z_forward()
-    w_j.z_send()
+    w_b.z_send()
     ag_conv.mid()
+    w_j.z_forward()
     w_d.z_wait()
-    w_b.z_send()
     w_d.end()
 
     def pre(q, lanes):
@@ -719,34 +739,33 @@
     r.pair[:, 0:CW] += pre(px, lanes_a)
     ag_conv.wait_y()
     r.pair[:, 0:CW] += pre(py, lanes_a)
-    w_j.z_forward()
+    w_b.z_forward()
     ag_conv.wait_d()
     r.pair[:, 0:CW] += pre(pd, lanes_a)
     settle(*ag_conv.out)
+    w_g.spread_wait()
+    w_g1.z_send(False)
+    w_j.z_wait()
     w_u.spread()
     ag_cot.start()
-    w_b.z_forward()
-    w_g.z_send()
-    w_j.z_wait()
     w_o.z_wait()
     w_j.end()
-    r.pair[:, CW : 2 * CW] = pre(0, lanes_b)
-    for q in range(1, PLANE):
-        r.pair[:, CW : 2 * CW] += pre(q, lanes_b)
+    r.pair[:, CW : 2 * CW] = (pre(0, lanes_b) + pre(1, lanes_b)) + (pre(2, lanes_b) + pre(3, lanes_b))
 
     def decay_terms(s, rg):
         log_a = -rate_scale * rg * r.chan[7:8]
-        gap = minus_expm1(2.0 * log_a)
+        root = jnp.exp(log_a)
+        gap = minus_expm1(2.0 * log_a, root)
         first = wide(0, s)
-        return log_a, gap, jnp.where(first, 1.0, jnp.sqrt(jnp.maximum(gap, floor_gap))), first
+        return root, gap, jnp.where(first, 1.0, jnp.sqrt(jnp.maximum(gap, floor_gap))), first
 
     def gates_two(o):
         s = pl.ds(o, 16)
         rg = jax.nn.sigmoid(r.pair[s, 0:CW] + r.chan[5:6])
         ig = jax.nn.sigmoid(r.pair[s, CW : 2 * CW] + r.chan[6:7])
-        log_a, _, mult, first = decay_terms(s, rg)
+        root, _, mult, first = decay_terms(s, rg)
         r.rgate[s], r.igate[s] = rg, ig
-        r.decay[s] = jnp.where(first, 0.0, jnp.exp(log_a))
+        r.decay[s] = jnp.where(first, 0.0, root)
         r.work[s] = mult * ig * r.conv[p, s].astype(f32)
 
     loop(M, 16, gates_two)
@@ -774,10 +793,10 @@
         r.own_f[k : k + 1] = ends[2 * k + 1]
         r.own_f[PLANE + k : PLANE + k + 1] = ends[2 * k]
     carry_f.send_core()
-    ag_cot.mid()
+    w_b.z_wait()
     carry_f.send()
-    w_b.z_wait()
-    w_g.z_forward()
+    w_g1.z_forward()
+    w_g2.z_send(False)
     w_b.end()
     r.work[...] = dot(r.n_one[...].reshape(M, D), weight_ib(lanes_b))
 
@@ -786,9 +805,8 @@
         r.gated[s], r.slope[s] = gelu_parts(r.work[s])
 
     loop(M, 16, gates_one)
-    w_o.end()
+    ag_cot.mid()
     carry_f.fold(r.into)
-    w_u.z_send()
     for k in range(PLANE):
         r.state[k, 0:8] = jnp.broadcast_to(r.into[k : k + 1], (8, CW))
 
@@ -801,6 +819,8 @@
 
     loop(T, 16, mix)
 
+    w_o.end()
+
     def out_part(o):
         q = pl.ds(o, step)
         r.part[:, :, q] = dot(r.mixed[...], r.w_o[:, :, :, q].reshape(CW, step)).astype(bf16).reshape(PLANE, T, step)
@@ -808,25 +828,27 @@
     loop(D, step, out_part)
     rs_one = Scatter(r.part, r.got_one)
     rs_one.start()
+    w_g1.z_wait()
+    w_g2.z_forward()
+    w_u.z_send()
     ag_cot.end()
-    w_g.z_wait()
     rs_one.mid()
-    w_u.z_forward()
-    w_dn.z_send()
     rs_one.end()
 
-    def norm_two(o, summed):
-        s = pl.ds(o, 16)
+    def norm_two(o, summed, _):
+        s = pl.ds(o, 32)
         v = r.x_all[p, s].astype(f32) + summed
         r.x_one[s] = v
         r.n_two[p, s] = (v * inverse_rms(v) * r.gains[1:2]).astype(bf16)
 
-    rs_one.each(16, norm_two)
+    rs_one.each(32, norm_two)
     ag_two.start()
+    w_u.z_forward()
+    w_dn.z_send()
     ag_two.mid()
-    w_u.z_wait()
-    w_g.end()
-    w_dn.z_forward()
+    w_g2.z_wait()
+    w_g1.end()
+    w_g2.end()
     ag_two.end()
 
     def mlp_in(o):
@@ -834,6 +856,8 @@
         r.pair[:, q] = dot(r.n_two[...].reshape(M, D), r.w_gu[:, :, :, q].reshape(D, step))
 
     loop(CF, step, mlp_in)
+    w_dn.z_forward()
+    w_u.z_wait()
     w_u.end()
     loop(CF, step, lambda o: mlp_in(pl.multiple_of(CF + o, step)))
 
@@ -846,7 +870,6 @@
         r.pair[s, CF : 2 * CF] = value
 
     loop(M, 16, gates_mlp)
-    w_dn.z_wait()
 
     half = CF // 2
     for k in (0, 1):
@@ -857,6 +880,8 @@
             )
     g_dn = RowsGrad(r.g_dn, r.h_dn, r.z_dn, r.t_dn, r.grad_mlp_down)
     g_dn.core_send()
+    w_dn.z_wait()
+    g_dn.z_send()
     w_dn.end()
 
     for k in range(CF // step):
@@ -876,7 +901,6 @@
     lax.fori_loop(0, RING, d_two_part, 0)
     rs_two = Scatter(r.part, r.got_two)
     rs_two.start()
-    g_dn.z_send()
 
     def grad_gate_up(lane0):
         lanes = pl.ds(lane0, CF)
@@ -893,39 +917,42 @@
     g_g = ColumnsGrad(r.w_gu, r.h_gu, r.z_gu, r.l_gu, RD, 0, CF, r.grads_gu)
     g_g.core_send()
     rs_two.mid()
-    grad_gate_up(CF)
-    g_u = ColumnsGrad(r.w_gu, r.h_gu, r.z_gu, r.l_gu, RD, CF, CF, r.grads_gu)
-    g_u.core_send()
     g_dn.z_forward()
     g_g.z_send()
+    grad_gate_up(CF)
+    g_u, g_v = (
+        ColumnsGrad(r.w_gu, r.h_gu, r.z_gu, r.l_gu, RD, lane0, CF // 2, r.grads_gu) for lane0 in (CF, CF + CF // 2)
+    )
+    g_u.core_send()
+    g_v.core_send()
 
     def act_part(o):
         q = pl.ds(o, step)
         r.part_act[:, :, q] = dot(r.hidden[...], r.w_dn[:, :, :, q].reshape(CF, step)).astype(bf16).reshape(PLANE, T, step)
 
     loop(D, step, act_part)
-    r.ggain[...] = jnp.zeros_like(r.ggain)
     r.gchan[...] = jnp.zeros_like(r.gchan)
     rs_two.end()
 
-    def norm_two_back(o, d_two):
-        s = pl.ds(o, 16)
+    def norm_two_back(o, d_two, _):
+        s = pl.ds(o, 32)
         v = r.x_one[s]
         rs = inverse_rms(v)
         z = v * rs
         dz = d_two * r.gains[1:2]
-        r.ggain[1:2] += jnp.sum(d_two * z, axis=0, keepdims=True)
         d_one = r.cot_all[p, s].astype(f32) + rs * (dz - z * jnp.mean(dz * z, axis=-1, keepdims=True))
         r.d_one[s] = d_one
         r.d_out[p, s] = d_one.astype(bf16)
 
-    rs_two.each(16, norm_two_back)
+    rs_two.each(32, norm_two_back)
     ag_out.start()
+    g_g.z_forward()
+    g_u.z_send()
     ag_out.mid()
-    g_g.z_forward()
     ag_out.end()
     rs_act = Scatter(r.part_act, r.got_act)
     rs_act.start()
+    g_u.z_forward()
 
     r.work[...] = dot_nt(r.d_out[...].reshape(M, D), r.w_o[...].reshape(CW, D))
 
@@ -970,6 +997,7 @@
     g_o = RowsGrad(r.w_o, r.h_o, r.z_o, r.t_o, r.grad_output_weight)
     g_o.core_send()
     carry_b.send()
+    g_v.z_send()
     rs_act.mid()
 
     def d_branch_part(z, _):
@@ -988,7 +1016,7 @@
     g_b.core_send()
     g_g.plane_send()
     carry_b.fold(r.into)
-    g_u.z_send()
+    g_b.z_send()
 
     def back(o):
         sums = [jnp.zeros((1, CW), f32)] * 2
@@ -1012,24 +1040,26 @@
 
     loop(T, 16, back)
 
-    def conv_part(q, _):
+    def conv_part(q):
         r.part_conv[q] = dot_nt(r.d_pre[...], r.w_di[:, :, ds(q * RW, RW, 16), :].reshape(CW, 2 * CW)).astype(bf16)
-        return 0
-
-    lax.fori_loop(0, RING, conv_part, 0)
+
+    rs_conv = Scatter(r.part_conv, r.got_conv)
+    conv_part(pd)
     rs_act.end()
-    rs_conv = Scatter(r.part_conv, r.got_conv)
-    rs_conv.start()
-
-    def finish_act(o, summed):
+    rs_conv.start_far()
+    conv_part(px)
+    conv_part(py)
+    rs_conv.start_near()
+    conv_part(p)
+    g_v.z_forward()
+
+    def finish_act(o, summed, _):
         s = pl.ds(o, 16)
         r.act[s] = (r.x_one[s] + summed).astype(bf16)
 
     rs_act.each(16, finish_act)
     deliver(r.act, r.activations)
     g_o.z_send()
-    g_b.z_send()
-    g_u.z_forward()
     g_dn.end()
 
     def grad_dec_inj(lanes):
@@ -1041,13 +1071,14 @@
         lax.fori_loop(0, RING, run, 0)
 
     grad_dec_inj(lanes_a)
-    g_d = ColumnsGrad(r.w_di, r.h_di, r.z_di, r.l_di, RW, 0, CW, r.grads_di)
+    g_d = ColumnsGrad(r.w_di, r.h_di, r.z_di, r.l_di, RW, 0, CW - 128, r.grads_di)
     g_d.core_send()
     rs_conv.mid()
     grad_dec_inj(lanes_b)
-    g_j = ColumnsGrad(r.w_di, r.h_di, r.z_di, r.l_di, RW, CW, CW, r.grads_di)
+    g_j = ColumnsGrad(r.w_di, r.h_di, r.z_di, r.l_di, RW, CW - 128, CW + 128, r.grads_di)
     g_j.core_send()
     g_b.z_forward()
+    g_d.z_send()
     rs_conv.end()
 
     for half in (0, 1):
@@ -1062,7 +1093,7 @@
     for k in range(PLANE):
         r.halo_out[4 * k : 4 * k + 4] = r.d_conv[k, 0:4]
     sent_b = push(r.halo_out, r.halo_in, to_prev, halo_b, pos > 0)
-    g_d.z_send()
+    g_o.z_forward()
 
     def taps_back(o):
         sums = [jnp.zeros((1, CW), f32)] * 5
@@ -1079,12 +1110,14 @@
             r.gchan[j : j + 1] += sums[j]
 
     loop(T, 16, taps_back)
+    small_grad.one()
 
     @pl.when(pos == places - 1)
     def _():
         r.halo_in[...] = jnp.zeros((16, CW), f32)
 
     arrived(r.halo_in, halo_b, pos < places - 1)
+    g_d.z_forward()
     g_j.z_send()
     for k in range(PLANE):
         r.d_conv[k, T : T + 8] = jnp.concatenate([r.halo_in[4 * k : 4 * k + 4], jnp.zeros((4, CW), f32)], axis=0)
@@ -1120,38 +1153,35 @@
     g_i = ColumnsGrad(r.w_ib, r.h_ib, r.z_ib, r.l_ib, RD, 0, CW, r.grads_ib)
     g_i.core_send()
     rs_three.mid()
-    g_o.z_forward()
+    g_j.z_forward()
     g_i.z_send()
     g_u.plane_send()
-    g_d.z_forward()
-    g_b.plane_send()
+    g_v.plane_send()
     rs_three.end()
 
-    def norm_one_back(o, d_n):
-        s = pl.ds(o, 16)
+    def norm_one_back(o, d_n, _):
+        s = pl.ds(o, 32)
         v = r.x_all[p, s].astype(f32)
         rs = inverse_rms(v)
         z = v * rs
         dz = d_n * r.gains[0:1]
-        r.ggain[0:1] += jnp.sum(d_n * z, axis=0, keepdims=True)
         r.d_x[s] = r.d_one[s] + rs * (dz - z * jnp.mean(dz * z, axis=-1, keepdims=True))
 
-    rs_three.each(16, norm_one_back)
+    rs_three.each(32, norm_one_back)
     deliver(r.d_x, r.d_tokens)
-    small_grad.one()
     settle(sent_b)
-    g_j.z_forward()
+    g_g.end()
+    g_b.plane_send()
+    g_o.end()
+    g_u.end()
+    g_v.end()
     g_i.z_forward()
-    g_g.end()
-    g_u.end()
     g_d.plane_send()
-    g_o.end()
-    small_grad.two()
     g_b.end()
     g_j.plane_send()
     g_i.plane_send()
+    small_grad.two()
     g_d.end()
-    small_grad.end()
     g_j.end()
     g_i.end()
     assert not sent
@@ -1187,7 +1217,7 @@
         "grads_gu": ((PLANE, RD, 2 * CF), bf16),
         "grad_output_weight": ((RW, D), f32),
         "grad_mlp_down": ((RF, D), f32),
-        "small_out": ((16, 128), f32),
+        "small_out": ((8, 128), f32),
     }
     columns = (("i", RD, CW), ("b", RD, CW), ("d", RW, CW), ("j", RW, CW), ("g", RD, CF), ("u", RD, CF))
     scratch = {
@@ -1249,19 +1279,18 @@
         "masks": ((7, M, 128), f32),
         "pack": ((16, 128), bf16),
         "pr": ((2 * RING, 16, 128), bf16),
-        "pp": ((PLANE, 2 * RING, 16, 128), bf16),
+        "line": ((16, 128), bf16),
+        "pp": ((PLANE, 16, 128), bf16),
         "act": ((T, D), bf16),
         "d_x": ((T, D), f32),
         "t_o": ((RW, D), f32),
         "t_dn": ((RF, D), f32),
-        "small_sum": ((16, 128), f32),
+        "small_sum": ((8, 128), f32),
         "gains": ((8, D), f32),
         "chan": ((8, CW), f32),
-        "ggain": ((8, D), f32),
         "gchan": ((8, CW), f32),
-        "gs": ((2 * RING, 16, 128), f32),
-        "gg": ((2 * RING, 16, 128), f32),
-        "gp": ((PLANE, 8, GL), f32),
+        "gs": ((2 * RING, 8, 128), f32),
+        "gg": ((2 * RING, 8, 128), f32),
     }
     dims = SimpleNamespace(
         T=T, D=D, W=W, F=F, CW=CW, CF=CF, RD=RD, RW=RW, RF=RF, NL=NL, SEGS=SEGS, receives=RECEIVES + 2 * RING * NL, names=[*ins, *outs, *scratch, "ss", "rs"]
@@ -1280,30 +1309,38 @@
         cost_estimate=pl.CostEstimate(flops=flops, bytes_accessed=8 * 2**20, transcendentals=M * CW * 16),
         name="griffin_layer",
     )(tokens, cotangent, pack, *[weights[name] for name in WEIGHTS])
-    return finish(dict(zip(outs, results, strict=True)), PLANE, CW, CF)
-
-
-def finish(got, blocks, CW, CF):
+    return finish({**dict(zip(outs, results, strict=True)), "pack": pack}, weights, CW, CF)
+
+
+def finish(got, weights, CW, CF):
     hbm = pl.BlockSpec(memory_space=pl.ANY)
     pairs = (
-        ("grads_ib", ("grad_input_weight", "grad_branch_weight"), CW),
-        ("grads_di", ("grad_decay_weight", "grad_inject_weight"), CW),
-        ("grads_gu", ("grad_mlp_gate", "grad_mlp_up"), CF),
+        ("grads_ib", ("input_weight", "branch_weight"), CW),
+        ("grads_gu", ("mlp_gate", "mlp_up"), CF),
+        ("grads_di", ("decay_weight", "inject_weight"), CW),
     )
+    gains = ("first_gain", "second_gain")
+    RD, RW = got["grads_ib"].shape[1], got["grads_di"].shape[1]
+    channels = {"conv_taps": (0, 4), "conv_bias": (4, 5), "decay_bias": (5, 6), "inject_bias": (6, 7)}
     plain = ("d_tokens", "activations", "grad_output_weight", "grad_mlp_down")
-    names = [*[name for name, _, _ in pairs], *plain]
+    shared = [name for _, names, _ in pairs[:2] for name in names]
+    source = {**got, **{name: weights[name] for name in shared}}
+    names = ["small_out", "pack", *[name for name, _, _ in pairs], *shared, *plain]
     shapes = {name: got[name] for name in plain}
-    for name, outs, C in pairs:
-        for out in outs:
-            shapes[out] = jax.ShapeDtypeStruct((got[name].shape[1], blocks * C), f32)
-    scratch = [pltpu.VMEM(got[name].shape, got[name].dtype) for name in names]
-    scratch += [pltpu.VMEM(shapes[out].shape, f32) for _, outs, _ in pairs for out in outs]
-    count = 2 * len(plain) + 3 * len(pairs)
+    for name, targets, C in pairs:
+        for target in targets:
+            shapes["grad_" + target] = jax.ShapeDtypeStruct((got[name].shape[1], PLANE * C), f32)
+    for name in gains:
+        shapes["grad_" + name] = jax.ShapeDtypeStruct((1, RD), f32)
+    for name, (low, high) in channels.items():
+        shapes["grad_" + name] = jax.ShapeDtypeStruct((high - low, RW), f32)
+    scratch = {name: (source[name].shape, source[name].dtype) for name in names}
+    scratch.update({name: (like.shape, f32) for name, like in shapes.items() if name not in plain})
 
     def body(*refs):
         ins = dict(zip(names, refs[: len(names)], strict=True))
         outs = dict(zip(shapes, refs[len(names) : len(names) + len(shapes)], strict=True))
-        held, sems = refs[len(names) + len(shapes) : -1], refs[-1]
+        held, sems = dict(zip(scratch, refs[len(names) + len(shapes) : -1], strict=True)), refs[-1]
         copies = []
 
         def copy(src, dst):
@@ -1311,21 +1348,42 @@
             copies[-1].start()
             return copies[-1]
 
-        loads = [copy(ins[name], held[i]) for i, name in enumerate(names)]
+        loads = {name: copy(ins[name], held[name]) for name in names}
         stores = []
-        for i, (_, targets, C) in enumerate(pairs):
-            loads[i].wait()
+        loads["small_out"].wait()
+        loads["pack"].wait()
+        for name, (low, high) in channels.items():
+            held["grad_" + name][...] = held["small_out"][low:high, 0:RW]
+            stores.append(copy(held["grad_" + name], outs["grad_" + name]))
+        for i, (name, targets, C) in enumerate(pairs):
+            loads[name].wait()
+            part, sums = C // (2 * RING), None
             for j, target in enumerate(targets):
-                wide = held[len(names) + 2 * i + j]
-                part = C // (2 * RING)
-                values = [held[i][k, :, j * C : (j + 1) * C].astype(f32) for k in range(blocks)]
-                wide[...] = jnp.concatenate(
+                values = [held[name][k, :, j * C : (j + 1) * C].astype(f32) for k in range(PLANE)]
+                wide = jnp.concatenate(
                     [value[:, g * part : (g + 1) * part] for g in range(2 * RING) for value in values], axis=1
                 )
-                stores.append(copy(wide, outs[target]))
-        for i, name in enumerate(plain):
-            loads[len(pairs) + i].wait()
-            stores.append(copy(held[len(pairs) + i], outs[name]))
+                held["grad_" + target][...] = wide
+                stores.append(copy(held["grad_" + target], outs["grad_" + target]))
+                if target in shared:
+                    loads[target].wait()
+                    product = wide * held[target][...].astype(f32)
+                    lanes = sum(product[:, k * 128 : (k + 1) * 128] for k in range(product.shape[1] // 128))
+                    sums = lanes if sums is None else sums + lanes
+            if sums is not None:
+                total = lax.dot_general(
+                    jnp.ones((8, 128), f32),
+                    sums,
+                    (((1,), (1,)), ((), ())),
+                    precision=lax.Precision.HIGHEST,
+                    preferred_element_type=f32,
+                )
+                target = "grad_" + gains[i]
+                held[target][...] = total[0:1] / held["pack"][...].astype(f32)[i : i + 1, 0:RD]
+                stores.append(copy(held[target], outs[target]))
+        for name in plain:
+            loads[name].wait()
+            stores.append(copy(held[name], outs[name]))
         for store in stores:
             store.wait()
 
@@ -1334,10 +1392,13 @@
         out_shape=[jax.ShapeDtypeStruct(like.shape, like.dtype) for like in shapes.values()],
         in_specs=[hbm] * len(names),
         out_specs=[hbm] * len(shapes),
-        scratch_shapes=[*scratch, pltpu.SemaphoreType.DMA((count,))],
+        scratch_shapes=[
+            *[pltpu.VMEM(shape, kind) for shape, kind in scratch.values()],
+            pltpu.SemaphoreType.DMA((len(names) + len(shapes),)),
+        ],
         compiler_params=pltpu.CompilerParams(vmem_limit_bytes=62 * 2**20),
         name="finish",
-    )(*[got[name] for name in names])
+    )(*[source[name] for name in names])
     return {**got, **dict(zip(shapes, results, strict=True))}
 
 
@@ -1410,18 +1471,18 @@
         return lax.psum_scatter(whole, AXES, scatter_dimension=axis, tiled=True).astype(f32)
 
     grads = [returned(got["grad_" + name]) for name in WEIGHTS]
-    gain_sum = returned(got["small_out"][:2, :RD], 1)
-    chan_sum = returned(got["small_out"][8:15, :RW], 1)
+    first, second, taps, *biases = (
+        returned(got["grad_" + name], 1)
+        for name in ("first_gain", "second_gain", "conv_taps", "conv_bias", "decay_bias", "inject_bias")
+    )
     return (
         got["activations"][None],
         got["d_tokens"][None],
         *grads,
-        gain_sum[0],
-        gain_sum[1],
-        chan_sum[:4].T,
-        chan_sum[4],
-        chan_sum[5],
-        chan_sum[6],
+        first[0],
+        second[0],
+        taps.T,
+        *[bias[0] for bias in biases],
     )
 
 

time: 199 us -> 185 us (0.930)
  Pallas kernels: 193 us -> 181 us
  local copies, waits for them, and re-layouts: 4.46 us -> 2.15 us
    pallas_call x1, Pallas kernels: 190 us -> 178 us  [run_layer(): pl.pallas_call(partial(layer, dims), out_shape=[jax.ShapeDtypeStruct(shap...]
where the time goes in v5:
time: 185 us
  Pallas kernels  181 us (98%)
  local copies, waits for them, and re-layouts  2.15 us (1%)
    pallas_call x1, Pallas kernels, run_layer(): pl.pallas_call(partial(layer, dims), out_shape=[jax.ShapeDtypeStruct(shap...  178 us
    pallas_call x1, Pallas kernels, finish(): pl.pallas_call(body, out_shape=[jax.ShapeDtypeStruct(like.shape, like.dty...  3.85 us

profile of v5, /device:TPU:0, one launch (start us, length us, event | category | flops | bytes accessed | tf_op | source)
XLA Modules:
  0.0 185.1 jit_solution(2948690901197309074)
XLA Ops:
  0.7 0.0 copy-start.7
  0.7 0.6 copy-done.7
  1.3 0.0 copy-start.5
  1.3 0.0 copy-start.6
  1.3 0.0 copy-start
  1.3 0.6 copy-done.5
  2.0 0.0 copy-done.6
  2.0 0.0 copy-start.3
  2.0 0.0 copy-start.4
  2.0 0.0 copy-start.1
  2.0 0.0 copy-start.2
  2.0 0.6 copy-done.3
  2.7 0.0 copy-done.4
  2.7 0.0 copy-done.1
  2.7 0.0 copy-done.2
  2.7 0.0 copy-done
  2.7 0.1 reshape.38
  2.9 0.1 convert_element_type.16
  2.9 0.6 fusion.6.refs_2_.refs_1_
  3.5 177.6 %griffin_layer.1 = (bf16[128,1024]{1,0:T(8,128)(2,1)}, f32[128,1024]{1,0:T(8,128)}, bf16[4,32,768]{2,1,0:T(8,128)(2,1)}, bf16[4,48,768]{2,1,0:T(8,128)(2,1)}, bf...) custom-call(bf16[128,1024]{1,0:T(8,128)(2,1)} %bitcast.23, ...), custom_call_target="tpu_custom_call" | custom-call | flops 14495514624 | bytes 8388608 | tf_op jit(solution)/shard_map/griffin_layer/pallas_call | solution.py:1299
  181.1 3.8 %finish.1 = (f32[128,1024]{1,0:T(8,128)}, bf16[128,1024]{1,0:T(8,128)(2,1)}, f32[48,1024]{1,0:T(8,128)}, f32[96,1024]{1,0:T(8,128)}, f32[32,1536]{1,0:T(8,128)},...) custom-call(f32[8,128]{1,0:T(8,128)} %get-tuple-element.40.refs_0_, ...), custom_call_target="tpu_custom_call" | custom-call | tf_op jit(solution)/shard_map/finish/pallas_call | solution.py:1390
  (4 shorter events, 0.1 us)
Async XLA Ops:
  0.7 0.7 copy-start.7
  1.3 0.7 copy-start.5
  1.3 0.7 copy-start.6
  1.3 1.4 copy-start
  2.0 0.7 copy-start.3
  2.0 0.7 copy-start.4
  2.0 0.7 copy-start.1
  2.0 0.7 copy-start.2

commit v6 on v5

--- a/solution.py
+++ b/solution.py
@@ -1,6 +1,6 @@
 import itertools
 import math
-from functools import partial
+from functools import cached_property, partial
 from types import SimpleNamespace
 
 import jax
@@ -17,7 +17,7 @@
 PLANE = 4
 SHARES = RING * 2 * PLANE
 SENDS = 60
-RECEIVES = 188
+RECEIVES = 174
 
 eps_norm = 1e-06
 floor_gap = 1e-05
@@ -137,13 +137,16 @@
     def keep_local(src, dst, rsem):
         pltpu.make_async_copy(src, dst, r.rs.at[rsem]).start()
 
+    idle = []
+
     def local_wait(src, dst, rsem):
         pltpu.make_async_copy(src, dst, r.rs.at[rsem]).wait()
+        idle.append(rsem)
 
     results = []
 
     def deliver(src, dst):
-        sem = new()
+        sem = idle.pop() if idle else new()
         keep_local(src, dst, sem)
         results.append((src, dst, sem))
 
@@ -273,8 +276,9 @@
         arrived(block(last), rz + last, (zh == 0) | (zh == last - 1))
 
     class ZSum:
-        def __init__(self, block, slot, add):
-            self.block, self.slot, self.add = block, slot, add
+        def __init__(self, block, slot, add, direct):
+            self.block, self.slot, self.add, self.direct = block, slot, add, direct
+            self.valid = (direct | (zh >= 1), zh >= 2, direct | (zh <= 2), zh <= 1)
             self.sems = new(4)
             self.out = []
 
@@ -282,10 +286,16 @@
             b, v, s = self.block, self.slot, self.sems
             last = RING - 1
             o = self.out
-            o.append(push(b(last), v(1), {"zh": zh + 1}, s + 1, zh == 0))
-            o.append(push(b(0), v(3), {"zh": zh - 1}, s + 3, zh == last, o[-1]))
-            o.append(push(b(zh + 2), v(1), {"zh": zh + 2}, s + 1, zh == 0))
-            o.append(push(b(zh - 2), v(3), {"zh": zh - 2}, s + 3, zh == last, o[-1]))
+            if self.direct:
+                o.append(push(b(last), v(2), {"zh": zh + last}, s + 2, zh == 0))
+                o.append(push(b(0), v(0), {"zh": zh - last}, s + 0, zh == last, o[-1]))
+                o.append(push(b(zh + 2), v(1), {"zh": zh + 2}, s + 1, zh <= 1))
+                o.append(push(b(zh - 2), v(3), {"zh": zh - 2}, s + 3, zh >= 2, o[-1]))
+            else:
+                o.append(push(b(last), v(1), {"zh": zh + 1}, s + 1, zh == 0))
+                o.append(push(b(0), v(3), {"zh": zh - 1}, s + 3, zh == last, o[-1]))
+                o.append(push(b(zh + 2), v(1), {"zh": zh + 2}, s + 1, zh == 0))
+                o.append(push(b(zh - 2), v(3), {"zh": zh - 2}, s + 3, zh == last, o[-1]))
             o.append(push(b(zh + 1), v(0), {"zh": zh + 1}, s + 0, zh < last))
             o.append(push(b(zh - 1), v(2), {"zh": zh - 1}, s + 2, zh > 0))
 
@@ -307,15 +317,12 @@
             self.out.append(push(b(0), v(3), {"zh": zh - 2}, s + 3, zh == last - 1, self.out[-1]))
 
         def end(self):
-            v, s = self.slot, self.sems
-            arrived(v(0), s, zh >= 1)
-            arrived(v(1), s + 1, zh >= 2)
-            arrived(v(2), s + 2, zh <= 2)
-            arrived(v(3), s + 3, zh <= 1)
+            for k, valid in enumerate(self.valid):
+                arrived(self.slot(k), self.sems + k, valid)
             settle(*self.out)
 
         def total(self, own, parts):
-            for part, pred in zip(parts, (zh >= 1, zh >= 2, zh <= 2, zh <= 1), strict=True):
+            for part, pred in zip(parts, self.valid, strict=True):
                 own = own + jnp.where(pred, part.astype(f32), 0.0)
             return own
 
@@ -323,8 +330,12 @@
         def __init__(self, src, raw, sorted_, w, R, C, lane0):
             self.src, self.raw, self.sorted = src, raw, sorted_
             self.w, self.R, self.C, self.lanes = w, R, C, pl.ds(lane0, C)
-            self.rl, self.ra, self.rz, self.rc = new(), new(), new(4), new()
             self.out = []
+
+        rl = cached_property(lambda self: new())
+        ra = cached_property(lambda self: new())
+        rz = cached_property(lambda self: new(4))
+        rc = cached_property(lambda self: new())
 
         def halves(self):
             out = []
@@ -378,7 +389,6 @@
     class Row(Column):
         def __init__(self, src, w):
             self.src, self.w, self.lanes = src, w, pl.ds(0, w.shape[3])
-            self.ra, self.rz, self.rc = new(), new(4), new()
             self.out = []
 
         def z_send(self):
@@ -386,17 +396,17 @@
             self.out += z_send(self.src, self.block, self.rz)
 
         def z_wait(self):
-            local_wait(self.src, self.block(zh), self.ra)
+            pltpu.make_async_copy(self.src, self.block(zh), r.rs.at[self.ra]).wait()
             super().z_wait()
 
     class ColumnsGrad:
-        def __init__(self, g, other, slots, land, R, lane0, lanes, result):
+        def __init__(self, g, other, slots, land, R, lane0, lanes, result, direct=False):
             self.g, self.other, self.slots, self.land = g, other, slots, land
             self.R, self.lanes, self.result = R, pl.ds(lane0, lanes), result
             self.rows = PLANE * R
             self.rc, self.rl = new(), new()
             self.zsum = ZSum(
-                lambda z: g.at[z, c, :, self.lanes], lambda k: slots.at[k, :, self.lanes], self.add_slot
+                lambda z: g.at[z, c, :, self.lanes], lambda k: slots.at[k, :, self.lanes], self.add_slot, direct
             )
 
         def add_slot(self, z, k):
@@ -519,6 +529,16 @@
             self.rr, self.rk = new(), new()
             self.out = []
 
+        def pack(self):
+            for load in small_loads:
+                local_wait(*load)
+            lengths = r.lens[...]
+            rows = [r.gain_a[...], r.gain_b[...], r.taps[...], r.bias_a[...], r.bias_b[...], r.bias_c[...]]
+            rows += [lax.shift_right_logical(lengths, 8), lengths & 255]
+            rows = [row.astype(f32) for row in rows]
+            rows = [jnp.concatenate([row, jnp.zeros((row.shape[0], 128 - row.shape[1]), f32)], axis=1) for row in rows]
+            r.pack[...] = jnp.concatenate([*rows, jnp.zeros((5, 128), f32)], axis=0).astype(bf16)
+
         def one(self):
             for at in range(2 * RING):
                 self.out.append(push(r.pack, r.pr.at[ring], ring_place(at), self.rr, ring != at))
@@ -545,9 +565,13 @@
                     r.gains[row : row + 1, at * GL : (at + 1) * GL] = wide[at : at + 1]
             whole = jnp.concatenate([r.pr[at, :, 0:RW].astype(f32) for at in range(2 * RING)], axis=1)
             r.chan[...] = whole[2:10]
-            rate = r.pack[...].astype(f32)
-            for k in range(CW // 128):
-                r.chan[7:8, k * 128 : (k + 1) * 128] = jnp.exp2(-rate[11 + k : 12 + k])
+            rates = r.rates[...].astype(f32)
+            rates = jnp.concatenate([rates[k : k + 1] for k in range(W // 128)], axis=1)
+            mine = jnp.zeros((1, CW), f32)
+            for k in range(PLANE):
+                at = [(g * PLANE + k) * RW for g in range(2 * RING)]
+                mine = jnp.where(p == k, jnp.concatenate([rates[:, o : o + RW] for o in at], axis=1), mine)
+            r.chan[7:8] = jnp.exp2(-mine)
 
         def four(self):
             where = lax.broadcasted_iota(jnp.int32, (T, 128), 0).astype(f32) + (pos * T).astype(f32)
@@ -612,12 +636,24 @@
     first_loads = [
         (src, dst, new())
         for src, dst in (
-            (r.pack_in, r.pack),
             (r.tokens, r.x_all.at[p]),
             (r.cotangent, r.cot_all.at[p]),
         )
     ]
-    for load in first_loads:
+    small_loads = [
+        (src, dst, new())
+        for src, dst in (
+            (r.first_gain, r.gain_a),
+            (r.second_gain, r.gain_b),
+            (r.conv_taps, r.taps),
+            (r.conv_bias, r.bias_a),
+            (r.decay_bias, r.bias_b),
+            (r.inject_bias, r.bias_c),
+            (r.doc_lengths, r.lens),
+            (r.decay_exponent, r.rates),
+        )
+    ]
+    for load in small_loads + first_loads:
         keep_local(*load)
 
     w_i = Column(r.input_weight, r.raw_i, r.sort_i, r.w_ib, RD, CW, 0)
@@ -639,15 +675,15 @@
 
     for w in (w_i, w_d, w_j, w_b, w_g, w_u):
         w.load()
+    small.pack()
     w_i.prepare()
     w_d.prepare()
     pl.semaphore_wait(barrier, len(plane_peers) + places - 1)
-    local_wait(*first_loads[0])
     small.one()
     w_o.z_send()
     w_i.spread()
     w_d.spread()
-    local_wait(*first_loads[1])
+    local_wait(*first_loads[0])
     ag_x.start()
     halo_x = new()
     sent_x = push(r.x_all.at[p, pl.ds(T - 16, 16)], r.x_halo.at[p], to_next, halo_x, pos < places - 1)
@@ -666,7 +702,7 @@
     ag_x.mid()
     w_i.z_forward()
     w_g.prepare()
-    local_wait(*first_loads[2])
+    local_wait(*first_loads[1])
     small.three()
 
     def norm_block(k):
@@ -946,13 +982,12 @@
 
     rs_two.each(32, norm_two_back)
     ag_out.start()
+    ag_out.mid()
     g_g.z_forward()
     g_u.z_send()
-    ag_out.mid()
     ag_out.end()
     rs_act = Scatter(r.part_act, r.got_act)
     rs_act.start()
-    g_u.z_forward()
 
     r.work[...] = dot_nt(r.d_out[...].reshape(M, D), r.w_o[...].reshape(CW, D))
 
@@ -997,6 +1032,7 @@
     g_o = RowsGrad(r.w_o, r.h_o, r.z_o, r.t_o, r.grad_output_weight)
     g_o.core_send()
     carry_b.send()
+    g_u.z_forward()
     g_v.z_send()
     rs_act.mid()
 
@@ -1116,9 +1152,9 @@
     def _():
         r.halo_in[...] = jnp.zeros((16, CW), f32)
 
-    arrived(r.halo_in, halo_b, pos < places - 1)
     g_d.z_forward()
     g_j.z_send()
+    arrived(r.halo_in, halo_b, pos < places - 1)
     for k in range(PLANE):
         r.d_conv[k, T : T + 8] = jnp.concatenate([r.halo_in[4 * k : 4 * k + 4], jnp.zeros((4, CW), f32)], axis=0)
 
@@ -1150,7 +1186,7 @@
         return 0
 
     lax.fori_loop(0, RING, grad_input, 0)
-    g_i = ColumnsGrad(r.w_ib, r.h_ib, r.z_ib, r.l_ib, RD, 0, CW, r.grads_ib)
+    g_i = ColumnsGrad(r.w_ib, r.h_ib, r.z_ib, r.l_ib, RD, 0, CW, r.grads_ib, True)
     g_i.core_send()
     rs_three.mid()
     g_j.z_forward()
@@ -1175,7 +1211,6 @@
     g_o.end()
     g_u.end()
     g_v.end()
-    g_i.z_forward()
     g_d.plane_send()
     g_b.end()
     g_j.plane_send()
@@ -1201,97 +1236,106 @@
 )
 
 
-def run_layer(NL, SEGS, tokens, cotangent, pack, weights):
+def run_layer(NL, tokens, cotangent, small, weights):
     T, D = tokens.shape
+    SEGS = small["doc_lengths"].shape[1]
     W, F = weights["branch_weight"].shape[1], weights["mlp_gate"].shape[1]
     CW, CF = W // PLANE, F // PLANE
     RD, RW, RF = D // SHARES, W // SHARES, F // SHARES
     GL, M, places = PLANE * RD, PLANE * T, RING * NL * 2
     hbm = pl.BlockSpec(memory_space=pl.ANY)
-    ins = ["tokens", "cotangent", "pack_in", *WEIGHTS]
-    outs = {
-        "activations": ((T, D), bf16),
-        "d_tokens": ((T, D), f32),
-        "grads_ib": ((PLANE, RD, 2 * CW), bf16),
-        "grads_di": ((PLANE, RW, 2 * CW), bf16),
-        "grads_gu": ((PLANE, RD, 2 * CF), bf16),
-        "grad_output_weight": ((RW, D), f32),
-        "grad_mlp_down": ((RF, D), f32),
-        "small_out": ((8, 128), f32),
-    }
+    ins = ["tokens", "cotangent", *small, *WEIGHTS]
+    outs = dict(
+        activations=((T, D), bf16),
+        d_tokens=((T, D), f32),
+        grads_ib=((PLANE, RD, 2 * CW), bf16),
+        grads_di=((PLANE, RW, 2 * CW), bf16),
+        grads_gu=((PLANE, RD, 2 * CF), bf16),
+        grad_output_weight=((RW, D), f32),
+        grad_mlp_down=((RF, D), f32),
+        small_out=((8, 128), f32),
+    )
     columns = (("i", RD, CW), ("b", RD, CW), ("d", RW, CW), ("j", RW, CW), ("g", RD, CF), ("u", RD, CF))
-    scratch = {
-        "w_ib": ((RING, 2, PLANE * RD, 2 * CW), bf16),
-        "w_di": ((RING, 2, PLANE * RW, 2 * CW), bf16),
-        "w_gu": ((RING, 2, PLANE * RD, 2 * CF), bf16),
-        "w_o": ((RING, 2, RW, D), bf16),
-        "w_dn": ((RING, 2, RF, D), bf16),
+    scratch = dict(
+        w_ib=((RING, 2, PLANE * RD, 2 * CW), bf16),
+        w_di=((RING, 2, PLANE * RW, 2 * CW), bf16),
+        w_gu=((RING, 2, PLANE * RD, 2 * CF), bf16),
+        w_o=((RING, 2, RW, D), bf16),
+        w_dn=((RING, 2, RF, D), bf16),
         **{"raw_" + n: ((R, PLANE * C), bf16) for n, R, C in columns},
         **{"sort_" + n: ((PLANE, R, C), bf16) for n, R, C in columns},
-        "h_ib": ((RING, PLANE * RD, 2 * CW), bf16),
-        "h_di": ((RING, PLANE * RW, 2 * CW), bf16),
-        "h_gu": ((RING, PLANE * RD, 2 * CF), bf16),
-        "h_o": ((RING, RW, D), bf16),
-        "h_dn": ((RING, RF, D), bf16),
-        "z_ib": ((4, PLANE * RD, 2 * CW), bf16),
-        "z_di": ((4, PLANE * RW, 2 * CW), bf16),
-        "z_gu": ((4, PLANE * RD, 2 * CF), bf16),
-        "z_o": ((4, RW, D), bf16),
-        "z_dn": ((4, RF, D), bf16),
-        "l_ib": ((PLANE, RD, 2 * CW), bf16),
-        "l_di": ((PLANE, RW, 2 * CW), bf16),
-        "l_gu": ((PLANE, RD, 2 * CF), bf16),
-        "n_one": ((PLANE, T, D), bf16),
-        "n_two": ((PLANE, T, D), bf16),
-        "cot_all": ((PLANE, T, D), bf16),
-        "d_out": ((PLANE, T, D), bf16),
-        "conv": ((PLANE, M, CW), bf16),
-        "part": ((PLANE, T, D), bf16),
-        "part_act": ((PLANE, T, D), bf16),
-        "part_conv": ((PLANE, M, CW), bf16),
-        "got_one": ((6, T // 2, D), bf16),
-        "got_two": ((6, T // 2, D), bf16),
-        "got_three": ((6, T // 2, D), bf16),
-        "got_act": ((6, T // 2, D), bf16),
-        "got_conv": ((6, M // 2, CW), bf16),
-        "mixed": ((M, CW), bf16),
-        "hidden": ((M, CF), bf16),
-        "d_pair": ((M, 2 * CF), bf16),
-        "d_gu": ((M, 2 * CW), bf16),
-        "d_pre": ((M, 2 * CW), bf16),
-        "pair": ((M, 2 * CF), f32),
-        "u": ((PLANE, T + 8, CW), f32),
-        "state": ((PLANE, T + 8, CW), f32),
-        "d_conv": ((PLANE, T + 8, CW), f32),
+        h_ib=((RING, PLANE * RD, 2 * CW), bf16),
+        h_di=((RING, PLANE * RW, 2 * CW), bf16),
+        h_gu=((RING, PLANE * RD, 2 * CF), bf16),
+        h_o=((RING, RW, D), bf16),
+        h_dn=((RING, RF, D), bf16),
+        z_ib=((4, PLANE * RD, 2 * CW), bf16),
+        z_di=((4, PLANE * RW, 2 * CW), bf16),
+        z_gu=((4, PLANE * RD, 2 * CF), bf16),
+        z_o=((4, RW, D), bf16),
+        z_dn=((4, RF, D), bf16),
+        l_ib=((PLANE, RD, 2 * CW), bf16),
+        l_di=((PLANE, RW, 2 * CW), bf16),
+        l_gu=((PLANE, RD, 2 * CF), bf16),
+        n_one=((PLANE, T, D), bf16),
+        n_two=((PLANE, T, D), bf16),
+        cot_all=((PLANE, T, D), bf16),
+        d_out=((PLANE, T, D), bf16),
+        conv=((PLANE, M, CW), bf16),
+        part=((PLANE, T, D), bf16),
+        part_act=((PLANE, T, D), bf16),
+        part_conv=((PLANE, M, CW), bf16),
+        got_one=((6, T // 2, D), bf16),
+        got_two=((6, T // 2, D), bf16),
+        got_three=((6, T // 2, D), bf16),
+        got_act=((6, T // 2, D), bf16),
+        got_conv=((6, M // 2, CW), bf16),
+        mixed=((M, CW), bf16),
+        hidden=((M, CF), bf16),
+        d_pair=((M, 2 * CF), bf16),
+        d_gu=((M, 2 * CW), bf16),
+        d_pre=((M, 2 * CW), bf16),
+        pair=((M, 2 * CF), f32),
+        u=((PLANE, T + 8, CW), f32),
+        state=((PLANE, T + 8, CW), f32),
+        d_conv=((PLANE, T + 8, CW), f32),
         **{name: ((M, CW), f32) for name in ("gated", "slope", "rgate", "igate", "decay", "work", "cum")},
-        "x_one": ((T, D), f32),
-        "d_one": ((T, D), f32),
-        "carry_f": ((RING * NL, 2 * PLANE, CW), f32),
-        "carry_b": ((RING * NL, 2 * PLANE, CW), f32),
+        x_one=((T, D), f32),
+        d_one=((T, D), f32),
+        carry_f=((RING * NL, 2 * PLANE, CW), f32),
+        carry_b=((RING * NL, 2 * PLANE, CW), f32),
         **{name: ((2 * PLANE, CW), f32) for name in ("own_f", "sib_f", "own_b", "sib_b")},
-        "halo_out": ((16, CW), f32),
-        "halo_in": ((16, CW), f32),
-        "into": ((8, CW), f32),
-        "x_all": ((PLANE, T, D), bf16),
-        "x_halo": ((PLANE, 16, D), bf16),
-        "n_halo": ((PLANE, 16, D), bf16),
-        "g_dn": ((RING, 2, RF, D), bf16),
-        "masks": ((7, M, 128), f32),
-        "pack": ((16, 128), bf16),
-        "pr": ((2 * RING, 16, 128), bf16),
-        "line": ((16, 128), bf16),
-        "pp": ((PLANE, 16, 128), bf16),
-        "act": ((T, D), bf16),
-        "d_x": ((T, D), f32),
-        "t_o": ((RW, D), f32),
-        "t_dn": ((RF, D), f32),
-        "small_sum": ((8, 128), f32),
-        "gains": ((8, D), f32),
-        "chan": ((8, CW), f32),
-        "gchan": ((8, CW), f32),
-        "gs": ((2 * RING, 8, 128), f32),
-        "gg": ((2 * RING, 8, 128), f32),
-    }
+        halo_out=((16, CW), f32),
+        halo_in=((16, CW), f32),
+        into=((8, CW), f32),
+        x_all=((PLANE, T, D), bf16),
+        x_halo=((PLANE, 16, D), bf16),
+        n_halo=((PLANE, 16, D), bf16),
+        g_dn=((RING, 2, RF, D), bf16),
+        masks=((7, M, 128), f32),
+        pack=((16, 128), bf16),
+        gain_a=((1, RD), bf16),
+        gain_b=((1, RD), bf16),
+        taps=((4, RW), bf16),
+        bias_a=((1, RW), bf16),
+        bias_b=((1, RW), bf16),
+        bias_c=((1, RW), bf16),
+        lens=((1, SEGS), jnp.int32),
+        rates=((W // 128, 128), jnp.int32),
+        pr=((2 * RING, 16, 128), bf16),
+        line=((16, 128), bf16),
+        pp=((PLANE, 16, 128), bf16),
+        act=((T, D), bf16),
+        d_x=((T, D), f32),
+        t_o=((RW, D), f32),
+        t_dn=((RF, D), f32),
+        small_sum=((8, 128), f32),
+        gains=((8, D), f32),
+        chan=((8, CW), f32),
+        gchan=((8, CW), f32),
+        gs=((2 * RING, 8, 128), f32),
+        gg=((2 * RING, 8, 128), f32),
+    )
     dims = SimpleNamespace(
         T=T, D=D, W=W, F=F, CW=CW, CF=CF, RD=RD, RW=RW, RF=RF, NL=NL, SEGS=SEGS, receives=RECEIVES + 2 * RING * NL, names=[*ins, *outs, *scratch, "ss", "rs"]
     )
@@ -1299,7 +1343,7 @@
     results = pl.pallas_call(
         partial(layer, dims),
         out_shape=[jax.ShapeDtypeStruct(shape, kind) for shape, kind in outs.values()],
-        in_specs=[hbm] * (3 + len(WEIGHTS)),
+        in_specs=[hbm] * len(ins),
         out_specs=[hbm] * len(outs),
         scratch_shapes=[pltpu.VMEM(shape, kind) for shape, kind in scratch.values()]
         + [pltpu.SemaphoreType.DMA((SENDS,)), pltpu.SemaphoreType.DMA((dims.receives,))],
@@ -1308,8 +1352,8 @@
         ),
         cost_estimate=pl.CostEstimate(flops=flops, bytes_accessed=8 * 2**20, transcendentals=M * CW * 16),
         name="griffin_layer",
-    )(tokens, cotangent, pack, *[weights[name] for name in WEIGHTS])
-    return finish({**dict(zip(outs, results, strict=True)), "pack": pack}, weights, CW, CF)
+    )(tokens, cotangent, *small.values(), *[weights[name] for name in WEIGHTS])
+    return finish({**small, **dict(zip(outs, results, strict=True))}, weights, CW, CF)
 
 
 def finish(got, weights, CW, CF):
@@ -1325,7 +1369,7 @@
     plain = ("d_tokens", "activations", "grad_output_weight", "grad_mlp_down")
     shared = [name for _, names, _ in pairs[:2] for name in names]
     source = {**got, **{name: weights[name] for name in shared}}
-    names = ["small_out", "pack", *[name for name, _, _ in pairs], *shared, *plain]
+    names = ["small_out", *gains, *[name for name, _, _ in pairs], *shared, *plain]
     shapes = {name: got[name] for name in plain}
     for name, targets, C in pairs:
         for target in targets:
@@ -1351,7 +1395,6 @@
         loads = {name: copy(ins[name], held[name]) for name in names}
         stores = []
         loads["small_out"].wait()
-        loads["pack"].wait()
         for name, (low, high) in channels.items():
             held["grad_" + name][...] = held["small_out"][low:high, 0:RW]
             stores.append(copy(held["grad_" + name], outs["grad_" + name]))
@@ -1379,7 +1422,8 @@
                     preferred_element_type=f32,
                 )
                 target = "grad_" + gains[i]
-                held[target][...] = total[0:1] / held["pack"][...].astype(f32)[i : i + 1, 0:RD]
+                loads[gains[i]].wait()
+                held[target][...] = total[0:1] / held[gains[i]][...].astype(f32)
                 stores.append(copy(held[target], outs[target]))
         for name in plain:
             loads[name].wait()
@@ -1424,7 +1468,6 @@
     inject_bias,
 ):
     devices = math.prod(sizes.values())
-    width = branch_weight.shape[1]
     at = {name: lax.axis_index(name) for name in AXES}
     mine = at["yl"] * 2 + at["xl"]
     ring = at["zh"] * 2 + at["c"]
@@ -1438,19 +1481,16 @@
         size = whole.shape[axis] // SHARES
         return lax.dynamic_slice_in_dim(whole, share * size, size, axis)
 
-    def rows(value):
-        value = value.astype(bf16)
-        return jnp.pad(value, ((0, 0), (0, 128 - value.shape[1])))
-
-    gains = pooled(jnp.stack([first_gain, second_gain]), 1)
-    chan = pooled(jnp.concatenate([conv_taps.T, jnp.stack([conv_bias, decay_bias, inject_bias])]), 1)
-    RD, RW = gains.shape[1], chan.shape[1]
-    rates = decay_exponent.reshape(2 * RING, PLANE, width // SHARES)
-    rates = lax.dynamic_index_in_dim(rates, mine, 1, keepdims=False).reshape(-1, 128)
-    lengths = jnp.concatenate([doc_lengths // 256, doc_lengths % 256])
-    pack = jnp.concatenate([rows(gains), rows(chan), rows(lengths), rows(rates)])
-    pack = jnp.pad(pack, ((0, 16 - pack.shape[0]), (0, 0)))
-
+    small = dict(
+        first_gain=pooled(first_gain[None], 1),
+        second_gain=pooled(second_gain[None], 1),
+        conv_taps=pooled(conv_taps.T, 1),
+        conv_bias=pooled(conv_bias[None], 1),
+        decay_bias=pooled(decay_bias[None], 1),
+        inject_bias=pooled(inject_bias[None], 1),
+        doc_lengths=doc_lengths,
+        decay_exponent=decay_exponent.reshape(-1, 128),
+    )
     weights = dict(
         zip(
             WEIGHTS,
@@ -1459,7 +1499,7 @@
         )
     )
     weights = {name: pooled(value) for name, value in weights.items()}
-    got = run_layer(sizes["zl"], doc_lengths.shape[1], tokens[0], cotangent[0], pack, weights)
+    got = run_layer(sizes["zl"], tokens[0], cotangent[0], small, weights)
 
     def returned(value, axis=0):
         if groups == 1:

time: 185 us -> 182 us (0.984)
  local copies, waits for them, and re-layouts: 2.15 us -> 0 us
    unnamed x16 -> x0, local copies, waits for them, and re-layouts: 1.98 us -> none
where the time goes in v6:
time: 182 us
  Pallas kernels  181 us (99%)
    pallas_call x1, Pallas kernels, run_layer(): pl.pallas_call(partial(layer, dims), out_shape=[jax.ShapeDtypeStruct(shap...  177 us
    pallas_call x1, Pallas kernels, finish(): pl.pallas_call(body, out_shape=[jax.ShapeDtypeStruct(like.shape, like.dty...  3.91 us

profile of v6, /device:TPU:0, one launch (start us, length us, event | category | flops | bytes accessed | tf_op | source)
XLA Modules:
  0.0 181.6 jit_solution(8493158735445597641)
XLA Ops:
  0.7 176.9 %griffin_layer.1 = (bf16[128,1024]{1,0:T(8,128)(2,1)}, f32[128,1024]{1,0:T(8,128)}, bf16[4,32,768]{2,1,0:T(8,128)(2,1)}, bf16[4,48,768]{2,1,0:T(8,128)(2,1)}, bf...) custom-call(bf16[128,1024]{1,0:T(8,128)(2,1)} %bitcast.22, ...), custom_call_target="tpu_custom_call" | custom-call | flops 14495514624 | bytes 8388608 | tf_op jit(solution)/shard_map/griffin_layer/pallas_call | solution.py:1343
  177.5 3.9 %finish.1 = (f32[128,1024]{1,0:T(8,128)}, bf16[128,1024]{1,0:T(8,128)(2,1)}, f32[48,1024]{1,0:T(8,128)}, f32[96,1024]{1,0:T(8,128)}, f32[32,1536]{1,0:T(8,128)},...) custom-call(f32[8,128]{1,0:T(8,128)} %get-tuple-element.40.refs_0_, ...), custom_call_target="tpu_custom_call" | custom-call | tf_op jit(solution)/shard_map/finish/pallas_call | solution.py:1434

commit v7 on v6

--- a/solution.py
+++ b/solution.py
@@ -16,8 +16,8 @@
 RING = 4
 PLANE = 4
 SHARES = RING * 2 * PLANE
-SENDS = 60
-RECEIVES = 174
+SENDS = 57
+RECEIVES = 180
 
 eps_norm = 1e-06
 floor_gap = 1e-05
@@ -54,6 +54,11 @@
 
 def inverse_rms(v):
     return lax.rsqrt(jnp.mean(v * v, axis=-1, keepdims=True) + eps_norm)
+
+
+def unsorted(parts):
+    size = parts[0].shape[1] // (2 * RING)
+    return jnp.concatenate([part[:, g * size : (g + 1) * size] for g in range(2 * RING) for part in parts], axis=1)
 
 
 def loop(total, step, body):
@@ -252,12 +257,14 @@
                 init = lax.fori_loop(0, self.half // step, run, init)
             return init
 
-    def z_send(src, block, rz):
+    def z_send(src, block, rz, away=(2, 1)):
         out = []
-        out.append(push(src, block(zh), {"zh": zh + 2}, rz + zh, zh + 2 < RING))
-        out.append(push(src, block(zh), {"zh": zh - 2}, rz + zh, zh - 2 >= 0, out[-1]))
-        out.append(push(src, block(zh), {"zh": zh + 1}, rz + zh, zh + 1 < RING))
-        out.append(push(src, block(zh), {"zh": zh - 1}, rz + zh, zh - 1 >= 0))
+        if 2 in away:
+            out.append(push(src, block(zh), {"zh": zh + 2}, rz + zh, zh + 2 < RING))
+            out.append(push(src, block(zh), {"zh": zh - 2}, rz + zh, zh - 2 >= 0, out[-1]))
+        if 1 in away:
+            out.append(push(src, block(zh), {"zh": zh + 1}, rz + zh, zh + 1 < RING))
+            out.append(push(src, block(zh), {"zh": zh - 1}, rz + zh, zh - 1 >= 0))
         return out
 
     def z_forward(block, rz):
@@ -268,12 +275,19 @@
         two = push(block(last), block(last), {"zh": zh - 1}, rz + last, zh == 1, one)
         return [one, two]
 
-    def z_wait(block, rz):
+    def z_wait(block, rz, use):
         last = RING - 1
-        arrived(block(0), rz, (zh == 1) | (zh == last))
-        arrived(block(1), rz + 1, zh != 1)
-        arrived(block(2), rz + 2, zh != 2)
-        arrived(block(last), rz + last, (zh == 0) | (zh == last - 1))
+
+        def take(k, pred, waited=None, instead=None):
+            arrived(block(k), rz + k, pred if waited is None else pred & ~waited)
+            return use(block(k), pred, instead)
+
+        out = [take(zh - 1, zh >= 1), take(zh + 1, zh < last)]
+        out.append(take(zh - 2, zh >= 2, zh == last - 1))
+        out.append(take(zh + 2, zh <= 1, zh == 1, out[-1]))
+        out.append(take(0, zh == last))
+        out.append(take(last, zh == 0, None, out[-1]))
+        return out
 
     class ZSum:
         def __init__(self, block, slot, add, direct):
@@ -373,14 +387,16 @@
             if spread:
                 arrived(self.block(zh), self.ra)
             self.out += z_send(self.block(zh), self.block, self.rz)
+            self.out.append(self.core_push(self.block(zh)))
 
         def z_forward(self):
             self.out += z_forward(self.block, self.rz)
 
+        def core_push(self, block, pred=None, instead=None):
+            return push(block, block, to_core, self.rc, pred, instead)
+
         def z_wait(self):
-            z_wait(self.block, self.rz)
-            half = self.w.at[:, c, :, self.lanes]
-            self.out.append(push(half, half, to_core, self.rc))
+            self.out += z_wait(self.block, self.rz, self.core_push)
 
         def end(self):
             arrived(self.w.at[:, 1 - c, :, self.lanes], self.rc)
@@ -391,18 +407,20 @@
             self.src, self.w, self.lanes = src, w, pl.ds(0, w.shape[3])
             self.out = []
 
-        def z_send(self):
-            keep_local(self.src, self.block(zh), self.ra)
-            self.out += z_send(self.src, self.block, self.rz)
+        def z_send(self, away=(2, 1)):
+            if 2 in away:
+                keep_local(self.src, self.block(zh), self.ra)
+            self.out += z_send(self.src, self.block, self.rz, away)
 
         def z_wait(self):
             pltpu.make_async_copy(self.src, self.block(zh), r.rs.at[self.ra]).wait()
+            self.out.append(self.core_push(self.block(zh)))
             super().z_wait()
 
     class ColumnsGrad:
-        def __init__(self, g, other, slots, land, R, lane0, lanes, result, direct=False):
+        def __init__(self, g, other, slots, land, R, lane0, lanes, direct=False):
             self.g, self.other, self.slots, self.land = g, other, slots, land
-            self.R, self.lanes, self.result = R, pl.ds(lane0, lanes), result
+            self.R, self.lanes = R, pl.ds(lane0, lanes)
             self.rows = PLANE * R
             self.rc, self.rl = new(), new()
             self.zsum = ZSum(
@@ -423,9 +441,10 @@
                 self.g.at[:, 1 - c, :, self.lanes], self.other.at[:, :, self.lanes], to_core, self.rc
             )
 
-        def z_send(self):
+        def core_sum(self):
             g, q = self.g, self.lanes
             arrived(self.other.at[:, :, q], self.rc)
+            settle(self.pushed)
             for z in range(RING):
 
                 def add(o):
@@ -433,6 +452,9 @@
                     g[z, c, s, q] = (g[z, c, s, q].astype(f32) + self.other[z, s, q].astype(f32)).astype(bf16)
 
                 loop(self.rows, 16, add)
+
+        def z_send(self):
+            self.core_sum()
             self.zsum.send()
 
         def z_forward(self):
@@ -449,7 +471,7 @@
 
             loop(PLANE * R, 16, add)
             dst = self.land.at[p, :, q]
-            self.out = [self.pushed]
+            self.out = []
             for k, dev in plane_peers:
                 self.out.append(push(g.at[zh, c, ds(k * R, R, 16), q], dst, dev, self.rl))
             keep_local(g.at[zh, c, ds(p * R, R, 16), q], dst, self.rl)
@@ -457,16 +479,49 @@
         def end(self):
             arrived(self.land.at[:, :, self.lanes], self.rl)
             settle(*self.out)
-            deliver(self.land.at[:, :, self.lanes], self.result.at[:, :, self.lanes])
+
+    def in_order(land, lane0, C, held, result):
+        held[...] = unsorted([land[k, :, lane0 : lane0 + C].astype(f32) for k in range(PLANE)])
+        deliver(held, result)
+
+    class LastGrad(ColumnsGrad):
+        def __init__(self, g, other, stage, slots, R, lane0, lanes, total, result):
+            super().__init__(g, other, slots, None, R, lane0, lanes)
+            self.stage, self.sum, self.result = stage, total, result
+            self.zsum.block, self.zsum.slot = (lambda z: stage.at[:, z]), (lambda k: slots.at[k])
+
+        def add_slot(self, z, k):
+            for q in range(PLANE):
+                self.stage[q, z] = (self.stage[q, z].astype(f32) + self.slots[k, q].astype(f32)).astype(bf16)
+
+        def plane_send(self):
+            R, dst = self.R, self.stage.at[p]
+            self.core_sum()
+            self.out = []
+            for k, dev in plane_peers:
+                self.out.append(push(self.g.at[:, c, ds(k * R, R, 16), self.lanes], dst, dev, self.rl))
+            keep_local(self.g.at[:, c, ds(p * R, R, 16), self.lanes], dst, self.rl)
+
+        def z_send(self):
+            arrived(self.stage, self.rl)
+            self.zsum.send()
+
+        def end(self):
+            self.zsum.end()
+            settle(*self.out)
+            values = [
+                self.zsum.total(self.stage[q, zh].astype(f32), [self.slots[k, q] for k in range(4)]) for q in range(PLANE)
+            ]
+            self.sum[...] = unsorted(values)
+            deliver(self.sum, self.result)
 
     class RowsGrad(ColumnsGrad):
         def __init__(self, g, other, slots, total, result):
-            super().__init__(g, other, slots, None, 0, 0, g.shape[3], result)
-            self.rows, self.sum = g.shape[2], total
+            super().__init__(g, other, slots, None, 0, 0, g.shape[3])
+            self.rows, self.sum, self.result = g.shape[2], total, result
 
         def end(self):
             self.zsum.end()
-            settle(self.pushed)
 
             def add(o):
                 s = pl.ds(o, 16)
@@ -680,13 +735,13 @@
     w_d.prepare()
     pl.semaphore_wait(barrier, len(plane_peers) + places - 1)
     small.one()
-    w_o.z_send()
+    local_wait(*first_loads[0])
+    halo_x = new()
+    sent_x = push(r.x_all.at[p, pl.ds(T - 16, 16)], r.x_halo.at[p], to_next, halo_x, pos < places - 1)
+    w_o.z_send((2,))
     w_i.spread()
     w_d.spread()
-    local_wait(*first_loads[0])
     ag_x.start()
-    halo_x = new()
-    sent_x = push(r.x_all.at[p, pl.ds(T - 16, 16)], r.x_halo.at[p], to_next, halo_x, pos < places - 1)
     w_j.prepare()
     w_i.z_send()
     small.two()
@@ -701,6 +756,7 @@
     sent_p = [push(r.x_halo.at[p], r.x_halo.at[p], dev, halo_p + p) for _, dev in plane_peers]
     ag_x.mid()
     w_i.z_forward()
+    w_o.z_send((1,))
     w_g.prepare()
     local_wait(*first_loads[1])
     small.three()
@@ -761,9 +817,9 @@
     loop(T, 16, convolve)
     ag_conv.start()
     w_d.z_forward()
-    w_b.z_send()
     ag_conv.mid()
     w_j.z_forward()
+    w_b.z_send()
     w_d.z_wait()
     w_d.end()
 
@@ -880,10 +936,11 @@
     rs_one.each(32, norm_two)
     ag_two.start()
     w_u.z_forward()
+    ag_two.mid()
     w_dn.z_send()
-    ag_two.mid()
     w_g2.z_wait()
     w_g1.end()
+    w_u.z_wait()
     w_g2.end()
     ag_two.end()
 
@@ -893,7 +950,6 @@
 
     loop(CF, step, mlp_in)
     w_dn.z_forward()
-    w_u.z_wait()
     w_u.end()
     loop(CF, step, lambda o: mlp_in(pl.multiple_of(CF + o, step)))
 
@@ -916,8 +972,8 @@
             )
     g_dn = RowsGrad(r.g_dn, r.h_dn, r.z_dn, r.t_dn, r.grad_mlp_down)
     g_dn.core_send()
+    g_dn.z_send()
     w_dn.z_wait()
-    g_dn.z_send()
     w_dn.end()
 
     for k in range(CF // step):
@@ -950,14 +1006,14 @@
         lax.fori_loop(0, RING, run, 0)
 
     grad_gate_up(0)
-    g_g = ColumnsGrad(r.w_gu, r.h_gu, r.z_gu, r.l_gu, RD, 0, CF, r.grads_gu)
+    g_g = ColumnsGrad(r.w_gu, r.h_gu, r.z_gu, r.l_gu, RD, 0, CF)
     g_g.core_send()
     rs_two.mid()
     g_dn.z_forward()
     g_g.z_send()
     grad_gate_up(CF)
     g_u, g_v = (
-        ColumnsGrad(r.w_gu, r.h_gu, r.z_gu, r.l_gu, RD, lane0, CF // 2, r.grads_gu) for lane0 in (CF, CF + CF // 2)
+        ColumnsGrad(r.w_gu, r.h_gu, r.z_gu, r.l_gu, RD, lane0, CF // 2) for lane0 in (CF, CF + CF // 2)
     )
     g_u.core_send()
     g_v.core_send()
@@ -1048,11 +1104,11 @@
         return 0
 
     lax.fori_loop(0, RING, d_branch_part, 0)
-    g_b = ColumnsGrad(r.w_ib, r.h_ib, r.z_ib, r.l_ib, RD, CW, CW, r.grads_ib)
+    g_b = ColumnsGrad(r.w_ib, r.h_ib, r.z_ib, r.l_ib, RD, CW, CW)
     g_b.core_send()
     g_g.plane_send()
     carry_b.fold(r.into)
-    g_b.z_send()
+    g_o.z_send()
 
     def back(o):
         sums = [jnp.zeros((1, CW), f32)] * 2
@@ -1095,7 +1151,7 @@
 
     rs_act.each(16, finish_act)
     deliver(r.act, r.activations)
-    g_o.z_send()
+    g_b.z_send()
     g_dn.end()
 
     def grad_dec_inj(lanes):
@@ -1107,13 +1163,17 @@
         lax.fori_loop(0, RING, run, 0)
 
     grad_dec_inj(lanes_a)
-    g_d = ColumnsGrad(r.w_di, r.h_di, r.z_di, r.l_di, RW, 0, CW - 128, r.grads_di)
+    g_d = ColumnsGrad(r.w_di, r.h_di, r.z_di, r.l_di, RW, 0, CW - 128)
     g_d.core_send()
     rs_conv.mid()
     grad_dec_inj(lanes_b)
-    g_j = ColumnsGrad(r.w_di, r.h_di, r.z_di, r.l_di, RW, CW - 128, CW + 128, r.grads_di)
+    g_j, g_k = (
+        ColumnsGrad(r.w_di, r.h_di, r.z_di, r.l_di, RW, lane0, lanes)
+        for lane0, lanes in ((CW - 128, 256), (CW + 128, CW - 128))
+    )
     g_j.core_send()
-    g_b.z_forward()
+    g_k.core_send()
+    g_o.z_forward()
     g_d.z_send()
     rs_conv.end()
 
@@ -1129,7 +1189,7 @@
     for k in range(PLANE):
         r.halo_out[4 * k : 4 * k + 4] = r.d_conv[k, 0:4]
     sent_b = push(r.halo_out, r.halo_in, to_prev, halo_b, pos > 0)
-    g_o.z_forward()
+    g_b.z_forward()
 
     def taps_back(o):
         sums = [jnp.zeros((1, CW), f32)] * 5
@@ -1186,14 +1246,20 @@
         return 0
 
     lax.fori_loop(0, RING, grad_input, 0)
-    g_i = ColumnsGrad(r.w_ib, r.h_ib, r.z_ib, r.l_ib, RD, 0, CW, r.grads_ib, True)
+    g_i = LastGrad(r.w_ib, r.h_ib, r.st_i, r.z_i, RD, 0, CW, r.t_i, r.grad_input_weight)
     g_i.core_send()
+    g_j.z_forward()
+    g_k.z_send()
     rs_three.mid()
-    g_j.z_forward()
-    g_i.z_send()
+    g_i.plane_send()
+    g_k.z_forward()
     g_u.plane_send()
     g_v.plane_send()
     rs_three.end()
+    g_i.z_send()
+    g_b.plane_send()
+    g_d.plane_send()
+    g_j.plane_send()
 
     def norm_one_back(o, d_n, _):
         s = pl.ds(o, 32)
@@ -1206,18 +1272,22 @@
     rs_three.each(32, norm_one_back)
     deliver(r.d_x, r.d_tokens)
     settle(sent_b)
+    g_i.z_forward()
+    g_k.plane_send()
     g_g.end()
-    g_b.plane_send()
-    g_o.end()
+    in_order(r.l_gu, 0, CF, r.t_g, r.grad_mlp_gate)
     g_u.end()
     g_v.end()
-    g_d.plane_send()
+    in_order(r.l_gu, CF, CF, r.t_u, r.grad_mlp_up)
     g_b.end()
-    g_j.plane_send()
-    g_i.plane_send()
+    in_order(r.l_ib, CW, CW, r.t_b, r.grad_branch_weight)
+    g_o.end()
     small_grad.two()
     g_d.end()
     g_j.end()
+    in_order(r.l_di, 0, CW, r.t_d, r.grad_decay_weight)
+    g_k.end()
+    in_order(r.l_di, CW, CW, r.t_j, r.grad_inject_weight)
     g_i.end()
     assert not sent
     for result in results:
@@ -1248,10 +1318,13 @@
     outs = dict(
         activations=((T, D), bf16),
         d_tokens=((T, D), f32),
-        grads_ib=((PLANE, RD, 2 * CW), bf16),
-        grads_di=((PLANE, RW, 2 * CW), bf16),
-        grads_gu=((PLANE, RD, 2 * CF), bf16),
+        grad_input_weight=((RD, W), f32),
+        grad_branch_weight=((RD, W), f32),
+        grad_decay_weight=((RW, W), f32),
+        grad_inject_weight=((RW, W), f32),
         grad_output_weight=((RW, D), f32),
+        grad_mlp_gate=((RD, F), f32),
+        grad_mlp_up=((RD, F), f32),
         grad_mlp_down=((RF, D), f32),
         small_out=((8, 128), f32),
     )
@@ -1327,6 +1400,14 @@
         pp=((PLANE, 16, 128), bf16),
         act=((T, D), bf16),
         d_x=((T, D), f32),
+        t_i=((RD, W), f32),
+        t_b=((RD, W), f32),
+        st_i=((PLANE, RING, RD, CW), bf16),
+        z_i=((4, PLANE, RD, CW), bf16),
+        t_d=((RW, W), f32),
+        t_j=((RW, W), f32),
+        t_g=((RD, F), f32),
+        t_u=((RD, F), f32),
         t_o=((RW, D), f32),
         t_dn=((RF, D), f32),
         small_sum=((8, 128), f32),
@@ -1353,28 +1434,21 @@
         cost_estimate=pl.CostEstimate(flops=flops, bytes_accessed=8 * 2**20, transcendentals=M * CW * 16),
         name="griffin_layer",
     )(tokens, cotangent, *small.values(), *[weights[name] for name in WEIGHTS])
-    return finish({**small, **dict(zip(outs, results, strict=True))}, weights, CW, CF)
-
-
-def finish(got, weights, CW, CF):
+    return finish({**small, **dict(zip(outs, results, strict=True))}, weights)
+
+
+def finish(got, weights):
     hbm = pl.BlockSpec(memory_space=pl.ANY)
-    pairs = (
-        ("grads_ib", ("input_weight", "branch_weight"), CW),
-        ("grads_gu", ("mlp_gate", "mlp_up"), CF),
-        ("grads_di", ("decay_weight", "inject_weight"), CW),
-    )
-    gains = ("first_gain", "second_gain")
-    RD, RW = got["grads_ib"].shape[1], got["grads_di"].shape[1]
+    behind = {"first_gain": ("input_weight", "branch_weight"), "second_gain": ("mlp_gate", "mlp_up")}
+    RD, RW = got["grad_input_weight"].shape[0], got["grad_decay_weight"].shape[0]
     channels = {"conv_taps": (0, 4), "conv_bias": (4, 5), "decay_bias": (5, 6), "inject_bias": (6, 7)}
-    plain = ("d_tokens", "activations", "grad_output_weight", "grad_mlp_down")
-    shared = [name for _, names, _ in pairs[:2] for name in names]
+    shared = [name for names in behind.values() for name in names]
+    rest = ["grad_" + name for name in WEIGHTS if name not in shared]
+    plain = [*["grad_" + name for name in shared], *rest, "d_tokens", "activations"]
     source = {**got, **{name: weights[name] for name in shared}}
-    names = ["small_out", *gains, *[name for name, _, _ in pairs], *shared, *plain]
+    names = ["small_out", *behind, *shared, *plain]
     shapes = {name: got[name] for name in plain}
-    for name, targets, C in pairs:
-        for target in targets:
-            shapes["grad_" + target] = jax.ShapeDtypeStruct((got[name].shape[1], PLANE * C), f32)
-    for name in gains:
+    for name in behind:
         shapes["grad_" + name] = jax.ShapeDtypeStruct((1, RD), f32)
     for name, (low, high) in channels.items():
         shapes["grad_" + name] = jax.ShapeDtypeStruct((high - low, RW), f32)
@@ -1394,42 +1468,35 @@
 
         loads = {name: copy(ins[name], held[name]) for name in names}
         stores = []
+
+        def store(name):
+            stores.append(copy(held[name], outs[name]))
+
         loads["small_out"].wait()
         for name, (low, high) in channels.items():
             held["grad_" + name][...] = held["small_out"][low:high, 0:RW]
-            stores.append(copy(held["grad_" + name], outs["grad_" + name]))
-        for i, (name, targets, C) in enumerate(pairs):
-            loads[name].wait()
-            part, sums = C // (2 * RING), None
-            for j, target in enumerate(targets):
-                values = [held[name][k, :, j * C : (j + 1) * C].astype(f32) for k in range(PLANE)]
-                wide = jnp.concatenate(
-                    [value[:, g * part : (g + 1) * part] for g in range(2 * RING) for value in values], axis=1
-                )
-                held["grad_" + target][...] = wide
-                stores.append(copy(held["grad_" + target], outs["grad_" + target]))
-                if target in shared:
-                    loads[target].wait()
-                    product = wide * held[target][...].astype(f32)
-                    lanes = sum(product[:, k * 128 : (k + 1) * 128] for k in range(product.shape[1] // 128))
-                    sums = lanes if sums is None else sums + lanes
-            if sums is not None:
-                total = lax.dot_general(
-                    jnp.ones((8, 128), f32),
-                    sums,
-                    (((1,), (1,)), ((), ())),
-                    precision=lax.Precision.HIGHEST,
-                    preferred_element_type=f32,
-                )
-                target = "grad_" + gains[i]
-                loads[gains[i]].wait()
-                held[target][...] = total[0:1] / held[gains[i]][...].astype(f32)
-                stores.append(copy(held[target], outs[target]))
+            store("grad_" + name)
         for name in plain:
             loads[name].wait()
-            stores.append(copy(held[name], outs[name]))
-        for store in stores:
-            store.wait()
+            store(name)
+        for gain, pair in behind.items():
+            sums = jnp.zeros((RD, 128), f32)
+            for name in pair:
+                loads[name].wait()
+                product = held["grad_" + name][...] * held[name][...].astype(f32)
+                sums = sums + sum(product[:, k * 128 : (k + 1) * 128] for k in range(product.shape[1] // 128))
+            total = lax.dot_general(
+                jnp.ones((8, 128), f32),
+                sums,
+                (((1,), (1,)), ((), ())),
+                precision=lax.Precision.HIGHEST,
+                preferred_element_type=f32,
+            )
+            loads[gain].wait()
+            held["grad_" + gain][...] = total[0:1] / held[gain][...].astype(f32)
+            store("grad_" + gain)
+        for each in stores:
+            each.wait()
 
     results = pl.pallas_call(
         body,

time: 182 us -> 176 us (0.967)
  Pallas kernels: 181 us -> 175 us
    pallas_call x1, Pallas kernels: 177 us -> 171 us  [run_layer(): pl.pallas_call(partial(layer, dims), out_shape=[jax.ShapeDtypeStruct(shap...]
where the time goes in v7:
time: 176 us
  Pallas kernels  175 us (99%)
    pallas_call x1, Pallas kernels, run_layer(): pl.pallas_call(partial(layer, dims), out_shape=[jax.ShapeDtypeStruct(shap...  171 us

profile of v7, /device:TPU:0, one launch (start us, length us, event | category | flops | bytes accessed | tf_op | source)
XLA Modules:
  0.0 175.7 jit_solution(12082312414531613365)
XLA Ops:
  0.7 171.4 %griffin_layer.1 = (bf16[128,1024]{1,0:T(8,128)(2,1)}, f32[128,1024]{1,0:T(8,128)}, f32[32,1536]{1,0:T(8,128)}, f32[32,1536]{1,0:T(8,128)}, f32[48,1536]{1,0:T(8...) custom-call(bf16[128,1024]{1,0:T(8,128)(2,1)} %bitcast.22, ...), custom_call_target="tpu_custom_call" | custom-call | flops 14495514624 | bytes 8388608 | tf_op jit(solution)/shard_map/griffin_layer/pallas_call | solution.py:1424
  172.0 3.5 %finish.1 = (f32[32,1536]{1,0:T(8,128)}, f32[32,1536]{1,0:T(8,128)}, f32[32,3072]{1,0:T(8,128)}, f32[32,3072]{1,0:T(8,128)}, f32[48,1536]{1,0:T(8,128)}, /*index...) custom-call(f32[8,128]{1,0:T(8,128)} %get-tuple-element.43.refs_0_, ...), custom_call_target="tpu_custom_call" | custom-call | tf_op jit(solution)/shard_map/finish/pallas_call | solution.py:1501

commit v8 on v7

--- a/solution.py
+++ b/solution.py
@@ -16,7 +16,7 @@
 RING = 4
 PLANE = 4
 SHARES = RING * 2 * PLANE
-SENDS = 57
+SENDS = 53
 RECEIVES = 180
 
 eps_norm = 1e-06
@@ -1163,15 +1163,14 @@
         lax.fori_loop(0, RING, run, 0)
 
     grad_dec_inj(lanes_a)
-    g_d = ColumnsGrad(r.w_di, r.h_di, r.z_di, r.l_di, RW, 0, CW - 128)
+    g_d, g_j, g_k = (
+        ColumnsGrad(r.w_di, r.h_di, r.z_di, r.l_di, RW, lane0, lanes)
+        for lane0, lanes in ((0, 128), (128, CW - 128), (CW, CW))
+    )
     g_d.core_send()
+    g_j.core_send()
     rs_conv.mid()
     grad_dec_inj(lanes_b)
-    g_j, g_k = (
-        ColumnsGrad(r.w_di, r.h_di, r.z_di, r.l_di, RW, lane0, lanes)
-        for lane0, lanes in ((CW - 128, 256), (CW + 128, CW - 128))
-    )
-    g_j.core_send()
     g_k.core_send()
     g_o.z_forward()
     g_d.z_send()
@@ -1190,6 +1189,7 @@
         r.halo_out[4 * k : 4 * k + 4] = r.d_conv[k, 0:4]
     sent_b = push(r.halo_out, r.halo_in, to_prev, halo_b, pos > 0)
     g_b.z_forward()
+    g_j.z_send()
 
     def taps_back(o):
         sums = [jnp.zeros((1, CW), f32)] * 5
@@ -1213,7 +1213,8 @@
         r.halo_in[...] = jnp.zeros((16, CW), f32)
 
     g_d.z_forward()
-    g_j.z_send()
+    g_u.plane_send()
+    g_v.plane_send()
     arrived(r.halo_in, halo_b, pos < places - 1)
     for k in range(PLANE):
         r.d_conv[k, T : T + 8] = jnp.concatenate([r.halo_in[4 * k : 4 * k + 4], jnp.zeros((4, CW), f32)], axis=0)
@@ -1250,11 +1251,9 @@
     g_i.core_send()
     g_j.z_forward()
     g_k.z_send()
+    g_i.plane_send()
     rs_three.mid()
-    g_i.plane_send()
     g_k.z_forward()
-    g_u.plane_send()
-    g_v.plane_send()
     rs_three.end()
     g_i.z_send()
     g_b.plane_send()

time: 176 us -> 175 us (level)
  no operation moved by 1% of the time
where the time goes in v8:
time: 175 us
  Pallas kernels  174 us (99%)
    pallas_call x1, Pallas kernels, run_layer(): pl.pallas_call(partial(layer, dims), out_shape=[jax.ShapeDtypeStruct(shap...  171 us

profile of v8, /device:TPU:0, one launch (start us, length us, event | category | flops | bytes accessed | tf_op | source)
XLA Modules:
  0.0 174.9 jit_solution(14665323645261112060)
XLA Ops:
  0.7 170.6 %griffin_layer.1 = (bf16[128,1024]{1,0:T(8,128)(2,1)}, f32[128,1024]{1,0:T(8,128)}, f32[32,1536]{1,0:T(8,128)}, f32[32,1536]{1,0:T(8,128)}, f32[48,1536]{1,0:T(8...) custom-call(bf16[128,1024]{1,0:T(8,128)(2,1)} %bitcast.22, ...), custom_call_target="tpu_custom_call" | custom-call | flops 14495514624 | bytes 8388608 | tf_op jit(solution)/shard_map/griffin_layer/pallas_call | solution.py:1423
  171.2 3.5 %finish.1 = (f32[32,1536]{1,0:T(8,128)}, f32[32,1536]{1,0:T(8,128)}, f32[32,3072]{1,0:T(8,128)}, f32[32,3072]{1,0:T(8,128)}, f32[48,1536]{1,0:T(8,128)}, /*index...) custom-call(f32[8,128]{1,0:T(8,128)} %get-tuple-element.43.refs_0_, ...), custom_call_target="tpu_custom_call" | custom-call | tf_op jit(solution)/shard_map/finish/pallas_call | solution.py:1500

commit v9 on v8

--- a/solution.py
+++ b/solution.py
@@ -142,18 +142,8 @@
     def keep_local(src, dst, rsem):
         pltpu.make_async_copy(src, dst, r.rs.at[rsem]).start()
 
-    idle = []
-
     def local_wait(src, dst, rsem):
         pltpu.make_async_copy(src, dst, r.rs.at[rsem]).wait()
-        idle.append(rsem)
-
-    results = []
-
-    def deliver(src, dst):
-        sem = idle.pop() if idle else new()
-        keep_local(src, dst, sem)
-        results.append((src, dst, sem))
 
     def ds(start, size, unit):
         return pl.ds(pl.multiple_of(start, unit), size)
@@ -482,7 +472,6 @@
 
     def in_order(land, lane0, C, held, result):
         held[...] = unsorted([land[k, :, lane0 : lane0 + C].astype(f32) for k in range(PLANE)])
-        deliver(held, result)
 
     class LastGrad(ColumnsGrad):
         def __init__(self, g, other, stage, slots, R, lane0, lanes, total, result):
@@ -513,7 +502,6 @@
                 self.zsum.total(self.stage[q, zh].astype(f32), [self.slots[k, q] for k in range(4)]) for q in range(PLANE)
             ]
             self.sum[...] = unsorted(values)
-            deliver(self.sum, self.result)
 
     class RowsGrad(ColumnsGrad):
         def __init__(self, g, other, slots, total, result):
@@ -528,7 +516,6 @@
                 self.sum[s] = self.zsum.total(self.g[zh, c, s].astype(f32), [self.slots[k, s] for k in range(4)])
 
             loop(self.rows, 16, add)
-            deliver(self.sum, self.result)
 
     class Carry:
         def __init__(self, own, sib, buf, later):
@@ -675,8 +662,9 @@
             value = r.gg[0]
             for at in range(1, 2 * RING):
                 value = value + r.gg[at]
-            r.small_sum[...] = value
-            deliver(r.small_sum, r.small_out)
+            r.small_out[0:7] = value[0:7]
+            gains = [r.gain_a[...].astype(f32), r.gain_b[...].astype(f32), jnp.zeros((1, 128 - 2 * RD), f32)]
+            r.small_out[7:8] = jnp.concatenate(gains, axis=1)
             settle(*self.out)
 
     barrier = pltpu.get_barrier_semaphore()
@@ -970,7 +958,7 @@
             r.g_dn[k * RING // 2 : (k + 1) * RING // 2, :, :, o : o + D // 2] = value.astype(bf16).reshape(
                 RING // 2, 2, RF, D // 2
             )
-    g_dn = RowsGrad(r.g_dn, r.h_dn, r.z_dn, r.t_dn, r.grad_mlp_down)
+    g_dn = RowsGrad(r.g_dn, r.h_dn, r.z_dn, r.grad_mlp_down, r.grad_mlp_down)
     g_dn.core_send()
     g_dn.z_send()
     w_dn.z_wait()
@@ -1085,7 +1073,7 @@
         r.w_o[:, :, :, q] = value.astype(bf16).reshape(RING, 2, RW, D // 2)
 
     loop(D, D // 2, grad_out)
-    g_o = RowsGrad(r.w_o, r.h_o, r.z_o, r.t_o, r.grad_output_weight)
+    g_o = RowsGrad(r.w_o, r.h_o, r.z_o, r.grad_output_weight, r.grad_output_weight)
     g_o.core_send()
     carry_b.send()
     g_u.z_forward()
@@ -1147,10 +1135,9 @@
 
     def finish_act(o, summed, _):
         s = pl.ds(o, 16)
-        r.act[s] = (r.x_one[s] + summed).astype(bf16)
+        r.activations[s] = (r.x_one[s] + summed).astype(bf16)
 
     rs_act.each(16, finish_act)
-    deliver(r.act, r.activations)
     g_b.z_send()
     g_dn.end()
 
@@ -1247,7 +1234,7 @@
         return 0
 
     lax.fori_loop(0, RING, grad_input, 0)
-    g_i = LastGrad(r.w_ib, r.h_ib, r.st_i, r.z_i, RD, 0, CW, r.t_i, r.grad_input_weight)
+    g_i = LastGrad(r.w_ib, r.h_ib, r.st_i, r.z_i, RD, 0, CW, r.grad_input_weight, r.grad_input_weight)
     g_i.core_send()
     g_j.z_forward()
     g_k.z_send()
@@ -1266,31 +1253,28 @@
         rs = inverse_rms(v)
         z = v * rs
         dz = d_n * r.gains[0:1]
-        r.d_x[s] = r.d_one[s] + rs * (dz - z * jnp.mean(dz * z, axis=-1, keepdims=True))
+        r.d_tokens[s] = r.d_one[s] + rs * (dz - z * jnp.mean(dz * z, axis=-1, keepdims=True))
 
     rs_three.each(32, norm_one_back)
-    deliver(r.d_x, r.d_tokens)
     settle(sent_b)
     g_i.z_forward()
     g_k.plane_send()
     g_g.end()
-    in_order(r.l_gu, 0, CF, r.t_g, r.grad_mlp_gate)
+    in_order(r.l_gu, 0, CF, r.grad_mlp_gate, r.grad_mlp_gate)
     g_u.end()
     g_v.end()
-    in_order(r.l_gu, CF, CF, r.t_u, r.grad_mlp_up)
+    in_order(r.l_gu, CF, CF, r.grad_mlp_up, r.grad_mlp_up)
     g_b.end()
-    in_order(r.l_ib, CW, CW, r.t_b, r.grad_branch_weight)
+    in_order(r.l_ib, CW, CW, r.grad_branch_weight, r.grad_branch_weight)
     g_o.end()
     small_grad.two()
     g_d.end()
     g_j.end()
-    in_order(r.l_di, 0, CW, r.t_d, r.grad_decay_weight)
+    in_order(r.l_di, 0, CW, r.grad_decay_weight, r.grad_decay_weight)
     g_k.end()
-    in_order(r.l_di, CW, CW, r.t_j, r.grad_inject_weight)
+    in_order(r.l_di, CW, CW, r.grad_inject_weight, r.grad_inject_weight)
     g_i.end()
     assert not sent
-    for result in results:
-        local_wait(*result)
 
 
 WEIGHTS = (
@@ -1397,19 +1381,8 @@
         pr=((2 * RING, 16, 128), bf16),
         line=((16, 128), bf16),
         pp=((PLANE, 16, 128), bf16),
-        act=((T, D), bf16),
-        d_x=((T, D), f32),
-        t_i=((RD, W), f32),
-        t_b=((RD, W), f32),
         st_i=((PLANE, RING, RD, CW), bf16),
         z_i=((4, PLANE, RD, CW), bf16),
-        t_d=((RW, W), f32),
-        t_j=((RW, W), f32),
-        t_g=((RD, F), f32),
-        t_u=((RD, F), f32),
-        t_o=((RW, D), f32),
-        t_dn=((RF, D), f32),
-        small_sum=((8, 128), f32),
         gains=((8, D), f32),
         chan=((8, CW), f32),
         gchan=((8, CW), f32),
@@ -1422,13 +1395,13 @@
     flops = 3 * 2 * M * (D * 2 * CW + W * 2 * CW + CW * D + 3 * D * CF)
     results = pl.pallas_call(
         partial(layer, dims),
-        out_shape=[jax.ShapeDtypeStruct(shape, kind) for shape, kind in outs.values()],
+        out_shape=[pltpu.VMEM(shape, kind) for shape, kind in outs.values()],
         in_specs=[hbm] * len(ins),
-        out_specs=[hbm] * len(outs),
+        out_specs=[pl.BlockSpec(memory_space=pltpu.VMEM)] * len(outs),
         scratch_shapes=[pltpu.VMEM(shape, kind) for shape, kind in scratch.values()]
         + [pltpu.SemaphoreType.DMA((SENDS,)), pltpu.SemaphoreType.DMA((dims.receives,))],
         compiler_params=pltpu.CompilerParams(
-            collective_id=0, has_side_effects=True, vmem_limit_bytes=62 * 2**20
+            collective_id=0, has_side_effects=True, vmem_limit_bytes=58 * 2**20
         ),
         cost_estimate=pl.CostEstimate(flops=flops, bytes_accessed=8 * 2**20, transcendentals=M * CW * 16),
         name="griffin_layer",
@@ -1445,13 +1418,14 @@
     rest = ["grad_" + name for name in WEIGHTS if name not in shared]
     plain = [*["grad_" + name for name in shared], *rest, "d_tokens", "activations"]
     source = {**got, **{name: weights[name] for name in shared}}
-    names = ["small_out", *behind, *shared, *plain]
+    names = ["small_out", *shared, *plain]
     shapes = {name: got[name] for name in plain}
     for name in behind:
         shapes["grad_" + name] = jax.ShapeDtypeStruct((1, RD), f32)
     for name, (low, high) in channels.items():
         shapes["grad_" + name] = jax.ShapeDtypeStruct((high - low, RW), f32)
-    scratch = {name: (source[name].shape, source[name].dtype) for name in names}
+    fetched = shared
+    scratch = {name: (source[name].shape, source[name].dtype) for name in fetched}
     scratch.update({name: (like.shape, f32) for name, like in shapes.items() if name not in plain})
 
     def body(*refs):
@@ -1465,20 +1439,19 @@
             copies[-1].start()
             return copies[-1]
 
-        loads = {name: copy(ins[name], held[name]) for name in names}
+        loads = {name: copy(ins[name], held[name]) for name in fetched}
+        held.update({name: ins[name] for name in names if name not in fetched})
         stores = []
 
         def store(name):
             stores.append(copy(held[name], outs[name]))
 
-        loads["small_out"].wait()
         for name, (low, high) in channels.items():
             held["grad_" + name][...] = held["small_out"][low:high, 0:RW]
             store("grad_" + name)
         for name in plain:
-            loads[name].wait()
             store(name)
-        for gain, pair in behind.items():
+        for i, (gain, pair) in enumerate(behind.items()):
             sums = jnp.zeros((RD, 128), f32)
             for name in pair:
                 loads[name].wait()
@@ -1491,8 +1464,7 @@
                 precision=lax.Precision.HIGHEST,
                 preferred_element_type=f32,
             )
-            loads[gain].wait()
-            held["grad_" + gain][...] = total[0:1] / held[gain][...].astype(f32)
+            held["grad_" + gain][...] = total[0:1] / held["small_out"][7:8, i * RD : (i + 1) * RD]
             store("grad_" + gain)
         for each in stores:
             each.wait()
@@ -1500,13 +1472,13 @@
     results = pl.pallas_call(
         body,
         out_shape=[jax.ShapeDtypeStruct(like.shape, like.dtype) for like in shapes.values()],
-        in_specs=[hbm] * len(names),
+        in_specs=[hbm if name in fetched else pl.BlockSpec(memory_space=pltpu.VMEM) for name in names],
         out_specs=[hbm] * len(shapes),
         scratch_shapes=[
             *[pltpu.VMEM(shape, kind) for shape, kind in scratch.values()],
             pltpu.SemaphoreType.DMA((len(names) + len(shapes),)),
         ],
-        compiler_params=pltpu.CompilerParams(vmem_limit_bytes=62 * 2**20),
+        compiler_params=pltpu.CompilerParams(vmem_limit_bytes=24 * 2**20),
         name="finish",
     )(*[source[name] for name in names])
     return {**got, **dict(zip(shapes, results, strict=True))}

time: 175 us -> 174 us (level)
  no operation moved by 1% of the time
where the time goes in v9:
time: 174 us
  Pallas kernels  173 us (99%)
    pallas_call x1, Pallas kernels, run_layer(): pl.pallas_call(partial(layer, dims), out_shape=[pltpu.VMEM(shape, kind) f...  170 us

profile of v9, /device:TPU:0, one launch (start us, length us, event | category | flops | bytes accessed | tf_op | source)
XLA Modules:
  0.0 173.6 jit_solution(7516527392312733466)
XLA Ops:
  0.7 0.0 copy-start
  0.7 0.0 copy-start.1
  0.7 0.0 copy-start.2
  0.7 0.0 copy-start.3
  0.7 170.0 %griffin_layer.1 = (bf16[128,1024]{1,0:T(8,128)(2,1)S(1)}, f32[128,1024]{1,0:T(8,128)S(1)}, f32[32,1536]{1,0:T(8,128)S(1)}, f32[32,1536]{1,0:T(8,128)S(1)}, f32[...) custom-call(bf16[128,1024]{1,0:T(8,128)(2,1)} %bitcast.18, ...), custom_call_target="tpu_custom_call" | custom-call | flops 14495514624 | bytes 8388608 | tf_op jit(solution)/shard_map/griffin_layer/pallas_call | solution.py:1396
  170.7 0.0 copy-done
  170.7 0.0 copy-done.1
  170.7 0.0 copy-done.2
  170.7 0.0 copy-done.3
  170.7 2.7 %finish.1 = (f32[32,1536]{1,0:T(8,128)}, f32[32,1536]{1,0:T(8,128)}, f32[32,3072]{1,0:T(8,128)}, f32[32,3072]{1,0:T(8,128)}, f32[48,1536]{1,0:T(8,128)}, /*index...) custom-call(f32[8,128]{1,0:T(8,128)S(1)} %get-tuple-element.43.refs_, ...), custom_call_target="tpu_custom_call" | custom-call | tf_op jit(solution)/shard_map/finish/pallas_call | solution.py:1472
Async XLA Ops:
  0.7 170.0 %copy-start = (bf16[32,3072]{1,0:T(8,128)(2,1)S(1)}, bf16[32,3072]{1,0:T(8,128)(2,1)}, u32[]{:S(2)}) copy-start(bf16[32,3072]{1,0:T(8,128)(2,1)} %refs_3_.1) | copy-start | bytes 589828
  0.7 170.0 %copy-start.1 = (bf16[32,3072]{1,0:T(8,128)(2,1)S(1)}, bf16[32,3072]{1,0:T(8,128)(2,1)}, u32[]{:S(2)}) copy-start(bf16[32,3072]{1,0:T(8,128)(2,1)} %refs_4_.1) | copy-start | bytes 589828
  0.7 170.0 %copy-start.2 = (bf16[32,1536]{1,0:T(8,128)(2,1)S(1)}, bf16[32,1536]{1,0:T(8,128)(2,1)}, u32[]{:S(2)}) copy-start(bf16[32,1536]{1,0:T(8,128)(2,1)} %refs_2_.1) | copy-start | bytes 294916
  0.7 170.0 %copy-start.3 = (bf16[32,1536]{1,0:T(8,128)(2,1)S(1)}, bf16[32,1536]{1,0:T(8,128)(2,1)}, u32[]{:S(2)}) copy-start(bf16[32,1536]{1,0:T(8,128)(2,1)} %refs_1_.1) | copy-start | bytes 294916

commit v10 on v9

--- a/solution.py
+++ b/solution.py
@@ -502,6 +502,20 @@
                 self.zsum.total(self.stage[q, zh].astype(f32), [self.slots[k, q] for k in range(4)]) for q in range(PLANE)
             ]
             self.sum[...] = unsorted(values)
+
+    def gain_grad(gain, *pairs):
+        sums = jnp.zeros((RD, 128), f32)
+        for grad, weight in pairs:
+            product = grad[...] * weight[...].astype(f32)
+            sums = sums + sum(product[:, k * 128 : (k + 1) * 128] for k in range(product.shape[1] // 128))
+        total = lax.dot_general(
+            jnp.ones((8, 128), f32),
+            sums,
+            (((1,), (1,)), ((), ())),
+            precision=lax.Precision.HIGHEST,
+            preferred_element_type=f32,
+        )
+        return total[0:1] / gain[...].astype(f32)
 
     class RowsGrad(ColumnsGrad):
         def __init__(self, g, other, slots, total, result):
@@ -663,8 +677,6 @@
             for at in range(1, 2 * RING):
                 value = value + r.gg[at]
             r.small_out[0:7] = value[0:7]
-            gains = [r.gain_a[...].astype(f32), r.gain_b[...].astype(f32), jnp.zeros((1, 128 - 2 * RD), f32)]
-            r.small_out[7:8] = jnp.concatenate(gains, axis=1)
             settle(*self.out)
 
     barrier = pltpu.get_barrier_semaphore()
@@ -1273,7 +1285,10 @@
     in_order(r.l_di, 0, CW, r.grad_decay_weight, r.grad_decay_weight)
     g_k.end()
     in_order(r.l_di, CW, CW, r.grad_inject_weight, r.grad_inject_weight)
+    second = gain_grad(r.gain_b, (r.grad_mlp_gate, r.raw_g), (r.grad_mlp_up, r.raw_u))
     g_i.end()
+    first = gain_grad(r.gain_a, (r.grad_input_weight, r.raw_i), (r.grad_branch_weight, r.raw_b))
+    r.small_out[7:8] = jnp.concatenate([first, second, jnp.zeros((1, 128 - 2 * RD), f32)], axis=1)
     assert not sent
 
 
@@ -1417,16 +1432,13 @@
     shared = [name for names in behind.values() for name in names]
     rest = ["grad_" + name for name in WEIGHTS if name not in shared]
     plain = [*["grad_" + name for name in shared], *rest, "d_tokens", "activations"]
-    source = {**got, **{name: weights[name] for name in shared}}
-    names = ["small_out", *shared, *plain]
+    names = ["small_out", *plain]
     shapes = {name: got[name] for name in plain}
     for name in behind:
         shapes["grad_" + name] = jax.ShapeDtypeStruct((1, RD), f32)
     for name, (low, high) in channels.items():
         shapes["grad_" + name] = jax.ShapeDtypeStruct((high - low, RW), f32)
-    fetched = shared
-    scratch = {name: (source[name].shape, source[name].dtype) for name in fetched}
-    scratch.update({name: (like.shape, f32) for name, like in shapes.items() if name not in plain})
+    scratch = {name: (like.shape, f32) for name, like in shapes.items() if name not in plain}
 
     def body(*refs):
         ins = dict(zip(names, refs[: len(names)], strict=True))
@@ -1439,8 +1451,7 @@
             copies[-1].start()
             return copies[-1]
 
-        loads = {name: copy(ins[name], held[name]) for name in fetched}
-        held.update({name: ins[name] for name in names if name not in fetched})
+        held.update(ins)
         stores = []
 
         def store(name):
@@ -1451,20 +1462,8 @@
             store("grad_" + name)
         for name in plain:
             store(name)
-        for i, (gain, pair) in enumerate(behind.items()):
-            sums = jnp.zeros((RD, 128), f32)
-            for name in pair:
-                loads[name].wait()
-                product = held["grad_" + name][...] * held[name][...].astype(f32)
-                sums = sums + sum(product[:, k * 128 : (k + 1) * 128] for k in range(product.shape[1] // 128))
-            total = lax.dot_general(
-                jnp.ones((8, 128), f32),
-                sums,
-                (((1,), (1,)), ((), ())),
-                precision=lax.Precision.HIGHEST,
-                preferred_element_type=f32,
-            )
-            held["grad_" + gain][...] = total[0:1] / held["small_out"][7:8, i * RD : (i + 1) * RD]
+        for i, gain in enumerate(behind):
+            held["grad_" + gain][...] = held["small_out"][7:8, i * RD : (i + 1) * RD]
             store("grad_" + gain)
         for each in stores:
             each.wait()
@@ -1472,7 +1471,7 @@
     results = pl.pallas_call(
         body,
         out_shape=[jax.ShapeDtypeStruct(like.shape, like.dtype) for like in shapes.values()],
-        in_specs=[hbm if name in fetched else pl.BlockSpec(memory_space=pltpu.VMEM) for name in names],
+        in_specs=[pl.BlockSpec(memory_space=pltpu.VMEM)] * len(names),
         out_specs=[hbm] * len(shapes),
         scratch_shapes=[
             *[pltpu.VMEM(shape, kind) for shape, kind in scratch.values()],
@@ -1480,7 +1479,7 @@
         ],
         compiler_params=pltpu.CompilerParams(vmem_limit_bytes=24 * 2**20),
         name="finish",
-    )(*[source[name] for name in names])
+    )(*[got[name] for name in names])
     return {**got, **dict(zip(shapes, results, strict=True))}
 
 

time: 174 us -> 173 us (level)
  no operation moved by 1% of the time
where the time goes in v10:
time: 173 us
  Pallas kernels  172 us (99%)
    pallas_call x1, Pallas kernels, run_layer(): pl.pallas_call(partial(layer, dims), out_shape=[pltpu.VMEM(shape, kind) f...  170 us

profile of v10, /device:TPU:0, one launch (start us, length us, event | category | flops | bytes accessed | tf_op | source)
XLA Modules:
  0.0 172.8 jit_solution(6015021472687410313)
XLA Ops:
  0.7 170.0 %griffin_layer.1 = (bf16[128,1024]{1,0:T(8,128)(2,1)S(1)}, f32[128,1024]{1,0:T(8,128)S(1)}, f32[32,1536]{1,0:T(8,128)S(1)}, f32[32,1536]{1,0:T(8,128)S(1)}, f32[...) custom-call(bf16[128,1024]{1,0:T(8,128)(2,1)} %bitcast.18, ...), custom_call_target="tpu_custom_call" | custom-call | flops 14495514624 | bytes 8388608 | tf_op jit(solution)/shard_map/griffin_layer/pallas_call | solution.py:1411
  170.7 1.9 %finish.1 = (f32[32,1536]{1,0:T(8,128)}, f32[32,1536]{1,0:T(8,128)}, f32[32,3072]{1,0:T(8,128)}, f32[32,3072]{1,0:T(8,128)}, f32[48,1536]{1,0:T(8,128)}, /*index...) custom-call(f32[8,128]{1,0:T(8,128)S(1)} %get-tuple-element.43.refs_, ...), custom_call_target="tpu_custom_call" | custom-call | tf_op jit(solution)/shard_map/finish/pallas_call | solution.py:1471
